TPU v7x, 512 devices: a whole 4x8x8 slice. The times are simulated.
512 devices in a mesh: seq: 16 (over y, z_lo), fsdp: 32 (over z_hi, x, core).
Axes of the slice: x: 4, y: 8, z: 8 (z_hi: 4, z_lo: 2; z = z_hi * 2 + z_lo), core: 2. Of those that a mesh axis runs over, the one named last changes fastest.
Arguments:
- q_video: bfloat16 [32, 1920, 1536], P('fsdp', 'seq'), may hold values from -42 to 42
- kv_video: bfloat16 [32, 1920, 2, 1536], P('fsdp', 'seq'), may hold values from -6 to 6
- q_text: bfloat16 [32, 128, 1536], P('fsdp', 'seq'), may hold values from -6 to 6
- kv_text: bfloat16 [32, 128, 2, 1536], P('fsdp', 'seq'), may hold values from -9 to 9
- text_lengths: int32 [32], P('fsdp'), may hold values from 1 to 128, as said below
- gate: float32 [32, 1536], P('fsdp'), may hold values from 0.5 to 4
- w_out: bfloat16 [1536, 1536], P('fsdp'), may hold values from -0.15625 to 0.15625
Outputs:
- attn_video: bfloat16 [32, 1920, 1536], P('fsdp', 'seq')
- attn_text: bfloat16 [32, 128, 1536], P('fsdp', 'seq')
- lse_video: float32 [32, 12, 1920], P('fsdp', None, 'seq')
- lse_text: float32 [32, 12, 128], P('fsdp', None, 'seq')
- proj_video: bfloat16 [32, 1920, 1536], P('fsdp', 'seq')
Inputs may be any that keep to these rules, and one draw needn't show every extreme that they name: `text_lengths`: some sample has all 128 text slots real.
All inputs are finite; a program needn't handle non-finite values.
Results may differ from a plain program's by a relative error of at most 0.018.
Values may be sent and summed in bfloat16 or wider, within the bound.
No kernel may reach another device: no remote copies, remote signals or barrier semaphores. Data moves between devices by JAX's collectives and lax.ppermute only.
A program may use at most 128 MiB of HBM per device.

v0:
```python
import math

import jax
import jax.numpy as jnp
from jax import lax
from jax.sharding import PartitionSpec as P

HEADS = 12
HEAD = 128


def attend_block(carry, queries, keyvals, valid):
    best, total, accum = carry
    count = keyvals.shape[0]
    keys = keyvals[:, 0].reshape(count, HEADS, HEAD)
    values = keyvals[:, 1].reshape(count, HEADS, HEAD)
    scores = jnp.einsum("qhd,khd->hqk", queries, keys, preferred_element_type=jnp.float32)
    scores = jnp.where(valid[None, None, :], scores * (1.0 / math.sqrt(HEAD)), -1e30)
    newbest = jnp.maximum(best, jnp.max(scores, axis=-1))
    factor = jnp.exp(best - newbest)
    weights = jnp.where(valid[None, None, :], jnp.exp(scores - newbest[..., None]), 0.0)
    total = total * factor + jnp.sum(weights, axis=-1)
    update = jnp.einsum(
        "hqk,khd->hqd", weights.astype(jnp.bfloat16), values, preferred_element_type=jnp.float32
    )
    accum = accum * factor[..., None] + update
    return (newbest, total, accum)


def attend(carry, queries, keyvals, valid):
    return attend_block(carry, queries, keyvals, valid)


def shards(q_video, kv_video, q_text, kv_text, text_lengths, gate, w_out):
    vid_rows = q_video.shape[1]
    length = text_lengths[0]
    queries = jnp.concatenate([q_video[0], q_text[0]], 0).reshape(-1, HEADS, HEAD)
    rows = queries.shape[0]
    start_state = (
        jnp.full((HEADS, rows), -1e30, jnp.float32),
        jnp.zeros((HEADS, rows), jnp.float32),
        jnp.zeros((HEADS, rows, HEAD), jnp.float32),
    )
    carry = start_state
    video_piece = lax.all_gather(kv_video, "seq", axis=1, tiled=True)
    text_piece = lax.all_gather(kv_text, "seq", axis=1, tiled=True)
    text_count = text_piece.shape[1]
    carry = attend(carry, queries, video_piece[0], jnp.ones((video_piece.shape[1],), bool))
    text_valid = jnp.arange(text_count) < length
    state = attend(carry, queries, text_piece[0], text_valid)
    best, total, accum = state
    lse = best + jnp.log(total)
    mixed = (accum / total[..., None]).transpose(1, 0, 2).reshape(rows, -1).astype(jnp.bfloat16)
    video_rows = mixed[:vid_rows]
    projected = jnp.dot(
        video_rows,
        lax.all_gather(w_out, "fsdp", axis=0, tiled=True),
        preferred_element_type=jnp.float32,
    )
    projected = (projected * gate[0][None, :]).astype(jnp.bfloat16)
    return (
        video_rows[None],
        mixed[vid_rows:][None],
        lse[:, :vid_rows][None],
        lse[:, vid_rows:][None],
        projected[None],
    )


def solution(mesh):
    placed = (
        P("fsdp", "seq", None),
        P("fsdp", "seq", None, None),
        P("fsdp", "seq", None),
        P("fsdp", "seq", None, None),
        P("fsdp"),
        P("fsdp", None),
        P("fsdp", None),
    )
    return jax.shard_map(
        shards,
        mesh=mesh,
        in_specs=placed,
        out_specs=(
            P("fsdp", "seq", None),
            P("fsdp", "seq", None),
            P("fsdp", None, "seq"),
            P("fsdp", None, "seq"),
            P("fsdp", "seq", None),
        ),
        check_vma=False,
    )
```

profile of v0, /device:TPU:1, one launch (start us, length us, event | category | flops | bytes accessed | tf_op | source)
XLA Modules:
  0.0 365.3 jit_solution(4366835602130396295)
XLA Ops:
  7.2 0.7 all-gather.3.cloned.1.call-update
  7.9 0.7 all-gather.5.cloned.1.call-update
  8.6 1.2 copy.37
  10.1 47.9 %all_gather.10 = bf16[1,128,2,1536]{3,2,0,1:T(2,128)(2,1)S(1)} all-gather(bf16[1,8,2,1536]{3,2,0,1:T(2,128)(2,1)} %bitcast.74), channel_id=1, replica_groups=mesh['seq'=16,'fsdp'=32] {'seq'}, dimensions={1}, use_global_device_ids=true | all-gather | bytes 835584 | tf_op jit(solution)/shard_map/all_gather | solution.py:46
  58.0 0.8 copy.44
  59.4 1.3 reduce
  60.7 0.8 fusion.38
  61.5 2.0 fusion.39
  63.6 214.6 %all-gather.3.cloned.1.call-done = bf16[1,1920,2,1536]{3,2,0,1:T(2,128)(2,1)} async-done(((bf16[1,120,2,1536]{3,2,0,1:T(2,128)(2,1)}), bf16[1,1920,2,1536]{3,2,0,1:T(2,128)(2,1)}) %all-gather.3.cloned.1.call-update) | async-done | bytes 11796496 | tf_op jit(solution)/shard_map/all_gather | solution.py:45
  278.2 29.6 %copy.40 = bf16[1,1920,2,1536]{1,3,2,0:T(8,128)(2,1)} copy(bf16[1,1920,2,1536]{3,2,0,1:T(2,128)(2,1)} %all-gather.3.cloned.1.call-done) | data formatting | bytes 23592960 | tf_op jit(solution)/shard_map/all_gather | solution.py:45
  307.8 5.1 %fusion.37 = (bf16[1920,1,1536]{0,2,1:T(8,128)(2,1)S(1)}, bf16[1920,1,1536]{0,2,1:T(8,128)(2,1)S(1)}) fusion(bf16[1920,2,1536]{0,2,1:T(8,128)(2,1)} %bitcast.64), kind=kLoop, calls=%fused_computation.45 | loop fusion | bytes 23592960 | tf_op jit(solution)/shard_map/slice | solution.py:15
  312.9 1.8 multiply_reduce_fusion
  315.0 4.2 %copy-done = f32[12,128,1920]{2,1,0:T(8,128)} copy-done((f32[12,128,1920]{2,1,0:T(8,128)}, f32[12,128,1920]{2,1,0:T(8,128)S(1)}, u32[]{:S(2)}) %copy-start) | copy-done | bytes 11796504
  319.1 2.1 fusion
  321.2 0.6 bitcast_add_fusion
  321.8 5.7 %fusion.17 = f32[128,12,128]{2,0,1:T(8,128)S(1)} fusion(bf16[1920,12,128]{0,2,1:T(8,128)(2,1)S(1)} %bitcast.66, f32[12,128,1920]{2,1,0:T(8,128)} %copy-done, f32[12,128]{1,0:T(8,128)S(1)} %get-tuple-element.28, f32[128,12]{0,1:T(8,128)} %get-tuple-element.25, f32[128,12]{0,1:T(8,128)} %get-tuple-element.26), kind=kOutput, calls=%fused_computation.17 | convolution fusion | flops 764215296 | bytes 18499584 | tf_op jit(solution)/shard_map/hqk,khd->hqd/dot_general | solution.py:23
  327.6 1.8 fusion.20
  329.4 0.2 copy.48
  329.7 0.9 copy.51
  330.7 0.6 copy.52
  331.3 0.7 copy.49
  332.0 0.6 slice_bitcast_fusion
  332.6 22.0 %all-gather.5.cloned.1.call-done = bf16[1536,1536]{1,0:T(8,128)(2,1)} async-done(((bf16[48,1536]{1,0:T(8,128)(2,1)}), bf16[1536,1536]{1,0:T(8,128)(2,1)}) %all-gather.5.cloned.1.call-update) | async-done | bytes 4718608 | tf_op jit(solution)/shard_map/all_gather | solution.py:57
  354.6 3.9 %fusion.7 = bf16[1,120,1536]{2,1,0:T(8,128)(2,1)} fusion(bf16[120,1536]{0,1:T(8,128)(2,1)S(1)} %bitcast.68, bf16[1536,1536]{1,0:T(8,128)(2,1)} %all-gather.5.cloned.1.call-done, f32[1536]{0:T(1024)} %reduce), kind=kOutput, calls=%fused_computation.9 | convolution fusion | flops 566599680 | bytes 5462016 | tf_op jit(solution)/shard_map/dot_general | solution.py:55
  (19 shorter events, 0.6 us)
Async XLA Ops:
  7.2 271.0 %all-gather.3.cloned.1.call-start = ((), (), s32[]{:S(2)}) async-start(), calls=%async_computation | async-start | bytes 12533760 | tf_op jit(solution)/shard_map/all_gather | solution.py:45
  7.9 346.7 %all-gather.5.cloned.1.call-start = ((), (), s32[]{:S(2)}) async-start(), calls=%async_computation.1 | async-start | bytes 4866048 | tf_op jit(solution)/shard_map/all_gather | solution.py:57
  60.7 254.0 %copy-start.4 = (pred[128]{0:T(512)(128)(4,1)}, pred[128]{0:T(512)(128)(4,1)S(1)}, u32[]{:S(2)}) copy-start(pred[128]{0:T(512)(128)(4,1)S(1)} %iota_compare_fusion) | copy-start | bytes 388
  307.8 5.1 %copy-start.3 = (bf16[1,8,1536]{2,1,0:T(8,128)(2,1)S(1)}, bf16[1,8,1536]{2,1,0:T(8,128)(2,1)}, u32[]{:S(2)}) copy-start(bf16[1,8,1536]{2,1,0:T(8,128)(2,1)} %param.9) | copy-start | bytes 73732
  312.9 1.9 copy-start.1
  314.7 4.4 %copy-start = (f32[12,128,1920]{2,1,0:T(8,128)}, f32[12,128,1920]{2,1,0:T(8,128)S(1)}, u32[]{:S(2)}) copy-start(f32[12,128,1920]{2,1,0:T(8,128)S(1)} %get-tuple-element.32) | copy-start | bytes 35389444
  314.7 7.1 %copy-start.2 = (f32[12,128]{1,0:T(8,128)}, f32[12,128]{1,0:T(8,128)S(1)}, u32[]{:S(2)}) copy-start(f32[12,128]{1,0:T(8,128)S(1)} %get-tuple-element.27) | copy-start | bytes 18436
Sparse Core Ops, SparseCore 0:
  10.1 268.0 all-gather.2
  281.3 73.2 all-gather.4
where the time goes:
time: 366 us; the launch traced here: 365 us
  waiting for transfers between devices  238 us (65%)
  blocking collectives  47.9 us (13%)
  local copies, waits for them, and re-layouts  45.1 us (12%)
  matrix products  15.3 us (4%)
  between operations  14.8 us (4%)
  other arithmetic  4.19 us (1%)
    all_gather x1, waiting for transfers between devices, shards(): video_piece = lax.all_gather(kv_video, 'seq', axis=1, tiled=True)  215 us
    all_gather x1, blocking collectives, shards(): text_piece = lax.all_gather(kv_text, 'seq', axis=1, tiled=True)  47.9 us
    all_gather x1, local copies, waits for them, and re-layouts, shards(): video_piece = lax.all_gather(kv_video, 'seq', axis=1, tiled=True)  29.6 us
    all_gather x1, waiting for transfers between devices, shards(): lax.all_gather(w_out, 'fsdp', axis=0, tiled=True)  22 us
    dot_general x2, matrix products, attend_block(): jnp.einsum('hqk,khd->hqd', weights.astype(jnp.bfloat16), values, preferre...  7.54 us
  transfers between devices with their start and end apart: 2, of which 2 were waited for; matrix products, arithmetic and copies ran while one was open for 15% of the time, Pallas kernels for 0%

commit v1 on v0

v1 whole, which is shorter than its diff:
```python
import functools
import math

import jax
import jax.numpy as jnp
from jax import lax
from jax.experimental import pallas as pl
from jax.experimental.pallas import tpu as pltpu
from jax.sharding import PartitionSpec as P

HEADS = 12
HEAD = 128
SLOPE = math.log2(math.e) / math.sqrt(HEAD)
LN2 = math.log(2.0)
LSE_ROWS = 16
VMEM = pltpu.VMEM


def pack_kernel(length_ref, base_ref, qv_ref, kvv_ref, qt_ref, kvt_ref, out_ref):
    vid = qv_ref.shape[0]
    txt = qt_ref.shape[0]
    slot = base_ref[0] + lax.broadcasted_iota(jnp.int32, (txt, HEAD), 0)
    valid = slot < length_ref[0]
    for h in range(HEADS):
        cols = pl.ds(h * HEAD, HEAD)
        out_ref[h, 0, :vid] = qv_ref[:, cols]
        out_ref[h, 0, vid:] = qt_ref[:, cols]
        keys = kvv_ref[:, cols]
        out_ref[h, 1, :vid] = keys
        out_ref[h, 1, vid:] = jnp.where(
            valid, kvt_ref[:, cols].astype(jnp.float32), keys[:1].astype(jnp.float32)
        ).astype(jnp.bfloat16)
        vcols = pl.ds((HEADS + h) * HEAD, HEAD)
        out_ref[h, 2, :vid] = kvv_ref[:, vcols]
        out_ref[h, 2, vid:] = jnp.where(
            valid, kvt_ref[:, vcols].astype(jnp.float32), 0.0
        ).astype(jnp.bfloat16)
    for h in range(HEADS, out_ref.shape[0]):
        out_ref[h] = jnp.zeros(out_ref.shape[1:], jnp.bfloat16)


def attend_kernel(vid, length_ref, x_ref, out_ref, vals_ref, keys_ref):
    sources, _, rows, _ = x_ref.shape
    txt = rows - vid
    step = pl.program_id(0)
    per = out_ref.shape[0]

    @pl.when(step == 0)
    def _():
        row = lax.broadcasted_iota(jnp.int32, (rows, HEAD), 0)
        for s in range(sources):
            valid = (row < vid) | (row - vid + s * txt < length_ref[0])
            keys_ref[pl.ds(s * rows, rows), :] = x_ref[s, 1]
            vals_ref[pl.ds(s * rows, rows), :HEAD] = x_ref[s, 2]
            vals_ref[pl.ds(s * rows, rows), HEAD:] = jnp.where(valid, 1.0, 0.0).astype(jnp.bfloat16)

    for j in range(per):
        q = x_ref[step * per + j, 0]
        scores = lax.dot_general(
            q, keys_ref[...], (((1,), (1,)), ((), ())), preferred_element_type=jnp.float32
        )
        best = jnp.max(scores, axis=1, keepdims=True) * SLOPE
        weights = jnp.exp2(scores * SLOPE - best).astype(jnp.bfloat16)
        both = jnp.dot(weights, vals_ref[...], preferred_element_type=jnp.float32)
        total = both[:, HEAD:]
        out_ref[j, :rows] = (both[:, :HEAD] / total).astype(jnp.bfloat16)
        lse = ((best + jnp.log2(total)) * LN2).T[:LSE_ROWS]
        high = lse.astype(jnp.bfloat16).astype(jnp.float32)
        mid = (lse - high).astype(jnp.bfloat16).astype(jnp.float32)
        low = lse - high - mid
        which = lax.broadcasted_iota(jnp.int32, lse.shape, 0)
        parts = jnp.where(which == 0, high, jnp.where(which == 1, mid, low))
        out_ref[j, rows:] = parts.astype(jnp.bfloat16)


def project_kernel(x_ref, w_ref, gate_ref, av_ref, at_ref, lv_ref, lt_ref, pv_ref):
    vid = av_ref.shape[0]
    rows = vid + at_ref.shape[0]
    mixed = jnp.concatenate([x_ref[h, :rows] for h in range(HEADS)], axis=1)

    @pl.when(pl.program_id(0) == 0)
    def _():
        av_ref[...] = mixed[:vid]
        at_ref[...] = mixed[vid:]
        for h in range(HEADS):
            parts = x_ref[h, rows:].astype(jnp.float32)
            lse = parts[0:1] + parts[1:2] + parts[2:3]
            lv_ref[pl.ds(h, 1), :] = lse[:, :vid]
            lt_ref[pl.ds(h, 1), :] = lse[:, vid:]

    out = jnp.dot(mixed, w_ref[...], preferred_element_type=jnp.float32)
    pv_ref[...] = (out[:vid] * gate_ref[...]).astype(jnp.bfloat16)


def shards(sources, q_video, kv_video, q_text, kv_text, text_lengths, gate, w_out):
    vid, feats = q_video.shape[1:]
    txt = q_text.shape[1]
    rows = vid + txt
    base = (lax.axis_index("seq") * txt).astype(jnp.int32).reshape(1)
    whole_w = lax.all_gather(w_out, "fsdp", axis=0, tiled=True)
    smem = pl.BlockSpec(memory_space=pltpu.SMEM)
    vmem = pl.BlockSpec(memory_space=VMEM)
    packed = pl.pallas_call(
        pack_kernel,
        out_shape=jax.ShapeDtypeStruct((sources, 3, rows, HEAD), jnp.bfloat16),
        in_specs=[smem, smem, vmem, vmem, vmem, vmem],
        out_specs=vmem,
        name="pack",
    )(
        text_lengths,
        base,
        q_video[0],
        kv_video.reshape(vid, 2 * feats),
        q_text[0],
        kv_text.reshape(txt, 2 * feats),
    )
    moved = lax.all_to_all(packed, "seq", 0, 0, tiled=True)
    per = 2
    mixed = pl.pallas_call(
        functools.partial(attend_kernel, vid),
        grid=(sources // per,),
        out_shape=jax.ShapeDtypeStruct((sources, rows + LSE_ROWS, HEAD), jnp.bfloat16),
        in_specs=[smem, vmem],
        out_specs=pl.BlockSpec((per, rows + LSE_ROWS, HEAD), lambda i: (i, 0, 0)),
        scratch_shapes=[
            VMEM((sources * rows, 2 * HEAD), jnp.bfloat16),
            VMEM((sources * rows, HEAD), jnp.bfloat16),
        ],
        compiler_params=pltpu.CompilerParams(vmem_limit_bytes=32 << 20),
        name="attend",
    )(text_lengths, moved)
    back = lax.all_to_all(mixed, "seq", 0, 0, tiled=True)
    cols = 512
    outs = pl.pallas_call(
        project_kernel,
        grid=(feats // cols,),
        out_shape=(
            jax.ShapeDtypeStruct((vid, feats), jnp.bfloat16),
            jax.ShapeDtypeStruct((txt, feats), jnp.bfloat16),
            jax.ShapeDtypeStruct((HEADS, vid), jnp.float32),
            jax.ShapeDtypeStruct((HEADS, txt), jnp.float32),
            jax.ShapeDtypeStruct((vid, feats), jnp.bfloat16),
        ),
        in_specs=[
            vmem,
            pl.BlockSpec((feats, cols), lambda i: (0, i)),
            pl.BlockSpec((1, cols), lambda i: (0, i)),
        ],
        out_specs=(vmem, vmem, vmem, vmem, pl.BlockSpec((vid, cols), lambda i: (0, i))),
        compiler_params=pltpu.CompilerParams(vmem_limit_bytes=32 << 20),
        name="project",
    )(back, whole_w, gate)
    return tuple(out[None] for out in outs)


def solution(mesh):
    placed = (
        P("fsdp", "seq", None),
        P("fsdp", "seq", None, None),
        P("fsdp", "seq", None),
        P("fsdp", "seq", None, None),
        P("fsdp"),
        P("fsdp", None),
        P("fsdp", None),
    )
    return jax.shard_map(
        functools.partial(shards, mesh.shape["seq"]),
        mesh=mesh,
        in_specs=placed,
        out_specs=(
            P("fsdp", "seq", None),
            P("fsdp", "seq", None),
            P("fsdp", None, "seq"),
            P("fsdp", None, "seq"),
            P("fsdp", "seq", None),
        ),
        check_vma=False,
    )
```

time: 366 us -> 110 us (0.30)
  waiting for transfers between devices: 238 us -> 0.68 us
  local copies, waits for them, and re-layouts: 45.1 us -> 6.31 us
  blocking collectives: 47.9 us -> 70.9 us
  matrix products: 15.3 us -> 0 us
  Pallas kernels: 0 us -> 15.3 us
  other arithmetic: 4.19 us -> 0 us
    all_gather x2 -> x1, waiting for transfers between devices: 237 us -> 0.01 us  [shards(): whole_w = lax.all_gather(w_out, 'fsdp', axis=0, tiled=True)]
    all_to_all x0 -> x2, blocking collectives: none -> 70.9 us  [the longest x1 47.6 us: shards(): moved = lax.all_to_all(packed, 'seq', 0, 0, tiled=True)]
    all_gather x1 -> x0, blocking collectives: 47.9 us -> none  [shards(): text_piece = lax.all_gather(kv_text, 'seq', axis=1, tiled=True)]
    all_gather x2 -> x0, local copies, waits for them, and re-layouts: 30.4 us -> none  [the longest x1 29.6 us: shards(): video_piece = lax.all_gather(kv_video, 'seq', axis=1, tiled=True)]
    pallas_call x0 -> x3, Pallas kernels: none -> 15.3 us  [the longest x1 10.2 us: shards(): pl.pallas_call(functools.partial(attend_kernel, vid), grid=(sources // pe...]
    dot_general x5 -> x0, matrix products: 15.3 us -> none  [the longest x2 7.54 us: attend_block(): jnp.einsum('hqk,khd->hqd', weights.astype(jnp.bfloat16), values, preferre...]
    slice x6 -> x0, local copies, waits for them, and re-layouts: 6.91 us -> none  [the longest x1 5.1 us: attend_block(): keys = keyvals[:, 0].reshape(count, HEADS, HEAD)]
  transfers between devices with their start and end apart: 2 -> 1, of which waited for: 2 -> 0; matrix products, arithmetic and copies ran while one was open for 15% -> 3% of each run, Pallas kernels for 0% -> 12%
where the time goes in v1:
time: 110 us; the launch traced here: 108 us
  blocking collectives  70.9 us (64%)
  Pallas kernels  15.3 us (14%)
  between operations  14.7 us (13%)
  local copies, waits for them, and re-layouts  6.31 us (6%)
    all_to_all x1, blocking collectives, shards(): moved = lax.all_to_all(packed, 'seq', 0, 0, tiled=True)  47.6 us
    all_to_all x1, blocking collectives, shards(): back = lax.all_to_all(mixed, 'seq', 0, 0, tiled=True)  23.3 us
    pallas_call x1, Pallas kernels, shards(): pl.pallas_call(functools.partial(attend_kernel, vid), grid=(sources // pe...  10.2 us
    unnamed x9, local copies, waits for them, and re-layouts  5.64 us
    pallas_call x1, Pallas kernels, shards(): pl.pallas_call(pack_kernel, out_shape=jax.ShapeDtypeStruct((sources, 3, r...  2.61 us
    pallas_call x1, Pallas kernels, shards(): pl.pallas_call(project_kernel, grid=(feats // cols,), out_shape=(jax.Shap...  2.49 us
  transfers between devices with their start and end apart: 1, of which 0 were waited for; matrix products, arithmetic and copies ran while one was open for 3% of the time, Pallas kernels for 12%

profile of v1, /device:TPU:1, one launch (start us, length us, event | category | flops | bytes accessed | tf_op | source)
XLA Modules:
  0.0 107.9 jit_solution(8706092149121818401)
XLA Ops:
  7.2 0.0 copy-start.2
  7.2 0.0 all-gather.2.cloned.1.call-start
  7.2 0.7 all-gather.2.cloned.1.call-update
  8.6 2.1 %copy.14 = bf16[15,8,2,1536]{3,1,2,0:T(8,128)(2,1)} copy(bf16[15,8,2,1536]{3,2,1,0:T(2,128)(2,1)} %bitcast.16) | data formatting | bytes 1474560
  10.6 0.0 copy-done.2
  10.6 0.6 copy.15
  11.3 2.6 %pack.1 = bf16[16,3,128,128]{3,2,1,0:T(8,128)(2,1)} custom-call(s32[1]{0:T(128)S(6)} %copy.16.length_ref, s32[1]{0:T(128)} %bitcast.base_ref, bf16[120,1536]{1,0:T(8,128)(2,1)} %bitcast.17, bf16[120,3072]{1,0:T(8,128)(2,1)} %bitcast.15, bf16[8,1536]{1,0:T(8,128)(2,1)} %bitcast.19, bf16[8,3072]{1,0:T(8,128)(2,1)} %bitcast.18), custom_call_target="tpu_custom_call" | custom-call | tf_op jit(solution)/shard_map/pack/pallas_call | solution.py:103
  13.9 47.6 %all_to_all.10.x_ref = bf16[16,3,128,128]{3,2,1,0:T(8,128)(2,1)S(1)} all-to-all(bf16[16,3,128,128]{3,2,1,0:T(8,128)(2,1)} %pack.1), channel_id=1, replica_groups=mesh['seq'=16,'fsdp'=32] {'seq'}, dimensions={0} | all-to-all | bytes 3145728 | tf_op jit(solution)/shard_map/all_to_all | solution.py:117
  61.5 0.0 copy-start.1
  61.5 10.2 %attend.1 = bf16[16,144,128]{2,1,0:T(8,128)(2,1)S(1)} custom-call(s32[1]{0:T(128)S(6)} %copy.16.length_ref, bf16[16,3,128,128]{3,2,1,0:T(8,128)(2,1)S(1)} %all_to_all.10.x_ref), custom_call_target="tpu_custom_call" | custom-call | tf_op jit(solution)/shard_map/attend/pallas_call | solution.py:119
  71.7 23.3 %all_to_all.11.x_ref = bf16[16,144,128]{2,1,0:T(8,128)(2,1)S(1)} all-to-all(bf16[16,144,128]{2,1,0:T(8,128)(2,1)S(1)} %attend.1), channel_id=1, replica_groups=mesh['seq'=16,'fsdp'=32] {'seq'}, dimensions={0} | all-to-all | bytes 1179648 | tf_op jit(solution)/shard_map/all_to_all | solution.py:132
  95.0 0.0 all-gather.2.cloned.1.call-done.w_ref
  95.0 0.0 copy-done.1
  95.0 0.0 copy-start
  95.0 2.3 %copy-done = bf16[1536,1536]{1,0:T(8,128)(2,1)S(1)} copy-done((bf16[1536,1536]{1,0:T(8,128)(2,1)S(1)}, bf16[1536,1536]{1,0:T(8,128)(2,1)}, u32[]{:S(2)}) %copy-start) | copy-done | bytes 4718616
  97.3 2.5 %project.1 = (bf16[120,1536]{1,0:T(8,128)(2,1)}, bf16[8,1536]{1,0:T(8,128)(2,1)}, f32[12,120]{1,0:T(8,128)S(1)}, f32[12,8]{1,0:T(8,128)S(1)}, bf16[120,1536]{1,0:T(8,128)(2,1)}) custom-call(bf16[16,144,128]{2,1,0:T(8,128)(2,1)S(1)} %all_to_all.11.x_ref, bf16[1536,1536]{1,0:T(8,128)(2,1)S(1)} %copy-done, f32[1,1536]{1,0:T(1,128)S(1)} %copy-done.1), custom_call_target="tpu_custom_call" | custom-call | tf_op jit(solution)/shard_map/project/pallas_call | solution.py:134
  99.8 0.6 copy.13
  100.4 0.7 copy.12
Async XLA Ops:
  7.2 3.5 %copy-start.2 = (bf16[1,8,2,1536]{3,2,1,0:T(2,128)(2,1)S(1)}, bf16[1,8,2,1536]{3,2,1,0:T(2,128)(2,1)}, u32[]{:S(2)}) copy-start(bf16[1,8,2,1536]{3,2,1,0:T(2,128)(2,1)} %param.10) | copy-start | bytes 147460
  7.2 87.8 %all-gather.2.cloned.1.call-start = ((), (), s32[]{:S(2)}) async-start(), calls=%async_computation.2 | async-start | bytes 4866048 | tf_op jit(solution)/shard_map/all_gather | solution.py:100
  61.5 33.5 %copy-start.1 = (f32[1,1536]{1,0:T(1,128)S(1)}, f32[1,1536]{1,0:T(1,128)}, u32[]{:S(2)}) copy-start(f32[1,1536]{1,0:T(1,128)} %gate_ref.1) | copy-start | bytes 18436
  95.0 2.3 %copy-start = (bf16[1536,1536]{1,0:T(8,128)(2,1)S(1)}, bf16[1536,1536]{1,0:T(8,128)(2,1)}, u32[]{:S(2)}) copy-start(bf16[1536,1536]{1,0:T(8,128)(2,1)} %all-gather.2.cloned.1.call-done.w_ref) | copy-start | bytes 14155780
Sparse Core Ops, SparseCore 0:
  11.1 80.9 all-gather.1

commit v2 on v1

v2 whole, which is shorter than its diff:
```python
import functools
import math

import jax
import jax.numpy as jnp
from jax import lax
from jax.experimental import pallas as pl
from jax.experimental.pallas import tpu as pltpu
from jax.sharding import Mesh
from jax.sharding import PartitionSpec as P

HEADS = 12
HEAD = 128
SLOPE = math.log2(math.e) / math.sqrt(HEAD)
LN2 = math.log(2.0)
LSE_ROWS = 16
FSDP = (4, 4, 2)
FSDP_AXES = ("zh", "x", "core")
GROUP = 4
VMEM = pltpu.VMEM


def pack_kernel(
    length_ref, base_ref, qv_hbm, kvv_hbm, qt_hbm, kvt_hbm, out_ref,
    qv_ref, kvv_ref, qt_ref, kvt_ref, split_ref, sems,
):
    vid = qv_ref.shape[0]
    txt = qt_ref.shape[0]
    pairs = ((kvv_hbm, kvv_ref), (kvt_hbm, kvt_ref), (qv_hbm, qv_ref), (qt_hbm, qt_ref))
    copies = [pltpu.make_async_copy(a, b, sems.at[i]) for i, (a, b) in enumerate(pairs)]
    for copy in copies:
        copy.start()
    for h in range(HEADS, out_ref.shape[0]):
        out_ref[h] = jnp.zeros(out_ref.shape[1:], jnp.bfloat16)
    copies[0].wait()
    copies[1].wait()
    slot = base_ref[0] + lax.broadcasted_iota(jnp.int32, (txt, HEAD), 0)
    valid = slot < length_ref[0]
    for h in range(HEADS):
        cols = pl.ds(h * HEAD, HEAD)
        video = kvv_ref[:, :, cols].astype(jnp.float32).reshape(2 * vid, HEAD)
        text = kvt_ref[:, :, cols].astype(jnp.float32).reshape(2 * txt, HEAD)
        split_ref[h, : 2 * vid] = video
        split_ref[h, 2 * vid :] = text
        keys = split_ref[h, pl.ds(0, vid, stride=2), :]
        text_keys = split_ref[h, pl.ds(2 * vid, txt, stride=2), :]
        text_values = split_ref[h, pl.ds(2 * vid + 1, txt, stride=2), :]
        out_ref[h, 1, :vid] = keys.astype(jnp.bfloat16)
        out_ref[h, 1, vid:] = jnp.where(valid, text_keys, keys[:1]).astype(jnp.bfloat16)
        out_ref[h, 2, :vid] = split_ref[h, pl.ds(1, vid, stride=2), :].astype(jnp.bfloat16)
        out_ref[h, 2, vid:] = jnp.where(valid, text_values, 0.0).astype(jnp.bfloat16)
    copies[2].wait()
    copies[3].wait()
    for h in range(HEADS):
        cols = pl.ds(h * HEAD, HEAD)
        out_ref[h, 0, :vid] = qv_ref[:, cols]
        out_ref[h, 0, vid:] = qt_ref[:, cols]


def attend_kernel(vid, length_ref, x_ref, out_ref, vals_ref, keys_ref, queries_ref):
    sources, _, rows, _ = x_ref.shape
    txt = rows - vid
    row = lax.broadcasted_iota(jnp.int32, (rows, HEAD), 0)
    for s in range(sources):
        valid = (row < vid) | (row - vid + s * txt < length_ref[0])
        here = pl.ds(s * rows, rows)
        queries_ref[here, :] = x_ref[s, 0]
        keys_ref[here, :] = x_ref[s, 1]
        vals_ref[here, :HEAD] = x_ref[s, 2]
        vals_ref[here, HEAD:] = jnp.where(valid, 1.0, 0.0).astype(jnp.bfloat16)

    def score(block):
        return lax.dot_general(
            queries_ref[pl.ds(block * GROUP * rows, GROUP * rows), :],
            keys_ref[...],
            (((1,), (1,)), ((), ())),
            preferred_element_type=jnp.float32,
        )

    blocks = sources // GROUP
    following = score(0)
    for block in range(blocks):
        scores = following
        if block + 1 < blocks:
            following = score(block + 1)
        best = jnp.max(scores, axis=1, keepdims=True) * SLOPE
        weights = jnp.exp2(scores * SLOPE - best).astype(jnp.bfloat16)
        both = jnp.dot(weights, vals_ref[...], preferred_element_type=jnp.float32)
        total = both[:, HEAD:]
        mixed = (both[:, :HEAD] / total).astype(jnp.bfloat16)
        wide = (best + jnp.log2(total)) * LN2
        for g in range(GROUP):
            s = block * GROUP + g
            out_ref[s, :rows] = mixed[g * rows : (g + 1) * rows]
            lse = wide[g * rows : (g + 1) * rows].T[:LSE_ROWS]
            high = lse.astype(jnp.bfloat16).astype(jnp.float32)
            mid = (lse - high).astype(jnp.bfloat16).astype(jnp.float32)
            which = lax.broadcasted_iota(jnp.int32, lse.shape, 0)
            parts = jnp.where(which == 0, high, jnp.where(which == 1, mid, lse - high - mid))
            out_ref[s, rows:] = parts.astype(jnp.bfloat16)


def project_kernel(place, *refs):
    x_ref, gate_ref, spot_ref, *pieces = refs[: -7]
    av_ref, at_ref, lv_ref, lt_ref, pv_ref, w_ref, sem = refs[-7:]
    vid = av_ref.shape[0]
    rows = vid + at_ref.shape[0]
    copies = [
        pltpu.make_async_copy(
            pieces[i].at[pl.ds(first, count), :],
            w_ref.at[pl.ds(pl.multiple_of(target, 16), count), :],
            sem,
        )
        for i, first, target, count in place(spot_ref)
    ]
    for copy in copies:
        copy.start()
    lses = []
    for h in range(HEADS):
        cols = pl.ds(h * HEAD, HEAD)
        av_ref[:, cols] = x_ref[h, :vid]
        at_ref[:, cols] = x_ref[h, vid:rows]
        parts = x_ref[h, rows:].astype(jnp.float32)
        lse = parts[0:1] + parts[1:2] + parts[2:3]
        lv_ref[h] = lse[:, :vid]
        lses.append(lse)
    lses += [lses[0]] * (HEAD - HEADS)
    lt_ref[...] = jnp.concatenate(lses, axis=0).T[vid:, :HEADS]
    for copy in copies:
        copy.wait()
    out = jnp.dot(av_ref[...], w_ref[...], preferred_element_type=jnp.float32)
    pv_ref[...] = (out * gate_ref[...]).astype(jnp.bfloat16)


def spot_of(zh, x, core, count):
    return ((zh * FSDP[1] + x) * FSDP[2] + core) * count


def ring(block, axis):
    n = lax.axis_size(axis)
    return [block] + [
        lax.ppermute(block, axis, [(i, (i + s) % n) for i in range(n)]) for s in range(1, n)
    ]


def gathered(w_out):
    column = jnp.concatenate(ring(w_out, "zh"), axis=0)
    mine = ring(column, "x")
    return (*mine, *(lax.ppermute(part, "core", [(0, 1), (1, 0)]) for part in mine))


def place(count, spot_ref):
    zh, x, core = spot_ref[0], spot_ref[1], spot_ref[2]
    return [
        (
            other * FSDP[1] + dx,
            dz * count,
            spot_of((zh + FSDP[0] - dz) % FSDP[0], (x + FSDP[1] - dx) % FSDP[1], core ^ other, count),
            count,
        )
        for other in range(FSDP[2])
        for dx in range(FSDP[1])
        for dz in range(FSDP[0])
    ]


def shards(sources, q_video, kv_video, q_text, kv_text, text_lengths, gate, w_out):
    vid, feats = q_video.shape[1:]
    txt = q_text.shape[1]
    rows = vid + txt
    base = (lax.axis_index("seq") * txt).astype(jnp.int32).reshape(1)
    pieces = gathered(w_out)
    spot = jnp.stack([lax.axis_index(axis) for axis in ("zh", "x", "core")]).astype(jnp.int32)
    smem = pl.BlockSpec(memory_space=pltpu.SMEM)
    vmem = pl.BlockSpec(memory_space=VMEM)
    anywhere = pl.BlockSpec(memory_space=pl.ANY)
    packed = pl.pallas_call(
        pack_kernel,
        out_shape=jax.ShapeDtypeStruct((sources, 3, rows, HEAD), jnp.bfloat16),
        in_specs=[smem, smem, anywhere, anywhere, anywhere, anywhere],
        out_specs=vmem,
        scratch_shapes=[
            VMEM((vid, feats), jnp.bfloat16),
            VMEM((vid, 2, feats), jnp.bfloat16),
            VMEM((txt, feats), jnp.bfloat16),
            VMEM((txt, 2, feats), jnp.bfloat16),
            VMEM((HEADS, 2 * rows, HEAD), jnp.float32),
            pltpu.SemaphoreType.DMA((4,)),
        ],
        compiler_params=pltpu.CompilerParams(vmem_limit_bytes=60 << 20),
        name="pack",
    )(
        text_lengths,
        base,
        q_video[0],
        kv_video[0],
        q_text[0],
        kv_text[0],
    )
    moved = lax.all_to_all(packed, "seq", 0, 0, tiled=True)
    mixed = pl.pallas_call(
        functools.partial(attend_kernel, vid),
        out_shape=jax.ShapeDtypeStruct((sources, rows + LSE_ROWS, HEAD), jnp.bfloat16),
        in_specs=[smem, vmem],
        out_specs=vmem,
        scratch_shapes=[
            VMEM((sources * rows, 2 * HEAD), jnp.bfloat16),
            VMEM((sources * rows, HEAD), jnp.bfloat16),
            VMEM((sources * rows, HEAD), jnp.bfloat16),
        ],
        compiler_params=pltpu.CompilerParams(vmem_limit_bytes=40 << 20),
        name="attend",
    )(text_lengths, moved)
    back = lax.all_to_all(mixed, "seq", 0, 0, tiled=True)
    attn_video, attn_text, lse_video, lse_text, proj_video = pl.pallas_call(
        functools.partial(project_kernel, functools.partial(place, w_out.shape[0])),
        out_shape=(
            jax.ShapeDtypeStruct((vid, feats), jnp.bfloat16),
            jax.ShapeDtypeStruct((txt, feats), jnp.bfloat16),
            jax.ShapeDtypeStruct((HEADS, 1, vid), jnp.float32),
            jax.ShapeDtypeStruct((txt, HEADS), jnp.float32),
            jax.ShapeDtypeStruct((vid, feats), jnp.bfloat16),
        ),
        in_specs=[vmem, vmem, smem, *[anywhere] * len(pieces)],
        out_specs=(vmem,) * 5,
        scratch_shapes=[VMEM((feats, feats), jnp.bfloat16), pltpu.SemaphoreType.DMA],
        compiler_params=pltpu.CompilerParams(vmem_limit_bytes=32 << 20),
        name="project",
    )(back, gate, spot, *pieces)
    return (
        attn_video[None],
        attn_text[None],
        lse_video.transpose(1, 0, 2),
        lse_text.T[None],
        proj_video[None],
    )


def solution(mesh):
    devices = mesh.devices.reshape(mesh.shape["seq"], *FSDP)
    mesh = Mesh(devices, ("seq", *FSDP_AXES))
    placed = (
        P(FSDP_AXES, "seq", None),
        P(FSDP_AXES, "seq", None, None),
        P(FSDP_AXES, "seq", None),
        P(FSDP_AXES, "seq", None, None),
        P(FSDP_AXES),
        P(FSDP_AXES, None),
        P(FSDP_AXES, None),
    )
    return jax.shard_map(
        functools.partial(shards, mesh.shape["seq"]),
        mesh=mesh,
        in_specs=placed,
        out_specs=(
            P(FSDP_AXES, "seq", None),
            P(FSDP_AXES, "seq", None),
            P(FSDP_AXES, None, "seq"),
            P(FSDP_AXES, None, "seq"),
            P(FSDP_AXES, "seq", None),
        ),
        check_vma=False,
    )
```

time: 110 us -> 106 us (0.964); the launches traced: 108 us -> 105 us
  blocking collectives: 70.9 us -> 0 us
  starting transfers between devices: 0.04 us -> 68.2 us
  waiting for transfers between devices: 0.68 us -> 18.4 us
  between operations: 14.7 us -> 1.5 us
  local copies, waits for them, and re-layouts: 6.31 us -> 0.06 us
  Pallas kernels: 15.3 us -> 17.1 us
    all_to_all x2 -> x0, blocking collectives: 70.9 us -> none  [the longest x1 47.6 us: shards(): moved = lax.all_to_all(packed, 'seq', 0, 0, tiled=True)]
    ppermute x0 -> x10, starting transfers between devices: none -> 37.5 us  [the longest x6 27.7 us: ring(): lax.ppermute(block, axis, [(i, (i + s) % n) for i in range(n)])]
    all_to_all x0 -> x2, starting transfers between devices: none -> 30.7 us  [the longest x1 21 us: shards(): back = lax.all_to_all(mixed, 'seq', 0, 0, tiled=True)]
    ppermute x0 -> x10, waiting for transfers between devices: none -> 13.7 us  [the longest x6 11.5 us: ring(): lax.ppermute(block, axis, [(i, (i + s) % n) for i in range(n)])]
    unnamed x9 -> x7, local copies, waits for them, and re-layouts: 5.64 us -> 0.05 us
    all_to_all x0 -> x2, waiting for transfers between devices: none -> 4.68 us  [the longest x1 4.67 us: shards(): back = lax.all_to_all(mixed, 'seq', 0, 0, tiled=True)]
    pallas_call x2, Pallas kernels: 12.7 us -> 14 us  [the longest x1 7.4 us: shards(): pl.pallas_call(functools.partial(project_kernel, functools.partial(place,...]
  transfers between devices with their start and end apart: 1 -> 12, of which waited for: 0 -> 3; matrix products, arithmetic and copies ran while one was open for 3% -> 0% of each run, Pallas kernels for 12% -> 6%
where the time goes in v2:
time: 106 us; the launch traced here: 105 us
  starting transfers between devices  68.2 us (64%)
  waiting for transfers between devices  18.4 us (17%)
  Pallas kernels  17.1 us (16%)
  between operations  1.5 us (1%)
    ppermute x6, starting transfers between devices, ring(): lax.ppermute(block, axis, [(i, (i + s) % n) for i in range(n)])  27.7 us
    all_to_all x1, starting transfers between devices, shards(): back = lax.all_to_all(mixed, 'seq', 0, 0, tiled=True)  21 us
    ppermute x6, waiting for transfers between devices, ring(): lax.ppermute(block, axis, [(i, (i + s) % n) for i in range(n)])  11.5 us
    ppermute x4, starting transfers between devices, gathered(): lax.ppermute(part, 'core', [(0, 1), (1, 0)])  9.77 us
    all_to_all x1, starting transfers between devices, shards(): moved = lax.all_to_all(packed, 'seq', 0, 0, tiled=True)  9.71 us
    pallas_call x1, Pallas kernels, shards(): pl.pallas_call(functools.partial(project_kernel, functools.partial(place,...  7.4 us
    pallas_call x1, Pallas kernels, shards(): pl.pallas_call(functools.partial(attend_kernel, vid), out_shape=jax.Shape...  6.6 us
    all_to_all x1, waiting for transfers between devices, shards(): back = lax.all_to_all(mixed, 'seq', 0, 0, tiled=True)  4.67 us
  transfers between devices with their start and end apart: 12, of which 3 were waited for; matrix products, arithmetic and copies ran while one was open for 0% of the time, Pallas kernels for 6%

profile of v2, /device:TPU:1, one launch (start us, length us, event | category | flops | bytes accessed | tf_op | source)
XLA Modules:
  0.0 105.3 jit_solution(978085994937522325)
XLA Ops:
  1.3 3.1 %pack.1 = bf16[16,3,128,128]{3,2,1,0:T(8,128)(2,1)} custom-call(s32[1]{0:T(128)S(6)} %copy.15.length_ref, s32[1]{0:T(128)} %bitcast.base_ref, bf16[120,1536]{1,0:T(8,128)(2,1)} %bitcast.16, bf16[120,2,1536]{2,1,0:T(2,128)(2,1)} %bitcast.15, bf16[8,1536]{1,0:T(8,128)(2,1)} %bitcast.18, bf16[8,2,1536]{2,1,0:T(2,128)(2,1)} %bitcast.17), custom_call_target="tpu_custom_call" | custom-call | tf_op jit(solution)/shard_map/pack/pallas_call | solution.py:177
  4.4 0.0 copy-start.1
  4.4 9.7 %all-to-all-start = ((bf16[16,3,128,128]{3,2,1,0:T(8,128)(2,1)}), bf16[16,3,128,128]{3,2,1,0:T(8,128)(2,1)S(1)}, u32[]{:S(2)}, u32[]{:S(2)}) async-start(bf16[16,3,128,128]{3,2,1,0:T(8,128)(2,1)} %pack.1), calls=%async_computation | async-start | bytes 3145728 | tf_op jit(solution)/shard_map/all_to_all | solution.py:200
  14.1 5.8 %collective-permute-start = (bf16[48,1536]{1,0:T(8,128)(2,1)S(1)}, bf16[48,1536]{1,0:T(8,128)(2,1)S(1)}, u32[]{:S(2)}, u32[]{:S(2)}) collective-permute-start(bf16[48,1536]{1,0:T(8,128)(2,1)S(1)} %copy-done.1), channel_id=1, source_target_pairs={{0,8},{8,16},{16,24},{24,0},{1,9},{9,17},{17,25},{25,1},{2,10},{10... | collective-permute-start | bytes 442376 | tf_op jit(solution)/shard_map/ppermute | solution.py:142
  19.9 7.9 %collective-permute-start.1 = (bf16[48,1536]{1,0:T(8,128)(2,1)S(1)}, bf16[48,1536]{1,0:T(8,128)(2,1)S(1)}, u32[]{:S(2)}, u32[]{:S(2)}) collective-permute-start(bf16[48,1536]{1,0:T(8,128)(2,1)S(1)} %copy-done.1), channel_id=1, source_target_pairs={{0,16},{8,24},{16,0},{24,8},{1,17},{9,25},{17,1},{25,9},{2,18},{10... | collective-permute-start | bytes 442376 | tf_op jit(solution)/shard_map/ppermute | solution.py:142
  27.9 3.4 %collective-permute-start.2 = (bf16[48,1536]{1,0:T(8,128)(2,1)S(1)}, bf16[48,1536]{1,0:T(8,128)(2,1)S(1)}, u32[]{:S(2)}, u32[]{:S(2)}) collective-permute-start(bf16[48,1536]{1,0:T(8,128)(2,1)S(1)} %copy-done.1), channel_id=1, source_target_pairs={{0,24},{8,0},{16,8},{24,16},{1,25},{9,1},{17,9},{25,17},{2,26},{10... | collective-permute-start | bytes 442376 | tf_op jit(solution)/shard_map/ppermute | solution.py:142
  31.3 11.5 %collective-permute-done.1 = bf16[48,1536]{1,0:T(8,128)(2,1)S(1)} collective-permute-done((bf16[48,1536]{1,0:T(8,128)(2,1)S(1)}, bf16[48,1536]{1,0:T(8,128)(2,1)S(1)}, u32[]{:S(2)}, u32[]{:S(2)}) %collective-permute-start.1) | collective-permute-done | bytes 147488 | tf_op jit(solution)/shard_map/ppermute | solution.py:142
  42.8 0.0 collective-permute-done.2
  42.8 0.0 copy-start
  42.8 3.2 %collective-permute-start.3 = (bf16[192,1536]{1,0:T(8,128)(2,1)S(1)}, bf16[192,1536]{1,0:T(8,128)(2,1)S(1)}, u32[]{:S(2)}, u32[]{:S(2)}) collective-permute-start(bf16[192,1536]{1,0:T(8,128)(2,1)S(1)} %constant_dynamic-update-slice_fusion.refs_3_), channel_id=1, source_target_pairs={{0,2},{2,4},{4,6},{6,0},{1,3},{3,5},{5,7},{7,1},{8,10},{10,12},{12... | collective-permute-start | bytes 1769480 | tf_op jit(solution)/shard_map/ppermute | solution.py:142
  46.0 4.4 %collective-permute-start.4 = (bf16[192,1536]{1,0:T(8,128)(2,1)S(1)}, bf16[192,1536]{1,0:T(8,128)(2,1)S(1)}, u32[]{:S(2)}, u32[]{:S(2)}) collective-permute-start(bf16[192,1536]{1,0:T(8,128)(2,1)S(1)} %constant_dynamic-update-slice_fusion.refs_3_), channel_id=1, source_target_pairs={{0,4},{2,6},{4,0},{6,2},{1,5},{3,7},{5,1},{7,3},{8,12},{10,14},{12... | collective-permute-start | bytes 1769480 | tf_op jit(solution)/shard_map/ppermute | solution.py:142
  50.4 3.1 %collective-permute-start.5 = (bf16[192,1536]{1,0:T(8,128)(2,1)S(1)}, bf16[192,1536]{1,0:T(8,128)(2,1)}, u32[]{:S(2)}, u32[]{:S(2)}) collective-permute-start(bf16[192,1536]{1,0:T(8,128)(2,1)S(1)} %constant_dynamic-update-slice_fusion.refs_3_), channel_id=1, source_target_pairs={{0,6},{2,0},{4,2},{6,4},{1,7},{3,1},{5,3},{7,5},{8,14},{10,8},{12,... | collective-permute-start | bytes 1769480 | tf_op jit(solution)/shard_map/ppermute | solution.py:142
  53.4 0.0 all-to-all-done.x_ref
  53.5 6.6 %attend.1 = bf16[16,144,128]{2,1,0:T(8,128)(2,1)} custom-call(s32[1]{0:T(128)S(6)} %copy.15.length_ref, bf16[16,3,128,128]{3,2,1,0:T(8,128)(2,1)S(1)} %all-to-all-done.x_ref), custom_call_target="tpu_custom_call" | custom-call | tf_op jit(solution)/shard_map/attend/pallas_call | solution.py:201
  60.1 21.0 %all-to-all-start.1 = ((bf16[16,144,128]{2,1,0:T(8,128)(2,1)}), bf16[16,144,128]{2,1,0:T(8,128)(2,1)S(1)}, u32[]{:S(2)}, u32[]{:S(2)}) async-start(bf16[16,144,128]{2,1,0:T(8,128)(2,1)} %attend.1), calls=%async_computation.1 | async-start | bytes 1179648 | tf_op jit(solution)/shard_map/all_to_all | solution.py:214
  81.1 3.5 %collective-permute-start.6 = (bf16[192,1536]{1,0:T(8,128)(2,1)S(1)}, bf16[192,1536]{1,0:T(8,128)(2,1)S(1)}, u32[]{:S(2)}, u32[]{:S(2)}) collective-permute-start(bf16[192,1536]{1,0:T(8,128)(2,1)S(1)} %constant_dynamic-update-slice_fusion.refs_3_), channel_id=1, source_target_pairs={{0,1},{1,0},{2,3},{3,2},{4,5},{5,4},{6,7},{7,6},{8,9},{9,8},{10,11... | collective-permute-start | bytes 1769480 | tf_op jit(solution)/shard_map/ppermute | solution.py:149
  84.6 0.0 collective-permute-done.3.refs_4_
  84.6 1.9 %collective-permute-start.7 = (bf16[192,1536]{1,0:T(8,128)(2,1)S(1)}, bf16[192,1536]{1,0:T(8,128)(2,1)}, u32[]{:S(2)}, u32[]{:S(2)}) collective-permute-start(bf16[192,1536]{1,0:T(8,128)(2,1)S(1)} %collective-permute-done.3.refs_4_), channel_id=1, source_target_pairs={{0,1},{1,0},{2,3},{3,2},{4,5},{5,4},{6,7},{7,6},{8,9},{9,8},{10,11... | collective-permute-start | bytes 1769480 | tf_op jit(solution)/shard_map/ppermute | solution.py:149
  86.5 2.4 %collective-permute-start.8 = (bf16[192,1536]{1,0:T(8,128)(2,1)S(1)}, bf16[192,1536]{1,0:T(8,128)(2,1)}, u32[]{:S(2)}, u32[]{:S(2)}) collective-permute-start(bf16[192,1536]{1,0:T(8,128)(2,1)S(1)} %collective-permute-done.4.refs_5_), channel_id=1, source_target_pairs={{0,1},{1,0},{2,3},{3,2},{4,5},{5,4},{6,7},{7,6},{8,9},{9,8},{10,11... | collective-permute-start | bytes 1769480 | tf_op jit(solution)/shard_map/ppermute | solution.py:149
  89.0 1.9 %collective-permute-start.9 = (bf16[192,1536]{1,0:T(8,128)(2,1)}, bf16[192,1536]{1,0:T(8,128)(2,1)}, u32[]{:S(2)}, u32[]{:S(2)}) collective-permute-start(bf16[192,1536]{1,0:T(8,128)(2,1)} %collective-permute-done.5.refs_6_), channel_id=1, source_target_pairs={{0,1},{1,0},{2,3},{3,2},{4,5},{5,4},{6,7},{7,6},{8,9},{9,8},{10,11... | collective-permute-start | bytes 1769480 | tf_op jit(solution)/shard_map/ppermute | solution.py:149
  90.9 0.1 pad_add_fusion.refs_2_
  91.0 2.2 %collective-permute-done.9.refs_10_ = bf16[192,1536]{1,0:T(8,128)(2,1)} collective-permute-done((bf16[192,1536]{1,0:T(8,128)(2,1)}, bf16[192,1536]{1,0:T(8,128)(2,1)}, u32[]{:S(2)}, u32[]{:S(2)}) %collective-permute-start.9) | collective-permute-done | bytes 589856 | tf_op jit(solution)/shard_map/ppermute | solution.py:149
  93.2 4.7 %all-to-all-done.1.refs_0_ = bf16[16,144,128]{2,1,0:T(8,128)(2,1)S(1)} async-done(((bf16[16,144,128]{2,1,0:T(8,128)(2,1)}), bf16[16,144,128]{2,1,0:T(8,128)(2,1)S(1)}, u32[]{:S(2)}, u32[]{:S(2)}) %all-to-all-start.1) | async-done | bytes 589856 | tf_op jit(solution)/shard_map/all_to_all | solution.py:214
  97.9 7.4 %project.1 = (bf16[120,1536]{1,0:T(8,128)(2,1)}, bf16[8,1536]{1,0:T(8,128)(2,1)}, f32[12,1,120]{2,1,0:T(1,128)}, f32[8,12]{1,0:T(8,128)}, bf16[120,1536]{1,0:T(8,128)(2,1)}) custom-call(bf16[16,144,128]{2,1,0:T(8,128)(2,1)S(1)} %all-to-all-done.1.refs_0_, f32[1,1536]{1,0:T(1,128)S(1)} %copy-done, s32[3]{0:T(128)S(1)} %pad_add_fusion.refs_2_, ...), custom_call_target="tpu_custom_call" | custom-call | tf_op jit(solution)/shard_map/project/pallas_call | solution.py:215
  (12 shorter events, 0.1 us)
Async XLA Ops:
  4.4 9.7 %copy-start.1 = (bf16[48,1536]{1,0:T(8,128)(2,1)S(1)}, bf16[48,1536]{1,0:T(8,128)(2,1)}, u32[]{:S(2)}) copy-start(bf16[48,1536]{1,0:T(8,128)(2,1)} %param.13) | copy-start | bytes 442372
  4.4 49.1 %all-to-all-start = ((bf16[16,3,128,128]{3,2,1,0:T(8,128)(2,1)}), bf16[16,3,128,128]{3,2,1,0:T(8,128)(2,1)S(1)}, u32[]{:S(2)}, u32[]{:S(2)}) async-start(bf16[16,3,128,128]{3,2,1,0:T(8,128)(2,1)} %pack.1), calls=%async_computation | async-start | bytes 3145728 | tf_op jit(solution)/shard_map/all_to_all | solution.py:200
  14.1 17.2 %collective-permute-start = (bf16[48,1536]{1,0:T(8,128)(2,1)S(1)}, bf16[48,1536]{1,0:T(8,128)(2,1)S(1)}, u32[]{:S(2)}, u32[]{:S(2)}) collective-permute-start(bf16[48,1536]{1,0:T(8,128)(2,1)S(1)} %copy-done.1), channel_id=1, source_target_pairs={{0,8},{8,16},{16,24},{24,0},{1,9},{9,17},{17,25},{25,1},{2,10},{10... | collective-permute-start | bytes 442376 | tf_op jit(solution)/shard_map/ppermute | solution.py:142
  19.9 22.9 %collective-permute-start.1 = (bf16[48,1536]{1,0:T(8,128)(2,1)S(1)}, bf16[48,1536]{1,0:T(8,128)(2,1)S(1)}, u32[]{:S(2)}, u32[]{:S(2)}) collective-permute-start(bf16[48,1536]{1,0:T(8,128)(2,1)S(1)} %copy-done.1), channel_id=1, source_target_pairs={{0,16},{8,24},{16,0},{24,8},{1,17},{9,25},{17,1},{25,9},{2,18},{10... | collective-permute-start | bytes 442376 | tf_op jit(solution)/shard_map/ppermute | solution.py:142
  27.9 14.9 %collective-permute-start.2 = (bf16[48,1536]{1,0:T(8,128)(2,1)S(1)}, bf16[48,1536]{1,0:T(8,128)(2,1)S(1)}, u32[]{:S(2)}, u32[]{:S(2)}) collective-permute-start(bf16[48,1536]{1,0:T(8,128)(2,1)S(1)} %copy-done.1), channel_id=1, source_target_pairs={{0,24},{8,0},{16,8},{24,16},{1,25},{9,1},{17,9},{25,17},{2,26},{10... | collective-permute-start | bytes 442376 | tf_op jit(solution)/shard_map/ppermute | solution.py:142
  42.8 55.1 %copy-start = (f32[1,1536]{1,0:T(1,128)S(1)}, f32[1,1536]{1,0:T(1,128)}, u32[]{:S(2)}) copy-start(f32[1,1536]{1,0:T(1,128)} %refs_1_.1) | copy-start | bytes 18436
  42.8 41.8 %collective-permute-start.3 = (bf16[192,1536]{1,0:T(8,128)(2,1)S(1)}, bf16[192,1536]{1,0:T(8,128)(2,1)S(1)}, u32[]{:S(2)}, u32[]{:S(2)}) collective-permute-start(bf16[192,1536]{1,0:T(8,128)(2,1)S(1)} %constant_dynamic-update-slice_fusion.refs_3_), channel_id=1, source_target_pairs={{0,2},{2,4},{4,6},{6,0},{1,3},{3,5},{5,7},{7,1},{8,10},{10,12},{12... | collective-permute-start | bytes 1769480 | tf_op jit(solution)/shard_map/ppermute | solution.py:142
  46.0 40.5 %collective-permute-start.4 = (bf16[192,1536]{1,0:T(8,128)(2,1)S(1)}, bf16[192,1536]{1,0:T(8,128)(2,1)S(1)}, u32[]{:S(2)}, u32[]{:S(2)}) collective-permute-start(bf16[192,1536]{1,0:T(8,128)(2,1)S(1)} %constant_dynamic-update-slice_fusion.refs_3_), channel_id=1, source_target_pairs={{0,4},{2,6},{4,0},{6,2},{1,5},{3,7},{5,1},{7,3},{8,12},{10,14},{12... | collective-permute-start | bytes 1769480 | tf_op jit(solution)/shard_map/ppermute | solution.py:142
  50.4 38.6 %collective-permute-start.5 = (bf16[192,1536]{1,0:T(8,128)(2,1)S(1)}, bf16[192,1536]{1,0:T(8,128)(2,1)}, u32[]{:S(2)}, u32[]{:S(2)}) collective-permute-start(bf16[192,1536]{1,0:T(8,128)(2,1)S(1)} %constant_dynamic-update-slice_fusion.refs_3_), channel_id=1, source_target_pairs={{0,6},{2,0},{4,2},{6,4},{1,7},{3,1},{5,3},{7,5},{8,14},{10,8},{12,... | collective-permute-start | bytes 1769480 | tf_op jit(solution)/shard_map/ppermute | solution.py:142
  60.1 37.8 %all-to-all-start.1 = ((bf16[16,144,128]{2,1,0:T(8,128)(2,1)}), bf16[16,144,128]{2,1,0:T(8,128)(2,1)S(1)}, u32[]{:S(2)}, u32[]{:S(2)}) async-start(bf16[16,144,128]{2,1,0:T(8,128)(2,1)} %attend.1), calls=%async_computation.1 | async-start | bytes 1179648 | tf_op jit(solution)/shard_map/all_to_all | solution.py:214
  81.1 9.9 %collective-permute-start.6 = (bf16[192,1536]{1,0:T(8,128)(2,1)S(1)}, bf16[192,1536]{1,0:T(8,128)(2,1)S(1)}, u32[]{:S(2)}, u32[]{:S(2)}) collective-permute-start(bf16[192,1536]{1,0:T(8,128)(2,1)S(1)} %constant_dynamic-update-slice_fusion.refs_3_), channel_id=1, source_target_pairs={{0,1},{1,0},{2,3},{3,2},{4,5},{5,4},{6,7},{7,6},{8,9},{9,8},{10,11... | collective-permute-start | bytes 1769480 | tf_op jit(solution)/shard_map/ppermute | solution.py:149
  84.6 6.4 %collective-permute-start.7 = (bf16[192,1536]{1,0:T(8,128)(2,1)S(1)}, bf16[192,1536]{1,0:T(8,128)(2,1)}, u32[]{:S(2)}, u32[]{:S(2)}) collective-permute-start(bf16[192,1536]{1,0:T(8,128)(2,1)S(1)} %collective-permute-done.3.refs_4_), channel_id=1, source_target_pairs={{0,1},{1,0},{2,3},{3,2},{4,5},{5,4},{6,7},{7,6},{8,9},{9,8},{10,11... | collective-permute-start | bytes 1769480 | tf_op jit(solution)/shard_map/ppermute | solution.py:149
  86.5 4.4 %collective-permute-start.8 = (bf16[192,1536]{1,0:T(8,128)(2,1)S(1)}, bf16[192,1536]{1,0:T(8,128)(2,1)}, u32[]{:S(2)}, u32[]{:S(2)}) collective-permute-start(bf16[192,1536]{1,0:T(8,128)(2,1)S(1)} %collective-permute-done.4.refs_5_), channel_id=1, source_target_pairs={{0,1},{1,0},{2,3},{3,2},{4,5},{5,4},{6,7},{7,6},{8,9},{9,8},{10,11... | collective-permute-start | bytes 1769480 | tf_op jit(solution)/shard_map/ppermute | solution.py:149
  89.0 4.2 %collective-permute-start.9 = (bf16[192,1536]{1,0:T(8,128)(2,1)}, bf16[192,1536]{1,0:T(8,128)(2,1)}, u32[]{:S(2)}, u32[]{:S(2)}) collective-permute-start(bf16[192,1536]{1,0:T(8,128)(2,1)} %collective-permute-done.5.refs_6_), channel_id=1, source_target_pairs={{0,1},{1,0},{2,3},{3,2},{4,5},{5,4},{6,7},{7,6},{8,9},{9,8},{10,11... | collective-permute-start | bytes 1769480 | tf_op jit(solution)/shard_map/ppermute | solution.py:149

commit v3 on v2

--- a/solution.py
+++ b/solution.py
@@ -14,8 +14,9 @@
 SLOPE = math.log2(math.e) / math.sqrt(HEAD)
 LN2 = math.log(2.0)
 LSE_ROWS = 16
-FSDP = (4, 4, 2)
-FSDP_AXES = ("zh", "x", "core")
+SIZES = {"y": 8, "zl": 2, "zh": 4, "x": 4, "core": 2}
+SEQ = ("y", "zl")
+FSDP = ("zh", "x", "core")
 GROUP = 4
 VMEM = pltpu.VMEM
 
@@ -100,21 +101,11 @@
             out_ref[s, rows:] = parts.astype(jnp.bfloat16)
 
 
-def project_kernel(place, *refs):
-    x_ref, gate_ref, spot_ref, *pieces = refs[: -7]
-    av_ref, at_ref, lv_ref, lt_ref, pv_ref, w_ref, sem = refs[-7:]
+def project_kernel(
+    x_ref, w_ref, more_ref, gate_ref, av_ref, at_ref, lv_ref, lt_ref, pv_ref
+):
     vid = av_ref.shape[0]
     rows = vid + at_ref.shape[0]
-    copies = [
-        pltpu.make_async_copy(
-            pieces[i].at[pl.ds(first, count), :],
-            w_ref.at[pl.ds(pl.multiple_of(target, 16), count), :],
-            sem,
-        )
-        for i, first, target, count in place(spot_ref)
-    ]
-    for copy in copies:
-        copy.start()
     lses = []
     for h in range(HEADS):
         cols = pl.ds(h * HEAD, HEAD)
@@ -126,51 +117,57 @@
         lses.append(lse)
     lses += [lses[0]] * (HEAD - HEADS)
     lt_ref[...] = jnp.concatenate(lses, axis=0).T[vid:, :HEADS]
-    for copy in copies:
-        copy.wait()
-    out = jnp.dot(av_ref[...], w_ref[...], preferred_element_type=jnp.float32)
-    pv_ref[...] = (out * gate_ref[...]).astype(jnp.bfloat16)
-
-
-def spot_of(zh, x, core, count):
-    return ((zh * FSDP[1] + x) * FSDP[2] + core) * count
-
-
-def ring(block, axis):
-    n = lax.axis_size(axis)
-    return [block] + [
-        lax.ppermute(block, axis, [(i, (i + s) % n) for i in range(n)]) for s in range(1, n)
-    ]
+    split = w_ref.shape[1]
+    for part, here in ((w_ref, pl.ds(0, split)), (more_ref, pl.ds(split, more_ref.shape[1]))):
+        out = jnp.dot(av_ref[...], part[...], preferred_element_type=jnp.float32)
+        pv_ref[:, here] = (out * gate_ref[:, here]).astype(jnp.bfloat16)
+
+
+def order_kernel(count, spot_ref, *refs):
+    *pieces, w_ref, more_ref = refs
+    split = w_ref.shape[1]
+    zl, zh, x, core = spot_ref[0], spot_ref[1], spot_ref[2], spot_ref[3]
+    nz, nx = SIZES["zh"], SIZES["x"]
+    near = 2 * zl - 1 + nz
+    of_z = (zh, zh + near, zh + nz - near, zh + nz // 2)
+    of_x = (x, x + nx - 1, x + 1, x + nx // 2)
+    for i, piece in enumerate(pieces):
+        which = i % len(of_x)
+        for j in range(len(of_z)):
+            row = (of_z[j] + nz) % nz * nx + (of_x[which]) % nx
+            row = (row * SIZES["core"] + (core ^ (i // len(of_x)))) * count
+            target = pl.ds(pl.multiple_of(row, 16), count)
+            w_ref[target, :] = piece[pl.ds(j * count, count), :split]
+            more_ref[target, :] = piece[pl.ds(j * count, count), split:]
 
 
 def gathered(w_out):
-    column = jnp.concatenate(ring(w_out, "zh"), axis=0)
-    mine = ring(column, "x")
-    return (*mine, *(lax.ppermute(part, "core", [(0, 1), (1, 0)]) for part in mine))
-
-
-def place(count, spot_ref):
-    zh, x, core = spot_ref[0], spot_ref[1], spot_ref[2]
-    return [
-        (
-            other * FSDP[1] + dx,
-            dz * count,
-            spot_of((zh + FSDP[0] - dz) % FSDP[0], (x + FSDP[1] - dx) % FSDP[1], core ^ other, count),
-            count,
-        )
-        for other in range(FSDP[2])
-        for dx in range(FSDP[1])
-        for dz in range(FSDP[0])
-    ]
+    nz, nx = SIZES["zh"], SIZES["x"]
+    between = []
+    for zh in range(nz):
+        here, there = nz + zh, (zh + 1) % nz
+        between += [(here, there), (there, here)]
+    first = lax.ppermute(w_out, ("zl", "zh"), between)
+    second = lax.ppermute(first, "zl", [(0, 1), (1, 0)])
+    third = lax.ppermute(second, ("zl", "zh"), between)
+    column = jnp.concatenate([w_out, first, second, third], axis=0)
+    up = [(i, (i + 1) % nx) for i in range(nx)]
+    down = [(i, (i - 1) % nx) for i in range(nx)]
+    left = lax.ppermute(column, "x", up)
+    right = lax.ppermute(column, "x", down)
+    half = column.shape[0] // 2
+    far = [lax.ppermute(left[:half], "x", up), lax.ppermute(right[half:], "x", down)]
+    mine = [column, left, right, jnp.concatenate(far, axis=0)]
+    return mine + [lax.ppermute(part, "core", [(0, 1), (1, 0)]) for part in mine]
 
 
 def shards(sources, q_video, kv_video, q_text, kv_text, text_lengths, gate, w_out):
     vid, feats = q_video.shape[1:]
     txt = q_text.shape[1]
     rows = vid + txt
-    base = (lax.axis_index("seq") * txt).astype(jnp.int32).reshape(1)
+    base = (lax.axis_index(SEQ) * txt).astype(jnp.int32).reshape(1)
     pieces = gathered(w_out)
-    spot = jnp.stack([lax.axis_index(axis) for axis in ("zh", "x", "core")]).astype(jnp.int32)
+    spot = jnp.stack([lax.axis_index(axis) for axis in ("zl", "zh", "x", "core")])
     smem = pl.BlockSpec(memory_space=pltpu.SMEM)
     vmem = pl.BlockSpec(memory_space=VMEM)
     anywhere = pl.BlockSpec(memory_space=pl.ANY)
@@ -197,7 +194,7 @@
         q_text[0],
         kv_text[0],
     )
-    moved = lax.all_to_all(packed, "seq", 0, 0, tiled=True)
+    moved = lax.all_to_all(packed, SEQ, 0, 0, tiled=True)
     mixed = pl.pallas_call(
         functools.partial(attend_kernel, vid),
         out_shape=jax.ShapeDtypeStruct((sources, rows + LSE_ROWS, HEAD), jnp.bfloat16),
@@ -211,9 +208,17 @@
         compiler_params=pltpu.CompilerParams(vmem_limit_bytes=40 << 20),
         name="attend",
     )(text_lengths, moved)
-    back = lax.all_to_all(mixed, "seq", 0, 0, tiled=True)
+    back = lax.all_to_all(mixed, SEQ, 0, 0, tiled=True)
+    halves = pl.pallas_call(
+        functools.partial(order_kernel, w_out.shape[0]),
+        out_shape=(jax.ShapeDtypeStruct((feats, feats // 2), jnp.bfloat16),) * 2,
+        in_specs=[smem, *[vmem] * len(pieces)],
+        out_specs=(vmem,) * 2,
+        compiler_params=pltpu.CompilerParams(vmem_limit_bytes=32 << 20),
+        name="order",
+    )(spot.astype(jnp.int32), *pieces)
     attn_video, attn_text, lse_video, lse_text, proj_video = pl.pallas_call(
-        functools.partial(project_kernel, functools.partial(place, w_out.shape[0])),
+        project_kernel,
         out_shape=(
             jax.ShapeDtypeStruct((vid, feats), jnp.bfloat16),
             jax.ShapeDtypeStruct((txt, feats), jnp.bfloat16),
@@ -221,12 +226,11 @@
             jax.ShapeDtypeStruct((txt, HEADS), jnp.float32),
             jax.ShapeDtypeStruct((vid, feats), jnp.bfloat16),
         ),
-        in_specs=[vmem, vmem, smem, *[anywhere] * len(pieces)],
+        in_specs=[vmem] * 4,
         out_specs=(vmem,) * 5,
-        scratch_shapes=[VMEM((feats, feats), jnp.bfloat16), pltpu.SemaphoreType.DMA],
         compiler_params=pltpu.CompilerParams(vmem_limit_bytes=32 << 20),
         name="project",
-    )(back, gate, spot, *pieces)
+    )(back, *halves, gate)
     return (
         attn_video[None],
         attn_text[None],
@@ -237,27 +241,27 @@
 
 
 def solution(mesh):
-    devices = mesh.devices.reshape(mesh.shape["seq"], *FSDP)
-    mesh = Mesh(devices, ("seq", *FSDP_AXES))
+    sources = mesh.shape["seq"]
+    mesh = Mesh(mesh.devices.reshape(tuple(SIZES.values())), tuple(SIZES))
     placed = (
-        P(FSDP_AXES, "seq", None),
-        P(FSDP_AXES, "seq", None, None),
-        P(FSDP_AXES, "seq", None),
-        P(FSDP_AXES, "seq", None, None),
-        P(FSDP_AXES),
-        P(FSDP_AXES, None),
-        P(FSDP_AXES, None),
+        P(FSDP, SEQ, None),
+        P(FSDP, SEQ, None, None),
+        P(FSDP, SEQ, None),
+        P(FSDP, SEQ, None, None),
+        P(FSDP),
+        P(FSDP, None),
+        P(FSDP, None),
     )
     return jax.shard_map(
-        functools.partial(shards, mesh.shape["seq"]),
+        functools.partial(shards, sources),
         mesh=mesh,
         in_specs=placed,
         out_specs=(
-            P(FSDP_AXES, "seq", None),
-            P(FSDP_AXES, "seq", None),
-            P(FSDP_AXES, None, "seq"),
-            P(FSDP_AXES, None, "seq"),
-            P(FSDP_AXES, "seq", None),
+            P(FSDP, SEQ, None),
+            P(FSDP, SEQ, None),
+            P(FSDP, None, SEQ),
+            P(FSDP, None, SEQ),
+            P(FSDP, SEQ, None),
         ),
         check_vma=False,
     )

time: 106 us -> 112 us (1.057)
  local copies, waits for them, and re-layouts: 0.06 us -> 13.3 us
  Pallas kernels: 17.1 us -> 13.2 us
  starting transfers between devices: 68.2 us -> 66.2 us
  waiting for transfers between devices: 18.4 us -> 16.8 us
    unnamed x7 -> x24, local copies, waits for them, and re-layouts: 0.05 us -> 10.9 us
    all_to_all x2, starting transfers between devices: 30.7 us -> 23.7 us  [the longest x1 14.1 us: shards(): back = lax.all_to_all(mixed, SEQ, 0, 0, tiled=True)]
    ppermute x6 -> x7, waiting for transfers between devices: 11.5 us -> 16.4 us  [the longest x1 7.65 us: gathered(): left = lax.ppermute(column, 'x', up)]
    all_to_all x2, waiting for transfers between devices: 4.68 us -> 0.01 us  [the longest x1 0.01 us: shards(): back = lax.all_to_all(mixed, SEQ, 0, 0, tiled=True)]
    pallas_call x1 -> x2, Pallas kernels: 7.4 us -> 3.56 us  [the longest x1 2.03 us: shards(): pl.pallas_call(functools.partial(order_kernel, w_out.shape[0]), out_shape...]
    ppermute x4, starting transfers between devices: 9.77 us -> 13.5 us  [gathered(): lax.ppermute(part, 'core', [(0, 1), (1, 0)])]
    ppermute x4, waiting for transfers between devices: 2.22 us -> 0.37 us  [gathered(): lax.ppermute(part, 'core', [(0, 1), (1, 0)])]
    concatenate x1 -> x2, local copies, waits for them, and re-layouts: 0.01 us -> 1.65 us  [the longest x1 0.98 us: gathered(): mine = [column, left, right, jnp.concatenate(far, axis=0)]]
  transfers between devices with their start and end apart: 12 -> 13, of which waited for: 3 -> 5; matrix products, arithmetic and copies ran while one was open for 0% -> 5% of each run, Pallas kernels for 6% -> 8%
where the time goes in v3:
time: 112 us; the launch traced here: 111 us
  starting transfers between devices  66.2 us (59%)
  waiting for transfers between devices  16.8 us (15%)
  local copies, waits for them, and re-layouts  13.3 us (12%)
  Pallas kernels  13.2 us (12%)
  between operations  1.51 us (1%)
    all_to_all x1, starting transfers between devices, shards(): back = lax.all_to_all(mixed, SEQ, 0, 0, tiled=True)  14.1 us
    ppermute x4, starting transfers between devices, gathered(): lax.ppermute(part, 'core', [(0, 1), (1, 0)])  13.5 us
    unnamed x24, local copies, waits for them, and re-layouts  10.9 us
    ppermute x1, starting transfers between devices, gathered(): first = lax.ppermute(w_out, ('zl', 'zh'), between)  9.94 us
    all_to_all x1, starting transfers between devices, shards(): moved = lax.all_to_all(packed, SEQ, 0, 0, tiled=True)  9.58 us
    ppermute x1, waiting for transfers between devices, gathered(): left = lax.ppermute(column, 'x', up)  7.65 us
    pallas_call x1, Pallas kernels, shards(): pl.pallas_call(functools.partial(attend_kernel, vid), out_shape=jax.Shape...  6.55 us
    ppermute x1, starting transfers between devices, gathered(): lax.ppermute(right[half:], 'x', down)  4.56 us
  transfers between devices with their start and end apart: 13, of which 5 were waited for; matrix products, arithmetic and copies ran while one was open for 5% of the time, Pallas kernels for 8%

profile of v3, /device:TPU:1, one launch (start us, length us, event | category | flops | bytes accessed | tf_op | source)
XLA Modules:
  0.0 111.1 jit_solution(1759423274273457226)
XLA Ops:
  1.3 3.1 %pack.1 = bf16[16,3,128,128]{3,2,1,0:T(8,128)(2,1)} custom-call(s32[1]{0:T(128)S(6)} %copy.16.length_ref, s32[1]{0:T(128)} %bitcast.base_ref, bf16[120,1536]{1,0:T(8,128)(2,1)} %bitcast.17, bf16[120,2,1536]{2,1,0:T(2,128)(2,1)} %bitcast.16, bf16[8,1536]{1,0:T(8,128)(2,1)} %bitcast.19, bf16[8,2,1536]{2,1,0:T(2,128)(2,1)} %bitcast.18), custom_call_target="tpu_custom_call" | custom-call | tf_op jit(solution)/shard_map/pack/pallas_call | solution.py:174
  4.4 9.6 %all-to-all-start = ((bf16[16,3,128,128]{3,2,1,0:T(8,128)(2,1)}), bf16[16,3,128,128]{3,2,1,0:T(8,128)(2,1)S(1)}, u32[]{:S(2)}, u32[]{:S(2)}) async-start(bf16[16,3,128,128]{3,2,1,0:T(8,128)(2,1)} %pack.1), calls=%async_computation | async-start | bytes 3145728 | tf_op jit(solution)/shard_map/all_to_all | solution.py:197
  14.0 9.9 %collective-permute-start = (bf16[48,1536]{1,0:T(8,128)(2,1)S(1)}, bf16[48,1536]{1,0:T(8,128)(2,1)S(1)}, u32[]{:S(2)}, u32[]{:S(2)}) collective-permute-start(bf16[48,1536]{1,0:T(8,128)(2,1)S(1)} %copy-done.9), channel_id=1, source_target_pairs={{32,8},{8,32},{40,16},{16,40},{48,24},{24,48},{56,0},{0,56},{33,9}... | collective-permute-start | bytes 442376 | tf_op jit(solution)/shard_map/ppermute | solution.py:150
  24.6 2.3 %collective-permute-done = bf16[48,1536]{1,0:T(8,128)(2,1)S(1)} collective-permute-done((bf16[48,1536]{1,0:T(8,128)(2,1)S(1)}, bf16[48,1536]{1,0:T(8,128)(2,1)S(1)}, u32[]{:S(2)}, u32[]{:S(2)}) %collective-permute-start) | collective-permute-done | bytes 147488 | tf_op jit(solution)/shard_map/ppermute | solution.py:150
  26.9 1.9 %collective-permute-start.1 = (bf16[48,1536]{1,0:T(8,128)(2,1)S(1)}, bf16[48,1536]{1,0:T(8,128)(2,1)S(1)}, u32[]{:S(2)}, u32[]{:S(2)}) collective-permute-start(bf16[48,1536]{1,0:T(8,128)(2,1)S(1)} %collective-permute-done), channel_id=1, source_target_pairs={{0,32},{32,0},{1,33},{33,1},{2,34},{34,2},{3,35},{35,3},{4,36},{36... | collective-permute-start | bytes 442376 | tf_op jit(solution)/shard_map/ppermute | solution.py:151
  29.5 4.0 %collective-permute-done.1 = bf16[48,1536]{1,0:T(8,128)(2,1)S(1)} collective-permute-done((bf16[48,1536]{1,0:T(8,128)(2,1)S(1)}, bf16[48,1536]{1,0:T(8,128)(2,1)S(1)}, u32[]{:S(2)}, u32[]{:S(2)}) %collective-permute-start.1) | collective-permute-done | bytes 147488 | tf_op jit(solution)/shard_map/ppermute | solution.py:151
  33.5 4.2 %collective-permute-start.2 = (bf16[48,1536]{1,0:T(8,128)(2,1)S(1)}, bf16[48,1536]{1,0:T(8,128)(2,1)S(1)}, u32[]{:S(2)}, u32[]{:S(2)}) collective-permute-start(bf16[48,1536]{1,0:T(8,128)(2,1)S(1)} %collective-permute-done.1), channel_id=1, source_target_pairs={{32,8},{8,32},{40,16},{16,40},{48,24},{24,48},{56,0},{0,56},{33,9}... | collective-permute-start | bytes 442376 | tf_op jit(solution)/shard_map/ppermute | solution.py:152
  38.4 2.5 %collective-permute-done.2 = bf16[48,1536]{1,0:T(8,128)(2,1)S(1)} collective-permute-done((bf16[48,1536]{1,0:T(8,128)(2,1)S(1)}, bf16[48,1536]{1,0:T(8,128)(2,1)S(1)}, u32[]{:S(2)}, u32[]{:S(2)}) %collective-permute-start.2) | collective-permute-done | bytes 147488 | tf_op jit(solution)/shard_map/ppermute | solution.py:152
  41.5 3.1 %collective-permute-start.3 = (bf16[192,1536]{1,0:T(8,128)(2,1)}, bf16[192,1536]{1,0:T(8,128)(2,1)S(1)}, u32[]{:S(2)}, u32[]{:S(2)}) collective-permute-start(bf16[192,1536]{1,0:T(8,128)(2,1)} %constant_dynamic-update-slice_fusion.refs_0_), channel_id=1, source_target_pairs={{0,2},{2,4},{4,6},{6,0},{1,3},{3,5},{5,7},{7,1},{8,10},{10,12},{12... | collective-permute-start | bytes 1769480 | tf_op jit(solution)/shard_map/ppermute | solution.py:156
  44.6 3.4 %collective-permute-start.4 = (bf16[192,1536]{1,0:T(8,128)(2,1)}, bf16[192,1536]{1,0:T(8,128)(2,1)S(1)}, u32[]{:S(2)}, u32[]{:S(2)}) collective-permute-start(bf16[192,1536]{1,0:T(8,128)(2,1)} %constant_dynamic-update-slice_fusion.refs_0_), channel_id=1, source_target_pairs={{0,6},{2,0},{4,2},{6,4},{1,7},{3,1},{5,3},{7,5},{8,14},{10,8},{12,... | collective-permute-start | bytes 1769480 | tf_op jit(solution)/shard_map/ppermute | solution.py:157
  48.0 7.7 %collective-permute-done.3.refs_1_ = bf16[192,1536]{1,0:T(8,128)(2,1)S(1)} collective-permute-done((bf16[192,1536]{1,0:T(8,128)(2,1)}, bf16[192,1536]{1,0:T(8,128)(2,1)S(1)}, u32[]{:S(2)}, u32[]{:S(2)}) %collective-permute-start.3) | collective-permute-done | bytes 589856 | tf_op jit(solution)/shard_map/ppermute | solution.py:156
  55.7 1.9 %collective-permute-start.5 = (bf16[96,1536]{1,0:T(8,128)(2,1)S(1)}, bf16[96,1536]{1,0:T(8,128)(2,1)}, u32[]{:S(2)}, u32[]{:S(2)}) collective-permute-start(bf16[96,1536]{1,0:T(8,128)(2,1)S(1)} %slice.8), channel_id=1, source_target_pairs={{0,2},{2,4},{4,6},{6,0},{1,3},{3,5},{5,7},{7,1},{8,10},{10,12},{12... | collective-permute-start | bytes 884744 | tf_op jit(solution)/shard_map/ppermute | solution.py:159
  58.4 4.6 %collective-permute-start.6 = (bf16[96,1536]{1,0:T(8,128)(2,1)}, bf16[96,1536]{1,0:T(8,128)(2,1)}, u32[]{:S(2)}, u32[]{:S(2)}) collective-permute-start(bf16[96,1536]{1,0:T(8,128)(2,1)} %slice.9), channel_id=1, source_target_pairs={{0,6},{2,0},{4,2},{6,4},{1,7},{3,1},{5,3},{7,5},{8,14},{10,8},{12,... | collective-permute-start | bytes 884744 | tf_op jit(solution)/shard_map/ppermute | solution.py:159
  63.0 6.5 %attend.1 = bf16[16,144,128]{2,1,0:T(8,128)(2,1)} custom-call(s32[1]{0:T(128)S(6)} %copy.16.length_ref, bf16[16,3,128,128]{3,2,1,0:T(8,128)(2,1)S(1)} %all-to-all-done.x_ref), custom_call_target="tpu_custom_call" | custom-call | tf_op jit(solution)/shard_map/attend/pallas_call | solution.py:198
  69.6 14.1 %all-to-all-start.1 = ((bf16[16,144,128]{2,1,0:T(8,128)(2,1)}), bf16[16,144,128]{2,1,0:T(8,128)(2,1)S(1)}, u32[]{:S(2)}, u32[]{:S(2)}) async-start(bf16[16,144,128]{2,1,0:T(8,128)(2,1)} %attend.1), calls=%async_computation.1 | async-start | bytes 1179648 | tf_op jit(solution)/shard_map/all_to_all | solution.py:211
  83.7 7.3 %collective-permute-start.7 = (bf16[192,1536]{1,0:T(8,128)(2,1)}, bf16[192,1536]{1,0:T(8,128)(2,1)S(1)}, u32[]{:S(2)}, u32[]{:S(2)}) collective-permute-start(bf16[192,1536]{1,0:T(8,128)(2,1)} %constant_dynamic-update-slice_fusion.refs_0_), channel_id=1, source_target_pairs={{0,1},{1,0},{2,3},{3,2},{4,5},{5,4},{6,7},{7,6},{8,9},{9,8},{10,11... | collective-permute-start | bytes 1769480 | tf_op jit(solution)/shard_map/ppermute | solution.py:161
  90.9 1.9 %collective-permute-start.9 = (bf16[192,1536]{1,0:T(8,128)(2,1)S(1)}, bf16[192,1536]{1,0:T(8,128)(2,1)}, u32[]{:S(2)}, u32[]{:S(2)}) collective-permute-start(bf16[192,1536]{1,0:T(8,128)(2,1)S(1)} %collective-permute-done.4.refs_2_), channel_id=1, source_target_pairs={{0,1},{1,0},{2,3},{3,2},{4,5},{5,4},{6,7},{7,6},{8,9},{9,8},{10,11... | collective-permute-start | bytes 1769480 | tf_op jit(solution)/shard_map/ppermute | solution.py:161
  92.9 2.4 %collective-permute-start.8 = (bf16[192,1536]{1,0:T(8,128)(2,1)S(1)}, bf16[192,1536]{1,0:T(8,128)(2,1)}, u32[]{:S(2)}, u32[]{:S(2)}) collective-permute-start(bf16[192,1536]{1,0:T(8,128)(2,1)S(1)} %collective-permute-done.3.refs_1_), channel_id=1, source_target_pairs={{0,1},{1,0},{2,3},{3,2},{4,5},{5,4},{6,7},{7,6},{8,9},{9,8},{10,11... | collective-permute-start | bytes 1769480 | tf_op jit(solution)/shard_map/ppermute | solution.py:161
  97.3 1.9 %collective-permute-start.10 = (bf16[192,1536]{1,0:T(8,128)(2,1)S(1)}, bf16[192,1536]{1,0:T(8,128)(2,1)}, u32[]{:S(2)}, u32[]{:S(2)}) collective-permute-start(bf16[192,1536]{1,0:T(8,128)(2,1)S(1)} %constant_dynamic-update-slice_fusion.4.refs_3_), channel_id=1, source_target_pairs={{0,1},{1,0},{2,3},{3,2},{4,5},{5,4},{6,7},{7,6},{8,9},{9,8},{10,11... | collective-permute-start | bytes 1769480 | tf_op jit(solution)/shard_map/ppermute | solution.py:161
  101.3 1.1 copy-done.3
  104.5 2.0 %order.1 = (bf16[1536,768]{1,0:T(8,128)(2,1)S(1)}, bf16[1536,768]{1,0:T(8,128)(2,1)S(1)}) custom-call(s32[4]{0:T(128)S(1)} %pad_add_fusion.spot_ref, bf16[192,1536]{1,0:T(8,128)(2,1)} %constant_dynamic-update-slice_fusion.refs_0_, bf16[192,1536]{1,0:T(8,128)(2,1)S(1)} %collective-permute-done.3.refs_1_, bf16[192,1536]{1,0:T(8,128)(2,1)S(1)} %copy-done.3, ...), custom_call_target="tpu_custom_call" | custom-call | tf_op jit(solution)/shard_map/order/pallas_call | solution.py:212
  106.5 1.4 %copy-done = bf16[1536,768]{1,0:T(8,128)(2,1)} copy-done((bf16[1536,768]{1,0:T(8,128)(2,1)}, bf16[1536,768]{1,0:T(8,128)(2,1)S(1)}, u32[]{:S(2)}) %copy-start) | copy-done | bytes 2359320
  107.9 1.7 %copy-done.1 = bf16[1536,768]{1,0:T(8,128)(2,1)S(1)} copy-done((bf16[1536,768]{1,0:T(8,128)(2,1)S(1)}, bf16[1536,768]{1,0:T(8,128)(2,1)}, u32[]{:S(2)}) %copy-start.1) | copy-done | bytes 2359320
  109.6 1.5 %project.1 = (bf16[120,1536]{1,0:T(8,128)(2,1)}, bf16[8,1536]{1,0:T(8,128)(2,1)}, f32[12,1,120]{2,1,0:T(1,128)}, f32[8,12]{1,0:T(8,128)}, bf16[120,1536]{1,0:T(8,128)(2,1)}) custom-call(bf16[16,144,128]{2,1,0:T(8,128)(2,1)S(1)} %all-to-all-done.1.x_ref, bf16[1536,768]{1,0:T(8,128)(2,1)S(1)} %get-tuple-element.12.w_ref, bf16[1536,768]{1,0:T(8,128)(2,1)S(1)} %copy-done.1, ...), custom_call_target="tpu_custom_call" | custom-call | tf_op jit(solution)/shard_map/project/pallas_call | solution.py:220
  (35 shorter events, 9.7 us)
Async XLA Ops:
  1.3 12.7 %copy-start.9 = (bf16[48,1536]{1,0:T(8,128)(2,1)S(1)}, bf16[48,1536]{1,0:T(8,128)(2,1)}, u32[]{:S(2)}) copy-start(bf16[48,1536]{1,0:T(8,128)(2,1)} %param.13) | copy-start | bytes 442372
  4.4 58.6 %all-to-all-start = ((bf16[16,3,128,128]{3,2,1,0:T(8,128)(2,1)}), bf16[16,3,128,128]{3,2,1,0:T(8,128)(2,1)S(1)}, u32[]{:S(2)}, u32[]{:S(2)}) async-start(bf16[16,3,128,128]{3,2,1,0:T(8,128)(2,1)} %pack.1), calls=%async_computation | async-start | bytes 3145728 | tf_op jit(solution)/shard_map/all_to_all | solution.py:197
  14.0 12.9 %collective-permute-start = (bf16[48,1536]{1,0:T(8,128)(2,1)S(1)}, bf16[48,1536]{1,0:T(8,128)(2,1)S(1)}, u32[]{:S(2)}, u32[]{:S(2)}) collective-permute-start(bf16[48,1536]{1,0:T(8,128)(2,1)S(1)} %copy-done.9), channel_id=1, source_target_pairs={{32,8},{8,32},{40,16},{16,40},{48,24},{24,48},{56,0},{0,56},{33,9}... | collective-permute-start | bytes 442376 | tf_op jit(solution)/shard_map/ppermute | solution.py:150
  26.9 6.6 %collective-permute-start.1 = (bf16[48,1536]{1,0:T(8,128)(2,1)S(1)}, bf16[48,1536]{1,0:T(8,128)(2,1)S(1)}, u32[]{:S(2)}, u32[]{:S(2)}) collective-permute-start(bf16[48,1536]{1,0:T(8,128)(2,1)S(1)} %collective-permute-done), channel_id=1, source_target_pairs={{0,32},{32,0},{1,33},{33,1},{2,34},{34,2},{3,35},{35,3},{4,36},{36... | collective-permute-start | bytes 442376 | tf_op jit(solution)/shard_map/ppermute | solution.py:151
  33.5 7.4 %collective-permute-start.2 = (bf16[48,1536]{1,0:T(8,128)(2,1)S(1)}, bf16[48,1536]{1,0:T(8,128)(2,1)S(1)}, u32[]{:S(2)}, u32[]{:S(2)}) collective-permute-start(bf16[48,1536]{1,0:T(8,128)(2,1)S(1)} %collective-permute-done.1), channel_id=1, source_target_pairs={{32,8},{8,32},{40,16},{16,40},{48,24},{24,48},{56,0},{0,56},{33,9}... | collective-permute-start | bytes 442376 | tf_op jit(solution)/shard_map/ppermute | solution.py:152
  41.5 14.1 %collective-permute-start.3 = (bf16[192,1536]{1,0:T(8,128)(2,1)}, bf16[192,1536]{1,0:T(8,128)(2,1)S(1)}, u32[]{:S(2)}, u32[]{:S(2)}) collective-permute-start(bf16[192,1536]{1,0:T(8,128)(2,1)} %constant_dynamic-update-slice_fusion.refs_0_), channel_id=1, source_target_pairs={{0,2},{2,4},{4,6},{6,0},{1,3},{3,5},{5,7},{7,1},{8,10},{10,12},{12... | collective-permute-start | bytes 1769480 | tf_op jit(solution)/shard_map/ppermute | solution.py:156
  44.6 13.0 %collective-permute-start.4 = (bf16[192,1536]{1,0:T(8,128)(2,1)}, bf16[192,1536]{1,0:T(8,128)(2,1)S(1)}, u32[]{:S(2)}, u32[]{:S(2)}) collective-permute-start(bf16[192,1536]{1,0:T(8,128)(2,1)} %constant_dynamic-update-slice_fusion.refs_0_), channel_id=1, source_target_pairs={{0,6},{2,0},{4,2},{6,4},{1,7},{3,1},{5,3},{7,5},{8,14},{10,8},{12,... | collective-permute-start | bytes 1769480 | tf_op jit(solution)/shard_map/ppermute | solution.py:157
  55.7 39.6 %collective-permute-start.5 = (bf16[96,1536]{1,0:T(8,128)(2,1)S(1)}, bf16[96,1536]{1,0:T(8,128)(2,1)}, u32[]{:S(2)}, u32[]{:S(2)}) collective-permute-start(bf16[96,1536]{1,0:T(8,128)(2,1)S(1)} %slice.8), channel_id=1, source_target_pairs={{0,2},{2,4},{4,6},{6,0},{1,3},{3,5},{5,7},{7,1},{8,10},{10,12},{12... | collective-permute-start | bytes 884744 | tf_op jit(solution)/shard_map/ppermute | solution.py:159
  57.6 39.6 %copy-start.2 = (bf16[192,1536]{1,0:T(8,128)(2,1)}, bf16[192,1536]{1,0:T(8,128)(2,1)S(1)}, u32[]{:S(2)}) copy-start(bf16[192,1536]{1,0:T(8,128)(2,1)S(1)} %collective-permute-done.4.refs_2_) | copy-start | bytes 1769476
  58.4 37.8 %collective-permute-start.6 = (bf16[96,1536]{1,0:T(8,128)(2,1)}, bf16[96,1536]{1,0:T(8,128)(2,1)}, u32[]{:S(2)}, u32[]{:S(2)}) collective-permute-start(bf16[96,1536]{1,0:T(8,128)(2,1)} %slice.9), channel_id=1, source_target_pairs={{0,6},{2,0},{4,2},{6,4},{1,7},{3,1},{5,3},{7,5},{8,14},{10,8},{12,... | collective-permute-start | bytes 884744 | tf_op jit(solution)/shard_map/ppermute | solution.py:159
  69.6 38.4 %all-to-all-start.1 = ((bf16[16,144,128]{2,1,0:T(8,128)(2,1)}), bf16[16,144,128]{2,1,0:T(8,128)(2,1)S(1)}, u32[]{:S(2)}, u32[]{:S(2)}) async-start(bf16[16,144,128]{2,1,0:T(8,128)(2,1)} %attend.1), calls=%async_computation.1 | async-start | bytes 1179648 | tf_op jit(solution)/shard_map/all_to_all | solution.py:211
  83.7 16.5 %collective-permute-start.7 = (bf16[192,1536]{1,0:T(8,128)(2,1)}, bf16[192,1536]{1,0:T(8,128)(2,1)S(1)}, u32[]{:S(2)}, u32[]{:S(2)}) collective-permute-start(bf16[192,1536]{1,0:T(8,128)(2,1)} %constant_dynamic-update-slice_fusion.refs_0_), channel_id=1, source_target_pairs={{0,1},{1,0},{2,3},{3,2},{4,5},{5,4},{6,7},{7,6},{8,9},{9,8},{10,11... | collective-permute-start | bytes 1769480 | tf_op jit(solution)/shard_map/ppermute | solution.py:161
  90.9 10.0 %collective-permute-start.9 = (bf16[192,1536]{1,0:T(8,128)(2,1)S(1)}, bf16[192,1536]{1,0:T(8,128)(2,1)}, u32[]{:S(2)}, u32[]{:S(2)}) collective-permute-start(bf16[192,1536]{1,0:T(8,128)(2,1)S(1)} %collective-permute-done.4.refs_2_), channel_id=1, source_target_pairs={{0,1},{1,0},{2,3},{3,2},{4,5},{5,4},{6,7},{7,6},{8,9},{9,8},{10,11... | collective-permute-start | bytes 1769480 | tf_op jit(solution)/shard_map/ppermute | solution.py:161
  92.9 8.1 %collective-permute-start.8 = (bf16[192,1536]{1,0:T(8,128)(2,1)S(1)}, bf16[192,1536]{1,0:T(8,128)(2,1)}, u32[]{:S(2)}, u32[]{:S(2)}) collective-permute-start(bf16[192,1536]{1,0:T(8,128)(2,1)S(1)} %collective-permute-done.3.refs_1_), channel_id=1, source_target_pairs={{0,1},{1,0},{2,3},{3,2},{4,5},{5,4},{6,7},{7,6},{8,9},{9,8},{10,11... | collective-permute-start | bytes 1769480 | tf_op jit(solution)/shard_map/ppermute | solution.py:161
  97.3 4.0 %collective-permute-start.10 = (bf16[192,1536]{1,0:T(8,128)(2,1)S(1)}, bf16[192,1536]{1,0:T(8,128)(2,1)}, u32[]{:S(2)}, u32[]{:S(2)}) collective-permute-start(bf16[192,1536]{1,0:T(8,128)(2,1)S(1)} %constant_dynamic-update-slice_fusion.4.refs_3_), channel_id=1, source_target_pairs={{0,1},{1,0},{2,3},{3,2},{4,5},{5,4},{6,7},{7,6},{8,9},{9,8},{10,11... | collective-permute-start | bytes 1769480 | tf_op jit(solution)/shard_map/ppermute | solution.py:161
  99.2 0.8 copy-start.4
  100.0 7.9 %copy-start.8 = (f32[1,1536]{1,0:T(1,128)S(1)}, f32[1,1536]{1,0:T(1,128)}, u32[]{:S(2)}) copy-start(f32[1,1536]{1,0:T(1,128)} %gate_ref.1) | copy-start | bytes 18436
  100.1 0.8 copy-start.6
  101.3 1.1 copy-start.3
  102.4 1.1 copy-start.5
  103.4 1.1 copy-start.7
  106.5 1.4 %copy-start = (bf16[1536,768]{1,0:T(8,128)(2,1)}, bf16[1536,768]{1,0:T(8,128)(2,1)S(1)}, u32[]{:S(2)}) copy-start(bf16[1536,768]{1,0:T(8,128)(2,1)S(1)} %get-tuple-element.13.more_ref) | copy-start | bytes 7077892
  107.9 1.7 %copy-start.1 = (bf16[1536,768]{1,0:T(8,128)(2,1)S(1)}, bf16[1536,768]{1,0:T(8,128)(2,1)}, u32[]{:S(2)}) copy-start(bf16[1536,768]{1,0:T(8,128)(2,1)} %copy-done) | copy-start | bytes 7077892

commit v4 on v3

--- a/solution.py
+++ b/solution.py
@@ -102,7 +102,7 @@
 
 
 def project_kernel(
-    x_ref, w_ref, more_ref, gate_ref, av_ref, at_ref, lv_ref, lt_ref, pv_ref
+    spot_ref, x_ref, w_ref, other_ref, gate_ref, av_ref, at_ref, lv_ref, lt_ref, pv_ref
 ):
     vid = av_ref.shape[0]
     rows = vid + at_ref.shape[0]
@@ -117,48 +117,21 @@
         lses.append(lse)
     lses += [lses[0]] * (HEAD - HEADS)
     lt_ref[...] = jnp.concatenate(lses, axis=0).T[vid:, :HEADS]
-    split = w_ref.shape[1]
-    for part, here in ((w_ref, pl.ds(0, split)), (more_ref, pl.ds(split, more_ref.shape[1]))):
-        out = jnp.dot(av_ref[...], part[...], preferred_element_type=jnp.float32)
-        pv_ref[:, here] = (out * gate_ref[:, here]).astype(jnp.bfloat16)
-
-
-def order_kernel(count, spot_ref, *refs):
-    *pieces, w_ref, more_ref = refs
-    split = w_ref.shape[1]
-    zl, zh, x, core = spot_ref[0], spot_ref[1], spot_ref[2], spot_ref[3]
-    nz, nx = SIZES["zh"], SIZES["x"]
-    near = 2 * zl - 1 + nz
-    of_z = (zh, zh + near, zh + nz - near, zh + nz // 2)
-    of_x = (x, x + nx - 1, x + 1, x + nx // 2)
-    for i, piece in enumerate(pieces):
-        which = i % len(of_x)
-        for j in range(len(of_z)):
-            row = (of_z[j] + nz) % nz * nx + (of_x[which]) % nx
-            row = (row * SIZES["core"] + (core ^ (i // len(of_x)))) * count
-            target = pl.ds(pl.multiple_of(row, 16), count)
-            w_ref[target, :] = piece[pl.ds(j * count, count), :split]
-            more_ref[target, :] = piece[pl.ds(j * count, count), split:]
-
-
-def gathered(w_out):
-    nz, nx = SIZES["zh"], SIZES["x"]
-    between = []
-    for zh in range(nz):
-        here, there = nz + zh, (zh + 1) % nz
-        between += [(here, there), (there, here)]
-    first = lax.ppermute(w_out, ("zl", "zh"), between)
-    second = lax.ppermute(first, "zl", [(0, 1), (1, 0)])
-    third = lax.ppermute(second, ("zl", "zh"), between)
-    column = jnp.concatenate([w_out, first, second, third], axis=0)
-    up = [(i, (i + 1) % nx) for i in range(nx)]
-    down = [(i, (i - 1) % nx) for i in range(nx)]
-    left = lax.ppermute(column, "x", up)
-    right = lax.ppermute(column, "x", down)
-    half = column.shape[0] // 2
-    far = [lax.ppermute(left[:half], "x", up), lax.ppermute(right[half:], "x", down)]
-    mine = [column, left, right, jnp.concatenate(far, axis=0)]
-    return mine + [lax.ppermute(part, "core", [(0, 1), (1, 0)]) for part in mine]
+    blocks = SIZES["zh"] * SIZES["x"]
+    mixed = av_ref[...].astype(jnp.float32)
+    width = mixed.shape[1] // (blocks * SIZES["core"])
+    even, odd = [
+        jnp.concatenate(
+            [mixed[:, (2 * i + c) * width : (2 * i + c + 1) * width] for i in range(blocks)], axis=1
+        )
+        for c in range(SIZES["core"])
+    ]
+    first = spot_ref[0] == 0
+    mine = jnp.where(first, even, odd).astype(jnp.bfloat16)
+    others = jnp.where(first, odd, even).astype(jnp.bfloat16)
+    out = jnp.dot(mine, w_ref[...], preferred_element_type=jnp.float32)
+    out += jnp.dot(others, other_ref[...], preferred_element_type=jnp.float32)
+    pv_ref[...] = (out * gate_ref[...]).astype(jnp.bfloat16)
 
 
 def shards(sources, q_video, kv_video, q_text, kv_text, text_lengths, gate, w_out):
@@ -166,8 +139,8 @@
     txt = q_text.shape[1]
     rows = vid + txt
     base = (lax.axis_index(SEQ) * txt).astype(jnp.int32).reshape(1)
-    pieces = gathered(w_out)
-    spot = jnp.stack([lax.axis_index(axis) for axis in ("zl", "zh", "x", "core")])
+    core = lax.axis_index("core")
+    mine = lax.all_gather(w_out, ("zh", "x"), axis=0, tiled=True)
     smem = pl.BlockSpec(memory_space=pltpu.SMEM)
     vmem = pl.BlockSpec(memory_space=VMEM)
     anywhere = pl.BlockSpec(memory_space=pl.ANY)
@@ -208,15 +181,9 @@
         compiler_params=pltpu.CompilerParams(vmem_limit_bytes=40 << 20),
         name="attend",
     )(text_lengths, moved)
+    after = lax.optimization_barrier((mine, mixed))[0]
+    others = lax.ppermute(after, "core", [(0, 1), (1, 0)])
     back = lax.all_to_all(mixed, SEQ, 0, 0, tiled=True)
-    halves = pl.pallas_call(
-        functools.partial(order_kernel, w_out.shape[0]),
-        out_shape=(jax.ShapeDtypeStruct((feats, feats // 2), jnp.bfloat16),) * 2,
-        in_specs=[smem, *[vmem] * len(pieces)],
-        out_specs=(vmem,) * 2,
-        compiler_params=pltpu.CompilerParams(vmem_limit_bytes=32 << 20),
-        name="order",
-    )(spot.astype(jnp.int32), *pieces)
     attn_video, attn_text, lse_video, lse_text, proj_video = pl.pallas_call(
         project_kernel,
         out_shape=(
@@ -226,11 +193,11 @@
             jax.ShapeDtypeStruct((txt, HEADS), jnp.float32),
             jax.ShapeDtypeStruct((vid, feats), jnp.bfloat16),
         ),
-        in_specs=[vmem] * 4,
+        in_specs=[smem, *[vmem] * 4],
         out_specs=(vmem,) * 5,
         compiler_params=pltpu.CompilerParams(vmem_limit_bytes=32 << 20),
         name="project",
-    )(back, *halves, gate)
+    )(core.astype(jnp.int32).reshape(1), back, mine, others, gate)
     return (
         attn_video[None],
         attn_text[None],

time: 112 us -> 128 us (1.14)
  starting transfers between devices: 66.2 us -> 10.6 us
  blocking collectives: 0 us -> 47.6 us
  waiting for transfers between devices: 16.8 us -> 40.1 us
  between operations: 1.51 us -> 14.7 us
  local copies, waits for them, and re-layouts: 13.3 us -> 1.67 us
  Pallas kernels: 13.2 us -> 11.2 us
    all_to_all x0 -> x1, blocking collectives: none -> 47.6 us  [shards(): moved = lax.all_to_all(packed, SEQ, 0, 0, tiled=True)]
    ppermute x11 -> x1, starting transfers between devices: 42.5 us -> 3.34 us  [shards(): others = lax.ppermute(after, 'core', [(0, 1), (1, 0)])]
    all_gather x0 -> x1, waiting for transfers between devices: none -> 21.9 us  [shards(): mine = lax.all_gather(w_out, ('zh', 'x'), axis=0, tiled=True)]
    all_to_all x1, waiting for transfers between devices: 0.01 us -> 17.5 us  [shards(): back = lax.all_to_all(mixed, SEQ, 0, 0, tiled=True)]
    ppermute x11 -> x1, waiting for transfers between devices: 16.8 us -> 0.01 us  [shards(): others = lax.ppermute(after, 'core', [(0, 1), (1, 0)])]
    all_to_all x1 -> x0, starting transfers between devices: 9.58 us -> none  [shards(): moved = lax.all_to_all(packed, SEQ, 0, 0, tiled=True)]
    unnamed x24 -> x4, local copies, waits for them, and re-layouts: 10.9 us -> 1.67 us
    all_to_all x1, starting transfers between devices: 14.1 us -> 7.27 us  [shards(): back = lax.all_to_all(mixed, SEQ, 0, 0, tiled=True)]
  transfers between devices with their start and end apart: 13 -> 3, of which waited for: 5 -> 2; matrix products, arithmetic and copies ran while one was open for 5% -> 0% of each run, Pallas kernels for 8% -> 8%
where the time goes in v4:
time: 128 us; the launch traced here: 126 us
  blocking collectives  47.6 us (37%)
  waiting for transfers between devices  40.1 us (31%)
  between operations  14.7 us (11%)
  Pallas kernels  11.2 us (9%)
  starting transfers between devices  10.6 us (8%)
  local copies, waits for them, and re-layouts  1.67 us (1%)
    all_to_all x1, blocking collectives, shards(): moved = lax.all_to_all(packed, SEQ, 0, 0, tiled=True)  47.6 us
    all_gather x1, waiting for transfers between devices, shards(): mine = lax.all_gather(w_out, ('zh', 'x'), axis=0, tiled=True)  21.9 us
    all_to_all x1, waiting for transfers between devices, shards(): back = lax.all_to_all(mixed, SEQ, 0, 0, tiled=True)  17.5 us
    all_to_all x1, starting transfers between devices, shards(): back = lax.all_to_all(mixed, SEQ, 0, 0, tiled=True)  7.27 us
    pallas_call x1, Pallas kernels, shards(): pl.pallas_call(functools.partial(attend_kernel, vid), out_shape=jax.Shape...  6.55 us
    ppermute x1, starting transfers between devices, shards(): others = lax.ppermute(after, 'core', [(0, 1), (1, 0)])  3.34 us
    pallas_call x1, Pallas kernels, shards(): pl.pallas_call(pack_kernel, out_shape=jax.ShapeDtypeStruct((sources, 3, r...  3.03 us
  transfers between devices with their start and end apart: 3, of which 2 were waited for; matrix products, arithmetic and copies ran while one was open for 0% of the time, Pallas kernels for 8%

profile of v4, /device:TPU:1, one launch (start us, length us, event | category | flops | bytes accessed | tf_op | source)
XLA Modules:
  0.0 126.0 jit_solution(9362670609496299582)
XLA Ops:
  7.2 0.0 all-gather.2.cloned.1.call-start
  7.2 0.7 all-gather.2.cloned.1.call-update
  8.6 3.0 %pack.1 = bf16[16,3,128,128]{3,2,1,0:T(8,128)(2,1)} custom-call(s32[1]{0:T(128)S(6)} %copy.12.length_ref, s32[1]{0:T(128)} %bitcast.1.base_ref, bf16[120,1536]{1,0:T(8,128)(2,1)} %bitcast.14, bf16[120,2,1536]{2,1,0:T(2,128)(2,1)} %bitcast.13, bf16[8,1536]{1,0:T(8,128)(2,1)} %bitcast.16, bf16[8,2,1536]{2,1,0:T(2,128)(2,1)} %bitcast.15), custom_call_target="tpu_custom_call" | custom-call | tf_op jit(solution)/shard_map/pack/pallas_call | solution.py:147
  11.6 47.6 %all_to_all.10.x_ref = bf16[16,3,128,128]{3,2,1,0:T(8,128)(2,1)S(1)} all-to-all(bf16[16,3,128,128]{3,2,1,0:T(8,128)(2,1)} %pack.1), channel_id=1, replica_groups=mesh['y'=8,'zl'=2,'zh'=4,'x'=4,'core'=2] {'y','zl'}, dimensions={0} | all-to-all | bytes 3145728 | tf_op jit(solution)/shard_map/all_to_all | solution.py:170
  59.2 0.0 copy-start.1
  59.2 6.5 %attend.1 = bf16[16,144,128]{2,1,0:T(8,128)(2,1)} custom-call(s32[1]{0:T(128)S(6)} %copy.12.length_ref, bf16[16,3,128,128]{3,2,1,0:T(8,128)(2,1)S(1)} %all_to_all.10.x_ref), custom_call_target="tpu_custom_call" | custom-call | tf_op jit(solution)/shard_map/attend/pallas_call | solution.py:171
  65.8 21.9 %all-gather.2.cloned.1.call-done.w_ref = bf16[768,1536]{1,0:T(8,128)(2,1)} async-done(((bf16[48,1536]{1,0:T(8,128)(2,1)}), bf16[768,1536]{1,0:T(8,128)(2,1)}) %all-gather.2.cloned.1.call-update) | async-done | bytes 2359312 | tf_op jit(solution)/shard_map/all_gather | solution.py:143
  87.7 3.3 %collective-permute-start = (bf16[768,1536]{1,0:T(8,128)(2,1)}, bf16[768,1536]{1,0:T(8,128)(2,1)S(1)}, u32[]{:S(2)}, u32[]{:S(2)}) collective-permute-start(bf16[768,1536]{1,0:T(8,128)(2,1)} %all-gather.2.cloned.1.call-done.w_ref), channel_id=1, source_target_pairs={{0,1},{1,0},{2,3},{3,2},{4,5},{5,4},{6,7},{7,6},{8,9},{9,8},{10,11... | collective-permute-start | bytes 7077896 | tf_op jit(solution)/shard_map/ppermute | solution.py:185
  91.0 7.3 %all-to-all-start.1 = ((bf16[16,144,128]{2,1,0:T(8,128)(2,1)}), bf16[16,144,128]{2,1,0:T(8,128)(2,1)S(1)}, u32[]{:S(2)}, u32[]{:S(2)}) async-start(bf16[16,144,128]{2,1,0:T(8,128)(2,1)} %attend.1), calls=%async_computation.1 | async-start | bytes 1179648 | tf_op jit(solution)/shard_map/all_to_all | solution.py:186
  98.3 17.5 %all-to-all-done.1.x_ref = bf16[16,144,128]{2,1,0:T(8,128)(2,1)S(1)} async-done(((bf16[16,144,128]{2,1,0:T(8,128)(2,1)}), bf16[16,144,128]{2,1,0:T(8,128)(2,1)S(1)}, u32[]{:S(2)}, u32[]{:S(2)}) %all-to-all-start.1) | async-done | bytes 589856 | tf_op jit(solution)/shard_map/all_to_all | solution.py:186
  115.8 0.0 collective-permute-done.other_ref
  115.8 0.0 copy-done.1
  115.8 0.0 copy-start
  115.8 1.7 %copy-done = bf16[768,1536]{1,0:T(8,128)(2,1)S(1)} copy-done((bf16[768,1536]{1,0:T(8,128)(2,1)S(1)}, bf16[768,1536]{1,0:T(8,128)(2,1)}, u32[]{:S(2)}) %copy-start) | copy-done | bytes 2359320
  117.5 1.7 %project.1 = (bf16[120,1536]{1,0:T(8,128)(2,1)}, bf16[8,1536]{1,0:T(8,128)(2,1)}, f32[12,1,120]{2,1,0:T(1,128)}, f32[8,12]{1,0:T(8,128)}, bf16[120,1536]{1,0:T(8,128)(2,1)}) custom-call(s32[1]{0:T(128)} %bitcast.spot_ref, bf16[16,144,128]{2,1,0:T(8,128)(2,1)S(1)} %all-to-all-done.1.x_ref, bf16[768,1536]{1,0:T(8,128)(2,1)S(1)} %copy-done, ...), custom_call_target="tpu_custom_call" | custom-call | tf_op jit(solution)/shard_map/project/pallas_call | solution.py:187
Async XLA Ops:
  7.2 80.5 %all-gather.2.cloned.1.call-start = ((), (), s32[]{:S(2)}) async-start(), calls=%async_computation.2 | async-start | bytes 2506752 | tf_op jit(solution)/shard_map/all_gather | solution.py:143
  59.2 56.6 %copy-start.1 = (f32[1,1536]{1,0:T(1,128)S(1)}, f32[1,1536]{1,0:T(1,128)}, u32[]{:S(2)}) copy-start(f32[1,1536]{1,0:T(1,128)} %gate_ref.1) | copy-start | bytes 18436
  87.7 28.2 %collective-permute-start = (bf16[768,1536]{1,0:T(8,128)(2,1)}, bf16[768,1536]{1,0:T(8,128)(2,1)S(1)}, u32[]{:S(2)}, u32[]{:S(2)}) collective-permute-start(bf16[768,1536]{1,0:T(8,128)(2,1)} %all-gather.2.cloned.1.call-done.w_ref), channel_id=1, source_target_pairs={{0,1},{1,0},{2,3},{3,2},{4,5},{5,4},{6,7},{7,6},{8,9},{9,8},{10,11... | collective-permute-start | bytes 7077896 | tf_op jit(solution)/shard_map/ppermute | solution.py:185
  91.0 24.8 %all-to-all-start.1 = ((bf16[16,144,128]{2,1,0:T(8,128)(2,1)}), bf16[16,144,128]{2,1,0:T(8,128)(2,1)S(1)}, u32[]{:S(2)}, u32[]{:S(2)}) async-start(bf16[16,144,128]{2,1,0:T(8,128)(2,1)} %attend.1), calls=%async_computation.1 | async-start | bytes 1179648 | tf_op jit(solution)/shard_map/all_to_all | solution.py:186
  115.8 1.7 %copy-start = (bf16[768,1536]{1,0:T(8,128)(2,1)S(1)}, bf16[768,1536]{1,0:T(8,128)(2,1)}, u32[]{:S(2)}) copy-start(bf16[768,1536]{1,0:T(8,128)(2,1)} %all-gather.2.cloned.1.call-done.w_ref) | copy-start | bytes 7077892
Sparse Core Ops, SparseCore 0:
  11.0 76.6 all-gather.1

commit v5 on v4

--- a/solution.py
+++ b/solution.py
@@ -102,7 +102,7 @@
 
 
 def project_kernel(
-    spot_ref, x_ref, w_ref, other_ref, gate_ref, av_ref, at_ref, lv_ref, lt_ref, pv_ref
+    spot_ref, x_ref, w_ref, gate_ref, av_ref, at_ref, lv_ref, lt_ref, half_ref, mixed_ref
 ):
     vid = av_ref.shape[0]
     rows = vid + at_ref.shape[0]
@@ -117,21 +117,26 @@
         lses.append(lse)
     lses += [lses[0]] * (HEAD - HEADS)
     lt_ref[...] = jnp.concatenate(lses, axis=0).T[vid:, :HEADS]
-    blocks = SIZES["zh"] * SIZES["x"]
+    nz, nx = SIZES["zh"], SIZES["x"]
     mixed = av_ref[...].astype(jnp.float32)
-    width = mixed.shape[1] // (blocks * SIZES["core"])
-    even, odd = [
-        jnp.concatenate(
-            [mixed[:, (2 * i + c) * width : (2 * i + c + 1) * width] for i in range(blocks)], axis=1
-        )
-        for c in range(SIZES["core"])
-    ]
-    first = spot_ref[0] == 0
-    mine = jnp.where(first, even, odd).astype(jnp.bfloat16)
-    others = jnp.where(first, odd, even).astype(jnp.bfloat16)
-    out = jnp.dot(mine, w_ref[...], preferred_element_type=jnp.float32)
-    out += jnp.dot(others, other_ref[...], preferred_element_type=jnp.float32)
-    pv_ref[...] = (out * gate_ref[...]).astype(jnp.bfloat16)
+    width = mixed.shape[1] // (nz * nx)
+    mixed = jnp.concatenate(
+        [mixed[:, (z * nx + x) * width :][:, :width] for x in range(nx) for z in range(nz)], axis=1
+    ).astype(jnp.bfloat16)
+    mixed_ref[...] = mixed
+    half = w_ref.shape[1]
+    here = pl.ds(pl.multiple_of(spot_ref[0] * half, half), half)
+    out = jnp.dot(mixed, w_ref[...], preferred_element_type=jnp.float32)
+    half_ref[...] = (out * gate_ref[:, here]).astype(jnp.bfloat16)
+
+
+def finish_kernel(spot_ref, mixed_ref, w_ref, gate_ref, half_ref, pv_ref):
+    half = w_ref.shape[1]
+    near = pl.ds(pl.multiple_of(spot_ref[0] * half, half), half)
+    here = pl.ds(pl.multiple_of((1 - spot_ref[0]) * half, half), half)
+    pv_ref[:, near] = half_ref[...]
+    out = jnp.dot(mixed_ref[...], w_ref[...], preferred_element_type=jnp.float32)
+    pv_ref[:, here] = (out * gate_ref[:, here]).astype(jnp.bfloat16)
 
 
 def shards(sources, q_video, kv_video, q_text, kv_text, text_lengths, gate, w_out):
@@ -140,7 +145,8 @@
     rows = vid + txt
     base = (lax.axis_index(SEQ) * txt).astype(jnp.int32).reshape(1)
     core = lax.axis_index("core")
-    mine = lax.all_gather(w_out, ("zh", "x"), axis=0, tiled=True)
+    spot = core.astype(jnp.int32).reshape(1)
+    along_z = lax.all_gather(w_out, ("zh", "core"), axis=0, tiled=True)
     smem = pl.BlockSpec(memory_space=pltpu.SMEM)
     vmem = pl.BlockSpec(memory_space=VMEM)
     anywhere = pl.BlockSpec(memory_space=pl.ANY)
@@ -168,6 +174,10 @@
         kv_text[0],
     )
     moved = lax.all_to_all(packed, SEQ, 0, 0, tiled=True)
+    half = feats // SIZES["core"]
+    along_z = lax.optimization_barrier((along_z, moved))[0]
+    mine = lax.dynamic_slice_in_dim(along_z, core * half, half, axis=1)
+    mine = lax.all_gather(mine, "x", axis=0, tiled=True)
     mixed = pl.pallas_call(
         functools.partial(attend_kernel, vid),
         out_shape=jax.ShapeDtypeStruct((sources, rows + LSE_ROWS, HEAD), jnp.bfloat16),
@@ -181,23 +191,32 @@
         compiler_params=pltpu.CompilerParams(vmem_limit_bytes=40 << 20),
         name="attend",
     )(text_lengths, moved)
-    after = lax.optimization_barrier((mine, mixed))[0]
-    others = lax.ppermute(after, "core", [(0, 1), (1, 0)])
     back = lax.all_to_all(mixed, SEQ, 0, 0, tiled=True)
-    attn_video, attn_text, lse_video, lse_text, proj_video = pl.pallas_call(
+    mine, back = lax.optimization_barrier((mine, back))
+    others = lax.ppermute(mine, "core", [(0, 1), (1, 0)])
+    attn_video, attn_text, lse_video, lse_text, part, ordered = pl.pallas_call(
         project_kernel,
         out_shape=(
             jax.ShapeDtypeStruct((vid, feats), jnp.bfloat16),
             jax.ShapeDtypeStruct((txt, feats), jnp.bfloat16),
             jax.ShapeDtypeStruct((HEADS, 1, vid), jnp.float32),
             jax.ShapeDtypeStruct((txt, HEADS), jnp.float32),
+            jax.ShapeDtypeStruct((vid, half), jnp.bfloat16),
             jax.ShapeDtypeStruct((vid, feats), jnp.bfloat16),
         ),
-        in_specs=[smem, *[vmem] * 4],
-        out_specs=(vmem,) * 5,
+        in_specs=[smem, *[vmem] * 3],
+        out_specs=(vmem,) * 6,
         compiler_params=pltpu.CompilerParams(vmem_limit_bytes=32 << 20),
         name="project",
-    )(core.astype(jnp.int32).reshape(1), back, mine, others, gate)
+    )(spot, back, mine, gate)
+    proj_video = pl.pallas_call(
+        finish_kernel,
+        out_shape=jax.ShapeDtypeStruct((vid, feats), jnp.bfloat16),
+        in_specs=[smem, *[vmem] * 4],
+        out_specs=vmem,
+        compiler_params=pltpu.CompilerParams(vmem_limit_bytes=32 << 20),
+        name="finish",
+    )(spot, ordered, others, gate, part)
     return (
         attn_video[None],
         attn_text[None],

time: 128 us -> 129 us (level)
  blocking collectives: 47.6 us -> 23.4 us
  waiting for transfers between devices: 40.1 us -> 63.2 us
  local copies, waits for them, and re-layouts: 1.67 us -> 3.58 us
  starting transfers between devices: 10.6 us -> 12.2 us
    all_gather x1 -> x2, waiting for transfers between devices: 21.9 us -> 60.9 us  [the longest x1 55.8 us: shards(): along_z = lax.all_gather(w_out, ('zh', 'core'), axis=0, tiled=True)]
    all_to_all x1, blocking collectives: 47.6 us -> 23.4 us  [shards(): back = lax.all_to_all(mixed, SEQ, 0, 0, tiled=True)]
    all_to_all x1, waiting for transfers between devices: 17.5 us -> 0.01 us  [shards(): moved = lax.all_to_all(packed, SEQ, 0, 0, tiled=True)]
    all_to_all x1, starting transfers between devices: 7.27 us -> 9.58 us  [shards(): moved = lax.all_to_all(packed, SEQ, 0, 0, tiled=True)]
    dynamic_slice x0 -> x1, local copies, waits for them, and re-layouts: none -> 1.92 us  [shards(): mine = lax.dynamic_slice_in_dim(along_z, core * half, half, axis=1)]
    ppermute x1, waiting for transfers between devices: 0.01 us -> 1.55 us  [shards(): others = lax.ppermute(mine, 'core', [(0, 1), (1, 0)])]
  transfers between devices with their start and end apart: 3 -> 4, of which waited for: 2 -> 3; matrix products, arithmetic and copies ran while one was open for 0% -> 0% of each run, Pallas kernels for 8% -> 5%
where the time goes in v5:
time: 129 us; the launch traced here: 128 us
  waiting for transfers between devices  63.2 us (49%)
  blocking collectives  23.4 us (18%)
  between operations  14.7 us (11%)
  starting transfers between devices  12.2 us (9%)
  Pallas kernels  11.1 us (9%)
  local copies, waits for them, and re-layouts  3.58 us (3%)
    all_gather x1, waiting for transfers between devices, shards(): along_z = lax.all_gather(w_out, ('zh', 'core'), axis=0, tiled=True)  55.8 us
    all_to_all x1, blocking collectives, shards(): back = lax.all_to_all(mixed, SEQ, 0, 0, tiled=True)  23.4 us
    all_to_all x1, starting transfers between devices, shards(): moved = lax.all_to_all(packed, SEQ, 0, 0, tiled=True)  9.58 us
    pallas_call x1, Pallas kernels, shards(): pl.pallas_call(functools.partial(attend_kernel, vid), out_shape=jax.Shape...  5.71 us
    all_gather x1, waiting for transfers between devices, shards(): mine = lax.all_gather(mine, 'x', axis=0, tiled=True)  5.12 us
    pallas_call x1, Pallas kernels, shards(): pl.pallas_call(pack_kernel, out_shape=jax.ShapeDtypeStruct((sources, 3, r...  3.04 us
  transfers between devices with their start and end apart: 4, of which 3 were waited for; matrix products, arithmetic and copies ran while one was open for 0% of the time, Pallas kernels for 5%

profile of v5, /device:TPU:1, one launch (start us, length us, event | category | flops | bytes accessed | tf_op | source)
XLA Modules:
  0.0 128.3 jit_solution(638761124383137090)
XLA Ops:
  7.8 3.0 %pack.1 = bf16[16,3,128,128]{3,2,1,0:T(8,128)(2,1)} custom-call(s32[1]{0:T(128)S(6)} %copy.12.length_ref, s32[1]{0:T(128)} %bitcast.1.base_ref, bf16[120,1536]{1,0:T(8,128)(2,1)} %bitcast.14, bf16[120,2,1536]{2,1,0:T(2,128)(2,1)} %bitcast.13, bf16[8,1536]{1,0:T(8,128)(2,1)} %bitcast.17, bf16[8,2,1536]{2,1,0:T(2,128)(2,1)} %bitcast.16), custom_call_target="tpu_custom_call" | custom-call | tf_op jit(solution)/shard_map/pack/pallas_call | solution.py:153
  10.9 9.6 %all-to-all-start = ((bf16[16,3,128,128]{3,2,1,0:T(8,128)(2,1)}), bf16[16,3,128,128]{3,2,1,0:T(8,128)(2,1)S(1)}, u32[]{:S(2)}, u32[]{:S(2)}) async-start(bf16[16,3,128,128]{3,2,1,0:T(8,128)(2,1)} %pack.1), calls=%async_computation | async-start | bytes 3145728 | tf_op jit(solution)/shard_map/all_to_all | solution.py:176
  20.4 0.0 all-gather.3.cloned.1.call-start
  20.5 0.7 all-gather.3.cloned.1.call-update
  21.2 0.0 all-gather.5.cloned.1.call-start
  21.2 55.8 %all-gather.3.cloned.1.call-done = bf16[384,1536]{1,0:T(8,128)(2,1)} async-done(((bf16[48,1536]{1,0:T(8,128)(2,1)}), bf16[384,1536]{1,0:T(8,128)(2,1)}) %all-gather.3.cloned.1.call-update) | async-done | bytes 1179664 | tf_op jit(solution)/shard_map/all_gather | solution.py:149
  77.1 0.0 all-to-all-done.x_ref
  77.1 1.9 %constant_dynamic-slice_fusion = bf16[384,768]{1,0:T(8,128)(2,1)} fusion(bf16[384,1536]{1,0:T(8,128)(2,1)} %all-gather.3.cloned.1.call-done, s32[]{:T(128)S(6)} %select_n.3), kind=kLoop, calls=%fused_computation | loop fusion | bytes 1179652 | tf_op jit(solution)/shard_map/dynamic_slice | solution.py:179
  79.0 0.0 all-gather.5.cloned.1.call-update
  79.0 0.0 copy-start.1
  79.0 5.7 %attend.1 = bf16[16,144,128]{2,1,0:T(8,128)(2,1)S(1)} custom-call(s32[1]{0:T(128)S(6)} %copy.12.length_ref, bf16[16,3,128,128]{3,2,1,0:T(8,128)(2,1)S(1)} %all-to-all-done.x_ref), custom_call_target="tpu_custom_call" | custom-call | tf_op jit(solution)/shard_map/attend/pallas_call | solution.py:181
  84.7 23.4 %all_to_all.10.x_ref = bf16[16,144,128]{2,1,0:T(8,128)(2,1)S(1)} all-to-all(bf16[16,144,128]{2,1,0:T(8,128)(2,1)S(1)} %attend.1), channel_id=1, replica_groups=mesh['y'=8,'zl'=2,'zh'=4,'x'=4,'core'=2] {'y','zl'}, dimensions={0} | all-to-all | bytes 1179648 | tf_op jit(solution)/shard_map/all_to_all | solution.py:194
  108.2 5.1 %all-gather.5.cloned.1.call-done.w_ref = bf16[1536,768]{1,0:T(8,128)(2,1)} async-done(((bf16[384,768]{1,0:T(8,128)(2,1)}), bf16[1536,768]{1,0:T(8,128)(2,1)}) %all-gather.5.cloned.1.call-update) | async-done | bytes 2359312 | tf_op jit(solution)/shard_map/all_gather | solution.py:180
  113.3 2.6 %collective-permute-start = (bf16[1536,768]{1,0:T(8,128)(2,1)}, bf16[1536,768]{1,0:T(8,128)(2,1)S(1)}, u32[]{:S(2)}, u32[]{:S(2)}) collective-permute-start(bf16[1536,768]{1,0:T(8,128)(2,1)} %all-gather.5.cloned.1.call-done.w_ref), channel_id=1, source_target_pairs={{0,1},{1,0},{2,3},{3,2},{4,5},{5,4},{6,7},{7,6},{8,9},{9,8},{10,11... | collective-permute-start | bytes 7077896 | tf_op jit(solution)/shard_map/ppermute | solution.py:196
  115.9 0.0 copy-done.1
  115.9 0.0 copy-start
  115.9 1.7 %copy-done = bf16[1536,768]{1,0:T(8,128)(2,1)S(1)} copy-done((bf16[1536,768]{1,0:T(8,128)(2,1)S(1)}, bf16[1536,768]{1,0:T(8,128)(2,1)}, u32[]{:S(2)}) %copy-start) | copy-done | bytes 2359320
  117.5 1.1 project.1
  118.7 1.6 %collective-permute-done.w_ref = bf16[1536,768]{1,0:T(8,128)(2,1)S(1)} collective-permute-done((bf16[1536,768]{1,0:T(8,128)(2,1)}, bf16[1536,768]{1,0:T(8,128)(2,1)S(1)}, u32[]{:S(2)}, u32[]{:S(2)}) %collective-permute-start) | collective-permute-done | bytes 2359328 | tf_op jit(solution)/shard_map/ppermute | solution.py:196
  120.2 1.2 finish.1
Async XLA Ops:
  10.9 66.2 %all-to-all-start = ((bf16[16,3,128,128]{3,2,1,0:T(8,128)(2,1)}), bf16[16,3,128,128]{3,2,1,0:T(8,128)(2,1)S(1)}, u32[]{:S(2)}, u32[]{:S(2)}) async-start(bf16[16,3,128,128]{3,2,1,0:T(8,128)(2,1)} %pack.1), calls=%async_computation | async-start | bytes 3145728 | tf_op jit(solution)/shard_map/all_to_all | solution.py:176
  20.4 56.6 %all-gather.3.cloned.1.call-start = ((), (), s32[]{:S(2)}) async-start(), calls=%async_computation.2 | async-start | bytes 1327104 | tf_op jit(solution)/shard_map/all_gather | solution.py:149
  21.2 92.1 %all-gather.5.cloned.1.call-start = ((), (), s32[]{:S(2)}) async-start(), calls=%async_computation.3 | async-start | bytes 2949120 | tf_op jit(solution)/shard_map/all_gather | solution.py:180
  79.0 36.9 %copy-start.1 = (f32[1,1536]{1,0:T(1,128)S(1)}, f32[1,1536]{1,0:T(1,128)}, u32[]{:S(2)}) copy-start(f32[1,1536]{1,0:T(1,128)} %gate_ref.3) | copy-start | bytes 18436
  113.3 6.9 %collective-permute-start = (bf16[1536,768]{1,0:T(8,128)(2,1)}, bf16[1536,768]{1,0:T(8,128)(2,1)S(1)}, u32[]{:S(2)}, u32[]{:S(2)}) collective-permute-start(bf16[1536,768]{1,0:T(8,128)(2,1)} %all-gather.5.cloned.1.call-done.w_ref), channel_id=1, source_target_pairs={{0,1},{1,0},{2,3},{3,2},{4,5},{5,4},{6,7},{7,6},{8,9},{9,8},{10,11... | collective-permute-start | bytes 7077896 | tf_op jit(solution)/shard_map/ppermute | solution.py:196
  115.9 1.7 %copy-start = (bf16[1536,768]{1,0:T(8,128)(2,1)S(1)}, bf16[1536,768]{1,0:T(8,128)(2,1)}, u32[]{:S(2)}) copy-start(bf16[1536,768]{1,0:T(8,128)(2,1)} %all-gather.5.cloned.1.call-done.w_ref) | copy-start | bytes 7077892
Sparse Core Ops, SparseCore 0:
  23.4 53.6 all-gather.2
  79.2 34.0 all-gather.4

commit v6 on v3

--- a/solution.py
+++ b/solution.py
@@ -141,16 +141,18 @@
             more_ref[target, :] = piece[pl.ds(j * count, count), split:]
 
 
-def gathered(w_out):
-    nz, nx = SIZES["zh"], SIZES["x"]
+def across(block):
+    nz = SIZES["zh"]
     between = []
     for zh in range(nz):
         here, there = nz + zh, (zh + 1) % nz
         between += [(here, there), (there, here)]
-    first = lax.ppermute(w_out, ("zl", "zh"), between)
-    second = lax.ppermute(first, "zl", [(0, 1), (1, 0)])
-    third = lax.ppermute(second, ("zl", "zh"), between)
-    column = jnp.concatenate([w_out, first, second, third], axis=0)
+    return lax.ppermute(block, ("zl", "zh"), between)
+
+
+def gathered(w_out, first, second):
+    nx = SIZES["x"]
+    column = jnp.concatenate([w_out, first, second, across(second)], axis=0)
     up = [(i, (i + 1) % nx) for i in range(nx)]
     down = [(i, (i - 1) % nx) for i in range(nx)]
     left = lax.ppermute(column, "x", up)
@@ -166,7 +168,9 @@
     txt = q_text.shape[1]
     rows = vid + txt
     base = (lax.axis_index(SEQ) * txt).astype(jnp.int32).reshape(1)
-    pieces = gathered(w_out)
+    first = across(w_out)
+    second = lax.ppermute(first, "zl", [(0, 1), (1, 0)])
+    pieces = gathered(w_out, first, second)
     spot = jnp.stack([lax.axis_index(axis) for axis in ("zl", "zh", "x", "core")])
     smem = pl.BlockSpec(memory_space=pltpu.SMEM)
     vmem = pl.BlockSpec(memory_space=VMEM)
@@ -194,6 +198,7 @@
         q_text[0],
         kv_text[0],
     )
+    packed = lax.optimization_barrier((packed, second))[0]
     moved = lax.all_to_all(packed, SEQ, 0, 0, tiled=True)
     mixed = pl.pallas_call(
         functools.partial(attend_kernel, vid),

time: 112 us -> 103 us (0.920)
  starting transfers between devices: 66.2 us -> 55.1 us
  waiting for transfers between devices: 16.8 us -> 19 us
    all_to_all x1, starting transfers between devices: 14.1 us -> 7.24 us  [shards(): back = lax.all_to_all(mixed, SEQ, 0, 0, tiled=True)]
    all_to_all x1, waiting for transfers between devices: 0.01 us -> 4.38 us  [shards(): moved = lax.all_to_all(packed, SEQ, 0, 0, tiled=True)]
    ppermute x4, starting transfers between devices: 13.5 us -> 9.17 us  [gathered(): lax.ppermute(part, 'core', [(0, 1), (1, 0)])]
    ppermute x3, waiting for transfers between devices: 8.77 us -> 6.23 us  [the longest x2 6.06 us: across(): return lax.ppermute(block, ('zl', 'zh'), between)]
    ppermute x3, starting transfers between devices: 16.1 us -> 17.8 us  [the longest x2 15.9 us: across(): return lax.ppermute(block, ('zl', 'zh'), between)]
    all_to_all x1, starting transfers between devices: 9.58 us -> 7.94 us  [shards(): moved = lax.all_to_all(packed, SEQ, 0, 0, tiled=True)]
  transfers between devices with their start and end apart: 13 -> 13, of which waited for: 5 -> 6; matrix products, arithmetic and copies ran while one was open for 5% -> 5% of each run, Pallas kernels for 8% -> 11%
where the time goes in v6:
time: 103 us; the launch traced here: 102 us
  starting transfers between devices  55.1 us (53%)
  waiting for transfers between devices  19 us (18%)
  local copies, waits for them, and re-layouts  13.3 us (13%)
  Pallas kernels  13.2 us (13%)
  between operations  1.5 us (1%)
    ppermute x2, starting transfers between devices, across(): return lax.ppermute(block, ('zl', 'zh'), between)  15.9 us
    unnamed x24, local copies, waits for them, and re-layouts  10.9 us
    ppermute x4, starting transfers between devices, gathered(): lax.ppermute(part, 'core', [(0, 1), (1, 0)])  9.17 us
    ppermute x1, waiting for transfers between devices, gathered(): left = lax.ppermute(column, 'x', up)  8.05 us
    all_to_all x1, starting transfers between devices, shards(): moved = lax.all_to_all(packed, SEQ, 0, 0, tiled=True)  7.94 us
    all_to_all x1, starting transfers between devices, shards(): back = lax.all_to_all(mixed, SEQ, 0, 0, tiled=True)  7.24 us
    pallas_call x1, Pallas kernels, shards(): pl.pallas_call(functools.partial(attend_kernel, vid), out_shape=jax.Shape...  6.54 us
    ppermute x2, waiting for transfers between devices, across(): return lax.ppermute(block, ('zl', 'zh'), between)  6.06 us
  transfers between devices with their start and end apart: 13, of which 6 were waited for; matrix products, arithmetic and copies ran while one was open for 5% of the time, Pallas kernels for 11%

profile of v6, /device:TPU:1, one launch (start us, length us, event | category | flops | bytes accessed | tf_op | source)
XLA Modules:
  0.0 102.3 jit_solution(7644645655588297663)
XLA Ops:
  0.6 11.5 %collective-permute-start = (bf16[48,1536]{1,0:T(8,128)(2,1)}, bf16[48,1536]{1,0:T(8,128)(2,1)S(1)}, u32[]{:S(2)}, u32[]{:S(2)}) collective-permute-start(bf16[48,1536]{1,0:T(8,128)(2,1)} %param.13), channel_id=1, source_target_pairs={{32,8},{8,32},{40,16},{16,40},{48,24},{24,48},{56,0},{0,56},{33,9}... | collective-permute-start | bytes 442376 | tf_op jit(solution)/shard_map/ppermute | solution.py:150
  12.1 3.8 %collective-permute-done = bf16[48,1536]{1,0:T(8,128)(2,1)S(1)} collective-permute-done((bf16[48,1536]{1,0:T(8,128)(2,1)}, bf16[48,1536]{1,0:T(8,128)(2,1)S(1)}, u32[]{:S(2)}, u32[]{:S(2)}) %collective-permute-start) | collective-permute-done | bytes 147488 | tf_op jit(solution)/shard_map/ppermute | solution.py:150
  15.9 1.9 %collective-permute-start.1 = (bf16[48,1536]{1,0:T(8,128)(2,1)S(1)}, bf16[48,1536]{1,0:T(8,128)(2,1)S(1)}, u32[]{:S(2)}, u32[]{:S(2)}) collective-permute-start(bf16[48,1536]{1,0:T(8,128)(2,1)S(1)} %collective-permute-done), channel_id=1, source_target_pairs={{0,32},{32,0},{1,33},{33,1},{2,34},{34,2},{3,35},{35,3},{4,36},{36... | collective-permute-start | bytes 442376 | tf_op jit(solution)/shard_map/ppermute | solution.py:172
  18.5 3.1 %pack.1 = bf16[16,3,128,128]{3,2,1,0:T(8,128)(2,1)} custom-call(s32[1]{0:T(128)S(6)} %copy.16.length_ref, s32[1]{0:T(128)} %bitcast.base_ref, bf16[120,1536]{1,0:T(8,128)(2,1)} %bitcast.17, bf16[120,2,1536]{2,1,0:T(2,128)(2,1)} %bitcast.16, bf16[8,1536]{1,0:T(8,128)(2,1)} %bitcast.19, bf16[8,2,1536]{2,1,0:T(2,128)(2,1)} %bitcast.18), custom_call_target="tpu_custom_call" | custom-call | tf_op jit(solution)/shard_map/pack/pallas_call | solution.py:178
  21.8 7.9 %all-to-all-start = ((bf16[16,3,128,128]{3,2,1,0:T(8,128)(2,1)}), bf16[16,3,128,128]{3,2,1,0:T(8,128)(2,1)S(1)}, u32[]{:S(2)}, u32[]{:S(2)}) async-start(bf16[16,3,128,128]{3,2,1,0:T(8,128)(2,1)} %pack.1), calls=%async_computation | async-start | bytes 3145728 | tf_op jit(solution)/shard_map/all_to_all | solution.py:202
  31.1 4.4 %collective-permute-start.2 = (bf16[48,1536]{1,0:T(8,128)(2,1)S(1)}, bf16[48,1536]{1,0:T(8,128)(2,1)S(1)}, u32[]{:S(2)}, u32[]{:S(2)}) collective-permute-start(bf16[48,1536]{1,0:T(8,128)(2,1)S(1)} %collective-permute-done.1), channel_id=1, source_target_pairs={{32,8},{8,32},{40,16},{16,40},{48,24},{24,48},{56,0},{0,56},{33,9}... | collective-permute-start | bytes 442376 | tf_op jit(solution)/shard_map/ppermute | solution.py:150
  36.2 2.3 %collective-permute-done.2 = bf16[48,1536]{1,0:T(8,128)(2,1)S(1)} collective-permute-done((bf16[48,1536]{1,0:T(8,128)(2,1)S(1)}, bf16[48,1536]{1,0:T(8,128)(2,1)S(1)}, u32[]{:S(2)}, u32[]{:S(2)}) %collective-permute-start.2) | collective-permute-done | bytes 147488 | tf_op jit(solution)/shard_map/ppermute | solution.py:150
  39.1 3.1 %collective-permute-start.3 = (bf16[192,1536]{1,0:T(8,128)(2,1)}, bf16[192,1536]{1,0:T(8,128)(2,1)S(1)}, u32[]{:S(2)}, u32[]{:S(2)}) collective-permute-start(bf16[192,1536]{1,0:T(8,128)(2,1)} %constant_dynamic-update-slice_fusion.refs_0_), channel_id=1, source_target_pairs={{0,2},{2,4},{4,6},{6,0},{1,3},{3,5},{5,7},{7,1},{8,10},{10,12},{12... | collective-permute-start | bytes 1769480 | tf_op jit(solution)/shard_map/ppermute | solution.py:158
  42.2 3.4 %collective-permute-start.4 = (bf16[192,1536]{1,0:T(8,128)(2,1)}, bf16[192,1536]{1,0:T(8,128)(2,1)S(1)}, u32[]{:S(2)}, u32[]{:S(2)}) collective-permute-start(bf16[192,1536]{1,0:T(8,128)(2,1)} %constant_dynamic-update-slice_fusion.refs_0_), channel_id=1, source_target_pairs={{0,6},{2,0},{4,2},{6,4},{1,7},{3,1},{5,3},{7,5},{8,14},{10,8},{12,... | collective-permute-start | bytes 1769480 | tf_op jit(solution)/shard_map/ppermute | solution.py:159
  45.6 8.1 %collective-permute-done.3.refs_1_ = bf16[192,1536]{1,0:T(8,128)(2,1)S(1)} collective-permute-done((bf16[192,1536]{1,0:T(8,128)(2,1)}, bf16[192,1536]{1,0:T(8,128)(2,1)S(1)}, u32[]{:S(2)}, u32[]{:S(2)}) %collective-permute-start.3) | collective-permute-done | bytes 589856 | tf_op jit(solution)/shard_map/ppermute | solution.py:158
  53.7 1.9 %collective-permute-start.5 = (bf16[96,1536]{1,0:T(8,128)(2,1)S(1)}, bf16[96,1536]{1,0:T(8,128)(2,1)}, u32[]{:S(2)}, u32[]{:S(2)}) collective-permute-start(bf16[96,1536]{1,0:T(8,128)(2,1)S(1)} %slice.8), channel_id=1, source_target_pairs={{0,2},{2,4},{4,6},{6,0},{1,3},{3,5},{5,7},{7,1},{8,10},{10,12},{12... | collective-permute-start | bytes 884744 | tf_op jit(solution)/shard_map/ppermute | solution.py:161
  56.4 4.6 %collective-permute-start.6 = (bf16[96,1536]{1,0:T(8,128)(2,1)}, bf16[96,1536]{1,0:T(8,128)(2,1)}, u32[]{:S(2)}, u32[]{:S(2)}) collective-permute-start(bf16[96,1536]{1,0:T(8,128)(2,1)} %slice.9), channel_id=1, source_target_pairs={{0,6},{2,0},{4,2},{6,4},{1,7},{3,1},{5,3},{7,5},{8,14},{10,8},{12,... | collective-permute-start | bytes 884744 | tf_op jit(solution)/shard_map/ppermute | solution.py:161
  61.0 4.4 %all-to-all-done.x_ref = bf16[16,3,128,128]{3,2,1,0:T(8,128)(2,1)S(1)} async-done(((bf16[16,3,128,128]{3,2,1,0:T(8,128)(2,1)}), bf16[16,3,128,128]{3,2,1,0:T(8,128)(2,1)S(1)}, u32[]{:S(2)}, u32[]{:S(2)}) %all-to-all-start) | async-done | bytes 1572896 | tf_op jit(solution)/shard_map/all_to_all | solution.py:202
  65.4 6.5 %attend.1 = bf16[16,144,128]{2,1,0:T(8,128)(2,1)} custom-call(s32[1]{0:T(128)S(6)} %copy.16.length_ref, bf16[16,3,128,128]{3,2,1,0:T(8,128)(2,1)S(1)} %all-to-all-done.x_ref), custom_call_target="tpu_custom_call" | custom-call | tf_op jit(solution)/shard_map/attend/pallas_call | solution.py:203
  71.9 7.2 %all-to-all-start.1 = ((bf16[16,144,128]{2,1,0:T(8,128)(2,1)}), bf16[16,144,128]{2,1,0:T(8,128)(2,1)S(1)}, u32[]{:S(2)}, u32[]{:S(2)}) async-start(bf16[16,144,128]{2,1,0:T(8,128)(2,1)} %attend.1), calls=%async_computation.1 | async-start | bytes 1179648 | tf_op jit(solution)/shard_map/all_to_all | solution.py:216
  79.2 2.9 %collective-permute-start.7 = (bf16[192,1536]{1,0:T(8,128)(2,1)}, bf16[192,1536]{1,0:T(8,128)(2,1)S(1)}, u32[]{:S(2)}, u32[]{:S(2)}) collective-permute-start(bf16[192,1536]{1,0:T(8,128)(2,1)} %constant_dynamic-update-slice_fusion.refs_0_), channel_id=1, source_target_pairs={{0,1},{1,0},{2,3},{3,2},{4,5},{5,4},{6,7},{7,6},{8,9},{9,8},{10,11... | collective-permute-start | bytes 1769480 | tf_op jit(solution)/shard_map/ppermute | solution.py:163
  82.1 1.9 %collective-permute-start.9 = (bf16[192,1536]{1,0:T(8,128)(2,1)S(1)}, bf16[192,1536]{1,0:T(8,128)(2,1)}, u32[]{:S(2)}, u32[]{:S(2)}) collective-permute-start(bf16[192,1536]{1,0:T(8,128)(2,1)S(1)} %collective-permute-done.4.refs_2_), channel_id=1, source_target_pairs={{0,1},{1,0},{2,3},{3,2},{4,5},{5,4},{6,7},{7,6},{8,9},{9,8},{10,11... | collective-permute-start | bytes 1769480 | tf_op jit(solution)/shard_map/ppermute | solution.py:163
  84.0 2.4 %collective-permute-start.8 = (bf16[192,1536]{1,0:T(8,128)(2,1)S(1)}, bf16[192,1536]{1,0:T(8,128)(2,1)}, u32[]{:S(2)}, u32[]{:S(2)}) collective-permute-start(bf16[192,1536]{1,0:T(8,128)(2,1)S(1)} %collective-permute-done.3.refs_1_), channel_id=1, source_target_pairs={{0,1},{1,0},{2,3},{3,2},{4,5},{5,4},{6,7},{7,6},{8,9},{9,8},{10,11... | collective-permute-start | bytes 1769480 | tf_op jit(solution)/shard_map/ppermute | solution.py:163
  88.5 1.9 %collective-permute-start.10 = (bf16[192,1536]{1,0:T(8,128)(2,1)S(1)}, bf16[192,1536]{1,0:T(8,128)(2,1)}, u32[]{:S(2)}, u32[]{:S(2)}) collective-permute-start(bf16[192,1536]{1,0:T(8,128)(2,1)S(1)} %constant_dynamic-update-slice_fusion.4.refs_3_), channel_id=1, source_target_pairs={{0,1},{1,0},{2,3},{3,2},{4,5},{5,4},{6,7},{7,6},{8,9},{9,8},{10,11... | collective-permute-start | bytes 1769480 | tf_op jit(solution)/shard_map/ppermute | solution.py:163
  92.5 1.1 %copy-done.3 = bf16[192,1536]{1,0:T(8,128)(2,1)S(1)} copy-done((bf16[192,1536]{1,0:T(8,128)(2,1)S(1)}, bf16[192,1536]{1,0:T(8,128)(2,1)}, u32[]{:S(2)}) %copy-start.3) | copy-done | bytes 589848
  95.7 2.0 %order.1 = (bf16[1536,768]{1,0:T(8,128)(2,1)S(1)}, bf16[1536,768]{1,0:T(8,128)(2,1)S(1)}) custom-call(s32[4]{0:T(128)S(1)} %pad_add_fusion.spot_ref, bf16[192,1536]{1,0:T(8,128)(2,1)} %constant_dynamic-update-slice_fusion.refs_0_, bf16[192,1536]{1,0:T(8,128)(2,1)S(1)} %collective-permute-done.3.refs_1_, bf16[192,1536]{1,0:T(8,128)(2,1)S(1)} %copy-done.3, ...), custom_call_target="tpu_custom_call" | custom-call | tf_op jit(solution)/shard_map/order/pallas_call | solution.py:217
  97.7 1.4 %copy-done = bf16[1536,768]{1,0:T(8,128)(2,1)} copy-done((bf16[1536,768]{1,0:T(8,128)(2,1)}, bf16[1536,768]{1,0:T(8,128)(2,1)S(1)}, u32[]{:S(2)}) %copy-start) | copy-done | bytes 2359320
  99.1 1.7 %copy-done.1 = bf16[1536,768]{1,0:T(8,128)(2,1)S(1)} copy-done((bf16[1536,768]{1,0:T(8,128)(2,1)S(1)}, bf16[1536,768]{1,0:T(8,128)(2,1)}, u32[]{:S(2)}) %copy-start.1) | copy-done | bytes 2359320
  100.8 1.5 %project.1 = (bf16[120,1536]{1,0:T(8,128)(2,1)}, bf16[8,1536]{1,0:T(8,128)(2,1)}, f32[12,1,120]{2,1,0:T(1,128)}, f32[8,12]{1,0:T(8,128)}, bf16[120,1536]{1,0:T(8,128)(2,1)}) custom-call(bf16[16,144,128]{2,1,0:T(8,128)(2,1)S(1)} %all-to-all-done.1.x_ref, bf16[1536,768]{1,0:T(8,128)(2,1)S(1)} %get-tuple-element.14.w_ref, bf16[1536,768]{1,0:T(8,128)(2,1)S(1)} %copy-done.1, ...), custom_call_target="tpu_custom_call" | custom-call | tf_op jit(solution)/shard_map/project/pallas_call | solution.py:225
  (35 shorter events, 9.8 us)
Async XLA Ops:
  0.6 15.3 %collective-permute-start = (bf16[48,1536]{1,0:T(8,128)(2,1)}, bf16[48,1536]{1,0:T(8,128)(2,1)S(1)}, u32[]{:S(2)}, u32[]{:S(2)}) collective-permute-start(bf16[48,1536]{1,0:T(8,128)(2,1)} %param.13), channel_id=1, source_target_pairs={{32,8},{8,32},{40,16},{16,40},{48,24},{24,48},{56,0},{0,56},{33,9}... | collective-permute-start | bytes 442376 | tf_op jit(solution)/shard_map/ppermute | solution.py:150
  15.9 5.9 %collective-permute-start.1 = (bf16[48,1536]{1,0:T(8,128)(2,1)S(1)}, bf16[48,1536]{1,0:T(8,128)(2,1)S(1)}, u32[]{:S(2)}, u32[]{:S(2)}) collective-permute-start(bf16[48,1536]{1,0:T(8,128)(2,1)S(1)} %collective-permute-done), channel_id=1, source_target_pairs={{0,32},{32,0},{1,33},{33,1},{2,34},{34,2},{3,35},{35,3},{4,36},{36... | collective-permute-start | bytes 442376 | tf_op jit(solution)/shard_map/ppermute | solution.py:172
  18.5 11.3 %copy-start.9 = (bf16[48,1536]{1,0:T(8,128)(2,1)S(1)}, bf16[48,1536]{1,0:T(8,128)(2,1)}, u32[]{:S(2)}) copy-start(bf16[48,1536]{1,0:T(8,128)(2,1)} %param.13) | copy-start | bytes 442372
  21.8 43.6 %all-to-all-start = ((bf16[16,3,128,128]{3,2,1,0:T(8,128)(2,1)}), bf16[16,3,128,128]{3,2,1,0:T(8,128)(2,1)S(1)}, u32[]{:S(2)}, u32[]{:S(2)}) async-start(bf16[16,3,128,128]{3,2,1,0:T(8,128)(2,1)} %pack.1), calls=%async_computation | async-start | bytes 3145728 | tf_op jit(solution)/shard_map/all_to_all | solution.py:202
  31.1 7.4 %collective-permute-start.2 = (bf16[48,1536]{1,0:T(8,128)(2,1)S(1)}, bf16[48,1536]{1,0:T(8,128)(2,1)S(1)}, u32[]{:S(2)}, u32[]{:S(2)}) collective-permute-start(bf16[48,1536]{1,0:T(8,128)(2,1)S(1)} %collective-permute-done.1), channel_id=1, source_target_pairs={{32,8},{8,32},{40,16},{16,40},{48,24},{24,48},{56,0},{0,56},{33,9}... | collective-permute-start | bytes 442376 | tf_op jit(solution)/shard_map/ppermute | solution.py:150
  39.1 14.5 %collective-permute-start.3 = (bf16[192,1536]{1,0:T(8,128)(2,1)}, bf16[192,1536]{1,0:T(8,128)(2,1)S(1)}, u32[]{:S(2)}, u32[]{:S(2)}) collective-permute-start(bf16[192,1536]{1,0:T(8,128)(2,1)} %constant_dynamic-update-slice_fusion.refs_0_), channel_id=1, source_target_pairs={{0,2},{2,4},{4,6},{6,0},{1,3},{3,5},{5,7},{7,1},{8,10},{10,12},{12... | collective-permute-start | bytes 1769480 | tf_op jit(solution)/shard_map/ppermute | solution.py:158
  42.2 13.4 %collective-permute-start.4 = (bf16[192,1536]{1,0:T(8,128)(2,1)}, bf16[192,1536]{1,0:T(8,128)(2,1)S(1)}, u32[]{:S(2)}, u32[]{:S(2)}) collective-permute-start(bf16[192,1536]{1,0:T(8,128)(2,1)} %constant_dynamic-update-slice_fusion.refs_0_), channel_id=1, source_target_pairs={{0,6},{2,0},{4,2},{6,4},{1,7},{3,1},{5,3},{7,5},{8,14},{10,8},{12,... | collective-permute-start | bytes 1769480 | tf_op jit(solution)/shard_map/ppermute | solution.py:159
  53.7 32.8 %collective-permute-start.5 = (bf16[96,1536]{1,0:T(8,128)(2,1)S(1)}, bf16[96,1536]{1,0:T(8,128)(2,1)}, u32[]{:S(2)}, u32[]{:S(2)}) collective-permute-start(bf16[96,1536]{1,0:T(8,128)(2,1)S(1)} %slice.8), channel_id=1, source_target_pairs={{0,2},{2,4},{4,6},{6,0},{1,3},{3,5},{5,7},{7,1},{8,10},{10,12},{12... | collective-permute-start | bytes 884744 | tf_op jit(solution)/shard_map/ppermute | solution.py:161
  55.6 32.8 %copy-start.2 = (bf16[192,1536]{1,0:T(8,128)(2,1)}, bf16[192,1536]{1,0:T(8,128)(2,1)S(1)}, u32[]{:S(2)}) copy-start(bf16[192,1536]{1,0:T(8,128)(2,1)S(1)} %collective-permute-done.4.refs_2_) | copy-start | bytes 1769476
  56.4 31.0 %collective-permute-start.6 = (bf16[96,1536]{1,0:T(8,128)(2,1)}, bf16[96,1536]{1,0:T(8,128)(2,1)}, u32[]{:S(2)}, u32[]{:S(2)}) collective-permute-start(bf16[96,1536]{1,0:T(8,128)(2,1)} %slice.9), channel_id=1, source_target_pairs={{0,6},{2,0},{4,2},{6,4},{1,7},{3,1},{5,3},{7,5},{8,14},{10,8},{12,... | collective-permute-start | bytes 884744 | tf_op jit(solution)/shard_map/ppermute | solution.py:161
  71.9 27.2 %all-to-all-start.1 = ((bf16[16,144,128]{2,1,0:T(8,128)(2,1)}), bf16[16,144,128]{2,1,0:T(8,128)(2,1)S(1)}, u32[]{:S(2)}, u32[]{:S(2)}) async-start(bf16[16,144,128]{2,1,0:T(8,128)(2,1)} %attend.1), calls=%async_computation.1 | async-start | bytes 1179648 | tf_op jit(solution)/shard_map/all_to_all | solution.py:216
  79.2 12.1 %collective-permute-start.7 = (bf16[192,1536]{1,0:T(8,128)(2,1)}, bf16[192,1536]{1,0:T(8,128)(2,1)S(1)}, u32[]{:S(2)}, u32[]{:S(2)}) collective-permute-start(bf16[192,1536]{1,0:T(8,128)(2,1)} %constant_dynamic-update-slice_fusion.refs_0_), channel_id=1, source_target_pairs={{0,1},{1,0},{2,3},{3,2},{4,5},{5,4},{6,7},{7,6},{8,9},{9,8},{10,11... | collective-permute-start | bytes 1769480 | tf_op jit(solution)/shard_map/ppermute | solution.py:163
  82.1 10.0 %collective-permute-start.9 = (bf16[192,1536]{1,0:T(8,128)(2,1)S(1)}, bf16[192,1536]{1,0:T(8,128)(2,1)}, u32[]{:S(2)}, u32[]{:S(2)}) collective-permute-start(bf16[192,1536]{1,0:T(8,128)(2,1)S(1)} %collective-permute-done.4.refs_2_), channel_id=1, source_target_pairs={{0,1},{1,0},{2,3},{3,2},{4,5},{5,4},{6,7},{7,6},{8,9},{9,8},{10,11... | collective-permute-start | bytes 1769480 | tf_op jit(solution)/shard_map/ppermute | solution.py:163
  84.0 8.1 %collective-permute-start.8 = (bf16[192,1536]{1,0:T(8,128)(2,1)S(1)}, bf16[192,1536]{1,0:T(8,128)(2,1)}, u32[]{:S(2)}, u32[]{:S(2)}) collective-permute-start(bf16[192,1536]{1,0:T(8,128)(2,1)S(1)} %collective-permute-done.3.refs_1_), channel_id=1, source_target_pairs={{0,1},{1,0},{2,3},{3,2},{4,5},{5,4},{6,7},{7,6},{8,9},{9,8},{10,11... | collective-permute-start | bytes 1769480 | tf_op jit(solution)/shard_map/ppermute | solution.py:163
  88.5 4.0 %collective-permute-start.10 = (bf16[192,1536]{1,0:T(8,128)(2,1)S(1)}, bf16[192,1536]{1,0:T(8,128)(2,1)}, u32[]{:S(2)}, u32[]{:S(2)}) collective-permute-start(bf16[192,1536]{1,0:T(8,128)(2,1)S(1)} %constant_dynamic-update-slice_fusion.4.refs_3_), channel_id=1, source_target_pairs={{0,1},{1,0},{2,3},{3,2},{4,5},{5,4},{6,7},{7,6},{8,9},{9,8},{10,11... | collective-permute-start | bytes 1769480 | tf_op jit(solution)/shard_map/ppermute | solution.py:163
  90.4 0.8 copy-start.4
  91.2 7.9 %copy-start.8 = (f32[1,1536]{1,0:T(1,128)S(1)}, f32[1,1536]{1,0:T(1,128)}, u32[]{:S(2)}) copy-start(f32[1,1536]{1,0:T(1,128)} %gate_ref.1) | copy-start | bytes 18436
  91.3 0.8 copy-start.6
  92.5 1.1 %copy-start.3 = (bf16[192,1536]{1,0:T(8,128)(2,1)S(1)}, bf16[192,1536]{1,0:T(8,128)(2,1)}, u32[]{:S(2)}) copy-start(bf16[192,1536]{1,0:T(8,128)(2,1)} %copy-done.2) | copy-start | bytes 1769476
  93.5 1.1 %copy-start.5 = (bf16[192,1536]{1,0:T(8,128)(2,1)S(1)}, bf16[192,1536]{1,0:T(8,128)(2,1)}, u32[]{:S(2)}) copy-start(bf16[192,1536]{1,0:T(8,128)(2,1)} %copy-done.4) | copy-start | bytes 1769476
  94.6 1.1 %copy-start.7 = (bf16[192,1536]{1,0:T(8,128)(2,1)S(1)}, bf16[192,1536]{1,0:T(8,128)(2,1)}, u32[]{:S(2)}) copy-start(bf16[192,1536]{1,0:T(8,128)(2,1)} %copy-done.6) | copy-start | bytes 1769476
  97.7 1.4 %copy-start = (bf16[1536,768]{1,0:T(8,128)(2,1)}, bf16[1536,768]{1,0:T(8,128)(2,1)S(1)}, u32[]{:S(2)}) copy-start(bf16[1536,768]{1,0:T(8,128)(2,1)S(1)} %get-tuple-element.15.more_ref) | copy-start | bytes 7077892
  99.1 1.7 %copy-start.1 = (bf16[1536,768]{1,0:T(8,128)(2,1)S(1)}, bf16[1536,768]{1,0:T(8,128)(2,1)}, u32[]{:S(2)}) copy-start(bf16[1536,768]{1,0:T(8,128)(2,1)} %copy-done) | copy-start | bytes 7077892

commit v7 on v6

--- a/solution.py
+++ b/solution.py
@@ -101,9 +101,9 @@
             out_ref[s, rows:] = parts.astype(jnp.bfloat16)
 
 
-def project_kernel(
-    x_ref, w_ref, more_ref, gate_ref, av_ref, at_ref, lv_ref, lt_ref, pv_ref
-):
+def project_kernel(spot_ref, x_ref, gate_ref, *refs):
+    pieces = refs[:8]
+    av_ref, at_ref, lv_ref, lt_ref, pv_ref, turned_ref, mixed_ref = refs[8:]
     vid = av_ref.shape[0]
     rows = vid + at_ref.shape[0]
     lses = []
@@ -111,34 +111,37 @@
         cols = pl.ds(h * HEAD, HEAD)
         av_ref[:, cols] = x_ref[h, :vid]
         at_ref[:, cols] = x_ref[h, vid:rows]
+        turned_ref[cols, :] = x_ref[h, :rows].astype(jnp.float32).T.astype(jnp.bfloat16)
         parts = x_ref[h, rows:].astype(jnp.float32)
         lse = parts[0:1] + parts[1:2] + parts[2:3]
         lv_ref[h] = lse[:, :vid]
         lses.append(lse)
     lses += [lses[0]] * (HEAD - HEADS)
     lt_ref[...] = jnp.concatenate(lses, axis=0).T[vid:, :HEADS]
-    split = w_ref.shape[1]
-    for part, here in ((w_ref, pl.ds(0, split)), (more_ref, pl.ds(split, more_ref.shape[1]))):
-        out = jnp.dot(av_ref[...], part[...], preferred_element_type=jnp.float32)
-        pv_ref[:, here] = (out * gate_ref[:, here]).astype(jnp.bfloat16)
-
-
-def order_kernel(count, spot_ref, *refs):
-    *pieces, w_ref, more_ref = refs
-    split = w_ref.shape[1]
+
     zl, zh, x, core = spot_ref[0], spot_ref[1], spot_ref[2], spot_ref[3]
     nz, nx = SIZES["zh"], SIZES["x"]
     near = 2 * zl - 1 + nz
     of_z = (zh, zh + near, zh + nz - near, zh + nz // 2)
     of_x = (x, x + nx - 1, x + 1, x + nx // 2)
-    for i, piece in enumerate(pieces):
-        which = i % len(of_x)
-        for j in range(len(of_z)):
-            row = (of_z[j] + nz) % nz * nx + (of_x[which]) % nx
-            row = (row * SIZES["core"] + (core ^ (i // len(of_x)))) * count
-            target = pl.ds(pl.multiple_of(row, 16), count)
-            w_ref[target, :] = piece[pl.ds(j * count, count), :split]
-            more_ref[target, :] = piece[pl.ds(j * count, count), split:]
+    depth = pieces[0].shape[0]
+    count = depth // nz
+    for i in range(len(pieces)):
+        for j in range(nz):
+            row = (of_z[j] + nz) % nz * nx + of_x[i % nx] % nx
+            row = (row * SIZES["core"] + (core ^ (i // nx))) * count
+            source = pl.ds(pl.multiple_of(row, 16), count)
+            mixed_ref[pl.ds(i * depth + j * count, count), :] = turned_ref[source, :]
+    mixed = mixed_ref[...].astype(jnp.float32).T[:vid].astype(jnp.bfloat16)
+    width = 512
+    for first in range(0, pv_ref.shape[1], width):
+        here = pl.ds(first, width)
+        out = jnp.zeros((vid, width), jnp.float32)
+        for i, piece in enumerate(pieces):
+            out += jnp.dot(
+                mixed[:, i * depth : (i + 1) * depth], piece[:, here], preferred_element_type=jnp.float32
+            )
+        pv_ref[:, here] = (out * gate_ref[:, here]).astype(jnp.bfloat16)
 
 
 def across(block):
@@ -214,14 +217,6 @@
         name="attend",
     )(text_lengths, moved)
     back = lax.all_to_all(mixed, SEQ, 0, 0, tiled=True)
-    halves = pl.pallas_call(
-        functools.partial(order_kernel, w_out.shape[0]),
-        out_shape=(jax.ShapeDtypeStruct((feats, feats // 2), jnp.bfloat16),) * 2,
-        in_specs=[smem, *[vmem] * len(pieces)],
-        out_specs=(vmem,) * 2,
-        compiler_params=pltpu.CompilerParams(vmem_limit_bytes=32 << 20),
-        name="order",
-    )(spot.astype(jnp.int32), *pieces)
     attn_video, attn_text, lse_video, lse_text, proj_video = pl.pallas_call(
         project_kernel,
         out_shape=(
@@ -231,11 +226,12 @@
             jax.ShapeDtypeStruct((txt, HEADS), jnp.float32),
             jax.ShapeDtypeStruct((vid, feats), jnp.bfloat16),
         ),
-        in_specs=[vmem] * 4,
+        in_specs=[smem, *[vmem] * (2 + len(pieces))],
         out_specs=(vmem,) * 5,
-        compiler_params=pltpu.CompilerParams(vmem_limit_bytes=32 << 20),
+        scratch_shapes=[VMEM((feats, rows), jnp.bfloat16)] * 2,
+        compiler_params=pltpu.CompilerParams(vmem_limit_bytes=16 << 20),
         name="project",
-    )(back, *halves, gate)
+    )(spot.astype(jnp.int32), back, gate, *pieces)
     return (
         attn_video[None],
         attn_text[None],

time: 103 us -> 102 us (level)
  the two profiles are of different devices: /device:TPU:1 before, /device:TPU:4 now
where the time goes in v7:
time: 102 us
  starting transfers between devices  50.3 us (49%)
  waiting for transfers between devices  32.7 us (32%)
  Pallas kernels  13.5 us (13%)
  local copies, waits for them, and re-layouts  3.49 us (3%)
  between operations  1.49 us (1%)
    ppermute x2, starting transfers between devices, across(): return lax.ppermute(block, ('zl', 'zh'), between)  16.9 us
    ppermute x4, starting transfers between devices, gathered(): lax.ppermute(part, 'core', [(0, 1), (1, 0)])  8.66 us
    ppermute x1, waiting for transfers between devices, gathered(): left = lax.ppermute(column, 'x', up)  8.29 us
    all_to_all x1, waiting for transfers between devices, shards(): moved = lax.all_to_all(packed, SEQ, 0, 0, tiled=True)  7.92 us
    all_to_all x1, starting transfers between devices, shards(): moved = lax.all_to_all(packed, SEQ, 0, 0, tiled=True)  7.43 us
    ppermute x2, waiting for transfers between devices, across(): return lax.ppermute(block, ('zl', 'zh'), between)  7.13 us
    pallas_call x1, Pallas kernels, shards(): pl.pallas_call(functools.partial(attend_kernel, vid), out_shape=jax.Shape...  6.54 us
    all_to_all x1, waiting for transfers between devices, shards(): back = lax.all_to_all(mixed, SEQ, 0, 0, tiled=True)  6.33 us
  transfers between devices with their start and end apart: 13, of which 7 were waited for; matrix products, arithmetic and copies ran while one was open for 3% of the time, Pallas kernels for 9%

profile of v7, /device:TPU:4, one launch (start us, length us, event | category | flops | bytes accessed | tf_op | source)
XLA Modules:
  0.0 101.6 jit_solution(3234889423480060284)
XLA Ops:
  0.6 10.9 %collective-permute-start = (bf16[48,1536]{1,0:T(8,128)(2,1)}, bf16[48,1536]{1,0:T(8,128)(2,1)S(1)}, u32[]{:S(2)}, u32[]{:S(2)}) collective-permute-start(bf16[48,1536]{1,0:T(8,128)(2,1)} %param.13), channel_id=1, source_target_pairs={{32,8},{8,32},{40,16},{16,40},{48,24},{24,48},{56,0},{0,56},{33,9}... | collective-permute-start | bytes 442376 | tf_op jit(solution)/shard_map/ppermute | solution.py:153
  11.6 4.0 %collective-permute-done = bf16[48,1536]{1,0:T(8,128)(2,1)S(1)} collective-permute-done((bf16[48,1536]{1,0:T(8,128)(2,1)}, bf16[48,1536]{1,0:T(8,128)(2,1)S(1)}, u32[]{:S(2)}, u32[]{:S(2)}) %collective-permute-start) | collective-permute-done | bytes 147488 | tf_op jit(solution)/shard_map/ppermute | solution.py:153
  15.6 1.9 %collective-permute-start.1 = (bf16[48,1536]{1,0:T(8,128)(2,1)S(1)}, bf16[48,1536]{1,0:T(8,128)(2,1)S(1)}, u32[]{:S(2)}, u32[]{:S(2)}) collective-permute-start(bf16[48,1536]{1,0:T(8,128)(2,1)S(1)} %collective-permute-done), channel_id=1, source_target_pairs={{0,32},{32,0},{1,33},{33,1},{2,34},{34,2},{3,35},{35,3},{4,36},{36... | collective-permute-start | bytes 442376 | tf_op jit(solution)/shard_map/ppermute | solution.py:175
  18.2 3.1 %pack.1 = bf16[16,3,128,128]{3,2,1,0:T(8,128)(2,1)} custom-call(s32[1]{0:T(128)S(6)} %copy.16.length_ref, s32[1]{0:T(128)} %bitcast.4.base_ref, bf16[120,1536]{1,0:T(8,128)(2,1)} %bitcast.17, bf16[120,2,1536]{2,1,0:T(2,128)(2,1)} %bitcast.16, bf16[8,1536]{1,0:T(8,128)(2,1)} %bitcast.19, bf16[8,2,1536]{2,1,0:T(2,128)(2,1)} %bitcast.18), custom_call_target="tpu_custom_call" | custom-call | tf_op jit(solution)/shard_map/pack/pallas_call | solution.py:181
  21.3 1.4 %collective-permute-done.1 = bf16[48,1536]{1,0:T(8,128)(2,1)S(1)} collective-permute-done((bf16[48,1536]{1,0:T(8,128)(2,1)S(1)}, bf16[48,1536]{1,0:T(8,128)(2,1)S(1)}, u32[]{:S(2)}, u32[]{:S(2)}) %collective-permute-start.1) | collective-permute-done | bytes 147488 | tf_op jit(solution)/shard_map/ppermute | solution.py:175
  22.7 7.4 %all-to-all-start = ((bf16[16,3,128,128]{3,2,1,0:T(8,128)(2,1)}), bf16[16,3,128,128]{3,2,1,0:T(8,128)(2,1)S(1)}, u32[]{:S(2)}, u32[]{:S(2)}) async-start(bf16[16,3,128,128]{3,2,1,0:T(8,128)(2,1)} %pack.1), calls=%async_computation | async-start | bytes 3145728 | tf_op jit(solution)/shard_map/all_to_all | solution.py:205
  30.1 6.0 %collective-permute-start.2 = (bf16[48,1536]{1,0:T(8,128)(2,1)S(1)}, bf16[48,1536]{1,0:T(8,128)(2,1)S(1)}, u32[]{:S(2)}, u32[]{:S(2)}) collective-permute-start(bf16[48,1536]{1,0:T(8,128)(2,1)S(1)} %collective-permute-done.1), channel_id=1, source_target_pairs={{32,8},{8,32},{40,16},{16,40},{48,24},{24,48},{56,0},{0,56},{33,9}... | collective-permute-start | bytes 442376 | tf_op jit(solution)/shard_map/ppermute | solution.py:153
  36.2 3.1 %collective-permute-done.2 = bf16[48,1536]{1,0:T(8,128)(2,1)S(1)} collective-permute-done((bf16[48,1536]{1,0:T(8,128)(2,1)S(1)}, bf16[48,1536]{1,0:T(8,128)(2,1)S(1)}, u32[]{:S(2)}, u32[]{:S(2)}) %collective-permute-start.2) | collective-permute-done | bytes 147488 | tf_op jit(solution)/shard_map/ppermute | solution.py:153
  39.3 3.1 %collective-permute-start.3 = (bf16[192,1536]{1,0:T(8,128)(2,1)S(1)}, bf16[192,1536]{1,0:T(8,128)(2,1)S(1)}, u32[]{:S(2)}, u32[]{:S(2)}) collective-permute-start(bf16[192,1536]{1,0:T(8,128)(2,1)S(1)} %constant_dynamic-update-slice_fusion.refs_0_), channel_id=1, source_target_pairs={{0,2},{2,4},{4,6},{6,0},{1,3},{3,5},{5,7},{7,1},{8,10},{10,12},{12... | collective-permute-start | bytes 1769480 | tf_op jit(solution)/shard_map/ppermute | solution.py:161
  42.4 2.7 %collective-permute-start.4 = (bf16[192,1536]{1,0:T(8,128)(2,1)S(1)}, bf16[192,1536]{1,0:T(8,128)(2,1)S(1)}, u32[]{:S(2)}, u32[]{:S(2)}) collective-permute-start(bf16[192,1536]{1,0:T(8,128)(2,1)S(1)} %constant_dynamic-update-slice_fusion.refs_0_), channel_id=1, source_target_pairs={{0,6},{2,0},{4,2},{6,4},{1,7},{3,1},{5,3},{7,5},{8,14},{10,8},{12,... | collective-permute-start | bytes 1769480 | tf_op jit(solution)/shard_map/ppermute | solution.py:162
  45.1 8.3 %collective-permute-done.3.refs_1_ = bf16[192,1536]{1,0:T(8,128)(2,1)S(1)} collective-permute-done((bf16[192,1536]{1,0:T(8,128)(2,1)S(1)}, bf16[192,1536]{1,0:T(8,128)(2,1)S(1)}, u32[]{:S(2)}, u32[]{:S(2)}) %collective-permute-start.3) | collective-permute-done | bytes 589856 | tf_op jit(solution)/shard_map/ppermute | solution.py:161
  54.1 3.1 %collective-permute-start.5 = (bf16[96,1536]{1,0:T(8,128)(2,1)}, bf16[96,1536]{1,0:T(8,128)(2,1)}, u32[]{:S(2)}, u32[]{:S(2)}) collective-permute-start(bf16[96,1536]{1,0:T(8,128)(2,1)} %slice.8), channel_id=1, source_target_pairs={{0,2},{2,4},{4,6},{6,0},{1,3},{3,5},{5,7},{7,1},{8,10},{10,12},{12... | collective-permute-start | bytes 884744 | tf_op jit(solution)/shard_map/ppermute | solution.py:164
  58.0 2.7 %collective-permute-start.6 = (bf16[96,1536]{1,0:T(8,128)(2,1)}, bf16[96,1536]{1,0:T(8,128)(2,1)}, u32[]{:S(2)}, u32[]{:S(2)}) collective-permute-start(bf16[96,1536]{1,0:T(8,128)(2,1)} %slice.9), channel_id=1, source_target_pairs={{0,6},{2,0},{4,2},{6,4},{1,7},{3,1},{5,3},{7,5},{8,14},{10,8},{12,... | collective-permute-start | bytes 884744 | tf_op jit(solution)/shard_map/ppermute | solution.py:164
  60.7 7.9 %all-to-all-done.x_ref = bf16[16,3,128,128]{3,2,1,0:T(8,128)(2,1)S(1)} async-done(((bf16[16,3,128,128]{3,2,1,0:T(8,128)(2,1)}), bf16[16,3,128,128]{3,2,1,0:T(8,128)(2,1)S(1)}, u32[]{:S(2)}, u32[]{:S(2)}) %all-to-all-start) | async-done | bytes 1572896 | tf_op jit(solution)/shard_map/all_to_all | solution.py:205
  68.6 6.5 %attend.1 = bf16[16,144,128]{2,1,0:T(8,128)(2,1)} custom-call(s32[1]{0:T(128)S(6)} %copy.16.length_ref, bf16[16,3,128,128]{3,2,1,0:T(8,128)(2,1)S(1)} %all-to-all-done.x_ref), custom_call_target="tpu_custom_call" | custom-call | tf_op jit(solution)/shard_map/attend/pallas_call | solution.py:206
  75.2 3.7 %all-to-all-start.1 = ((bf16[16,144,128]{2,1,0:T(8,128)(2,1)}), bf16[16,144,128]{2,1,0:T(8,128)(2,1)S(1)}, u32[]{:S(2)}, u32[]{:S(2)}) async-start(bf16[16,144,128]{2,1,0:T(8,128)(2,1)} %attend.1), calls=%async_computation.1 | async-start | bytes 1179648 | tf_op jit(solution)/shard_map/all_to_all | solution.py:219
  78.9 1.9 %collective-permute-start.7 = (bf16[192,1536]{1,0:T(8,128)(2,1)S(1)}, bf16[192,1536]{1,0:T(8,128)(2,1)}, u32[]{:S(2)}, u32[]{:S(2)}) collective-permute-start(bf16[192,1536]{1,0:T(8,128)(2,1)S(1)} %constant_dynamic-update-slice_fusion.refs_0_), channel_id=1, source_target_pairs={{0,1},{1,0},{2,3},{3,2},{4,5},{5,4},{6,7},{7,6},{8,9},{9,8},{10,11... | collective-permute-start | bytes 1769480 | tf_op jit(solution)/shard_map/ppermute | solution.py:166
  80.8 2.4 %collective-permute-start.8 = (bf16[192,1536]{1,0:T(8,128)(2,1)S(1)}, bf16[192,1536]{1,0:T(8,128)(2,1)}, u32[]{:S(2)}, u32[]{:S(2)}) collective-permute-start(bf16[192,1536]{1,0:T(8,128)(2,1)S(1)} %collective-permute-done.3.refs_1_), channel_id=1, source_target_pairs={{0,1},{1,0},{2,3},{3,2},{4,5},{5,4},{6,7},{7,6},{8,9},{9,8},{10,11... | collective-permute-start | bytes 1769480 | tf_op jit(solution)/shard_map/ppermute | solution.py:166
  83.3 1.9 %collective-permute-start.9 = (bf16[192,1536]{1,0:T(8,128)(2,1)S(1)}, bf16[192,1536]{1,0:T(8,128)(2,1)}, u32[]{:S(2)}, u32[]{:S(2)}) collective-permute-start(bf16[192,1536]{1,0:T(8,128)(2,1)S(1)} %collective-permute-done.4.refs_2_), channel_id=1, source_target_pairs={{0,1},{1,0},{2,3},{3,2},{4,5},{5,4},{6,7},{7,6},{8,9},{9,8},{10,11... | collective-permute-start | bytes 1769480 | tf_op jit(solution)/shard_map/ppermute | solution.py:166
  86.2 1.0 constant_dynamic-update-slice_fusion.4.refs_3_
  87.2 2.4 %collective-permute-start.10 = (bf16[192,1536]{1,0:T(8,128)(2,1)S(1)}, bf16[192,1536]{1,0:T(8,128)(2,1)}, u32[]{:S(2)}, u32[]{:S(2)}) collective-permute-start(bf16[192,1536]{1,0:T(8,128)(2,1)S(1)} %constant_dynamic-update-slice_fusion.4.refs_3_), channel_id=1, source_target_pairs={{0,1},{1,0},{2,3},{3,2},{4,5},{5,4},{6,7},{7,6},{8,9},{9,8},{10,11... | collective-permute-start | bytes 1769480 | tf_op jit(solution)/shard_map/ppermute | solution.py:166
  89.7 1.6 %collective-permute-done.10.refs_7_ = bf16[192,1536]{1,0:T(8,128)(2,1)} collective-permute-done((bf16[192,1536]{1,0:T(8,128)(2,1)S(1)}, bf16[192,1536]{1,0:T(8,128)(2,1)}, u32[]{:S(2)}, u32[]{:S(2)}) %collective-permute-start.10) | collective-permute-done | bytes 589856 | tf_op jit(solution)/shard_map/ppermute | solution.py:166
  91.3 6.3 %all-to-all-done.1.x_ref = bf16[16,144,128]{2,1,0:T(8,128)(2,1)S(1)} async-done(((bf16[16,144,128]{2,1,0:T(8,128)(2,1)}), bf16[16,144,128]{2,1,0:T(8,128)(2,1)S(1)}, u32[]{:S(2)}, u32[]{:S(2)}) %all-to-all-start.1) | async-done | bytes 589856 | tf_op jit(solution)/shard_map/all_to_all | solution.py:219
  97.7 3.9 %project.1 = (bf16[120,1536]{1,0:T(8,128)(2,1)}, bf16[8,1536]{1,0:T(8,128)(2,1)}, f32[12,1,120]{2,1,0:T(1,128)}, f32[8,12]{1,0:T(8,128)}, bf16[120,1536]{1,0:T(8,128)(2,1)}) custom-call(s32[4]{0:T(128)S(1)} %pad_add_fusion.spot_ref, bf16[16,144,128]{2,1,0:T(8,128)(2,1)S(1)} %all-to-all-done.1.x_ref, f32[1,1536]{1,0:T(1,128)S(1)} %copy-done, ...), custom_call_target="tpu_custom_call" | custom-call | tf_op jit(solution)/shard_map/project/pallas_call | solution.py:220
  (18 shorter events, 2.6 us)
Async XLA Ops:
  0.6 15.0 %collective-permute-start = (bf16[48,1536]{1,0:T(8,128)(2,1)}, bf16[48,1536]{1,0:T(8,128)(2,1)S(1)}, u32[]{:S(2)}, u32[]{:S(2)}) collective-permute-start(bf16[48,1536]{1,0:T(8,128)(2,1)} %param.13), channel_id=1, source_target_pairs={{32,8},{8,32},{40,16},{16,40},{48,24},{24,48},{56,0},{0,56},{33,9}... | collective-permute-start | bytes 442376 | tf_op jit(solution)/shard_map/ppermute | solution.py:153
  15.6 7.0 %collective-permute-start.1 = (bf16[48,1536]{1,0:T(8,128)(2,1)S(1)}, bf16[48,1536]{1,0:T(8,128)(2,1)S(1)}, u32[]{:S(2)}, u32[]{:S(2)}) collective-permute-start(bf16[48,1536]{1,0:T(8,128)(2,1)S(1)} %collective-permute-done), channel_id=1, source_target_pairs={{0,32},{32,0},{1,33},{33,1},{2,34},{34,2},{3,35},{35,3},{4,36},{36... | collective-permute-start | bytes 442376 | tf_op jit(solution)/shard_map/ppermute | solution.py:175
  21.3 8.8 %copy-start.1 = (bf16[48,1536]{1,0:T(8,128)(2,1)S(1)}, bf16[48,1536]{1,0:T(8,128)(2,1)}, u32[]{:S(2)}) copy-start(bf16[48,1536]{1,0:T(8,128)(2,1)} %param.13) | copy-start | bytes 442372
  22.7 46.0 %all-to-all-start = ((bf16[16,3,128,128]{3,2,1,0:T(8,128)(2,1)}), bf16[16,3,128,128]{3,2,1,0:T(8,128)(2,1)S(1)}, u32[]{:S(2)}, u32[]{:S(2)}) async-start(bf16[16,3,128,128]{3,2,1,0:T(8,128)(2,1)} %pack.1), calls=%async_computation | async-start | bytes 3145728 | tf_op jit(solution)/shard_map/all_to_all | solution.py:205
  30.1 9.1 %collective-permute-start.2 = (bf16[48,1536]{1,0:T(8,128)(2,1)S(1)}, bf16[48,1536]{1,0:T(8,128)(2,1)S(1)}, u32[]{:S(2)}, u32[]{:S(2)}) collective-permute-start(bf16[48,1536]{1,0:T(8,128)(2,1)S(1)} %collective-permute-done.1), channel_id=1, source_target_pairs={{32,8},{8,32},{40,16},{16,40},{48,24},{24,48},{56,0},{0,56},{33,9}... | collective-permute-start | bytes 442376 | tf_op jit(solution)/shard_map/ppermute | solution.py:153
  39.3 14.1 %collective-permute-start.3 = (bf16[192,1536]{1,0:T(8,128)(2,1)S(1)}, bf16[192,1536]{1,0:T(8,128)(2,1)S(1)}, u32[]{:S(2)}, u32[]{:S(2)}) collective-permute-start(bf16[192,1536]{1,0:T(8,128)(2,1)S(1)} %constant_dynamic-update-slice_fusion.refs_0_), channel_id=1, source_target_pairs={{0,2},{2,4},{4,6},{6,0},{1,3},{3,5},{5,7},{7,1},{8,10},{10,12},{12... | collective-permute-start | bytes 1769480 | tf_op jit(solution)/shard_map/ppermute | solution.py:161
  42.4 14.9 %collective-permute-start.4 = (bf16[192,1536]{1,0:T(8,128)(2,1)S(1)}, bf16[192,1536]{1,0:T(8,128)(2,1)S(1)}, u32[]{:S(2)}, u32[]{:S(2)}) collective-permute-start(bf16[192,1536]{1,0:T(8,128)(2,1)S(1)} %constant_dynamic-update-slice_fusion.refs_0_), channel_id=1, source_target_pairs={{0,6},{2,0},{4,2},{6,4},{1,7},{3,1},{5,3},{7,5},{8,14},{10,8},{12,... | collective-permute-start | bytes 1769480 | tf_op jit(solution)/shard_map/ppermute | solution.py:162
  54.1 31.0 %collective-permute-start.5 = (bf16[96,1536]{1,0:T(8,128)(2,1)}, bf16[96,1536]{1,0:T(8,128)(2,1)}, u32[]{:S(2)}, u32[]{:S(2)}) collective-permute-start(bf16[96,1536]{1,0:T(8,128)(2,1)} %slice.8), channel_id=1, source_target_pairs={{0,2},{2,4},{4,6},{6,0},{1,3},{3,5},{5,7},{7,1},{8,10},{10,12},{12... | collective-permute-start | bytes 884744 | tf_op jit(solution)/shard_map/ppermute | solution.py:164
  58.0 28.2 %collective-permute-start.6 = (bf16[96,1536]{1,0:T(8,128)(2,1)}, bf16[96,1536]{1,0:T(8,128)(2,1)}, u32[]{:S(2)}, u32[]{:S(2)}) collective-permute-start(bf16[96,1536]{1,0:T(8,128)(2,1)} %slice.9), channel_id=1, source_target_pairs={{0,6},{2,0},{4,2},{6,4},{1,7},{3,1},{5,3},{7,5},{8,14},{10,8},{12,... | collective-permute-start | bytes 884744 | tf_op jit(solution)/shard_map/ppermute | solution.py:164
  75.2 22.5 %copy-start = (f32[1,1536]{1,0:T(1,128)S(1)}, f32[1,1536]{1,0:T(1,128)}, u32[]{:S(2)}) copy-start(f32[1,1536]{1,0:T(1,128)} %gate_ref.1) | copy-start | bytes 18436
  75.2 22.5 %all-to-all-start.1 = ((bf16[16,144,128]{2,1,0:T(8,128)(2,1)}), bf16[16,144,128]{2,1,0:T(8,128)(2,1)S(1)}, u32[]{:S(2)}, u32[]{:S(2)}) async-start(bf16[16,144,128]{2,1,0:T(8,128)(2,1)} %attend.1), calls=%async_computation.1 | async-start | bytes 1179648 | tf_op jit(solution)/shard_map/all_to_all | solution.py:219
  78.9 10.8 %collective-permute-start.7 = (bf16[192,1536]{1,0:T(8,128)(2,1)S(1)}, bf16[192,1536]{1,0:T(8,128)(2,1)}, u32[]{:S(2)}, u32[]{:S(2)}) collective-permute-start(bf16[192,1536]{1,0:T(8,128)(2,1)S(1)} %constant_dynamic-update-slice_fusion.refs_0_), channel_id=1, source_target_pairs={{0,1},{1,0},{2,3},{3,2},{4,5},{5,4},{6,7},{7,6},{8,9},{9,8},{10,11... | collective-permute-start | bytes 1769480 | tf_op jit(solution)/shard_map/ppermute | solution.py:166
  80.8 8.8 %collective-permute-start.8 = (bf16[192,1536]{1,0:T(8,128)(2,1)S(1)}, bf16[192,1536]{1,0:T(8,128)(2,1)}, u32[]{:S(2)}, u32[]{:S(2)}) collective-permute-start(bf16[192,1536]{1,0:T(8,128)(2,1)S(1)} %collective-permute-done.3.refs_1_), channel_id=1, source_target_pairs={{0,1},{1,0},{2,3},{3,2},{4,5},{5,4},{6,7},{7,6},{8,9},{9,8},{10,11... | collective-permute-start | bytes 1769480 | tf_op jit(solution)/shard_map/ppermute | solution.py:166
  83.3 6.4 %collective-permute-start.9 = (bf16[192,1536]{1,0:T(8,128)(2,1)S(1)}, bf16[192,1536]{1,0:T(8,128)(2,1)}, u32[]{:S(2)}, u32[]{:S(2)}) collective-permute-start(bf16[192,1536]{1,0:T(8,128)(2,1)S(1)} %collective-permute-done.4.refs_2_), channel_id=1, source_target_pairs={{0,1},{1,0},{2,3},{3,2},{4,5},{5,4},{6,7},{7,6},{8,9},{9,8},{10,11... | collective-permute-start | bytes 1769480 | tf_op jit(solution)/shard_map/ppermute | solution.py:166
  87.2 4.2 %collective-permute-start.10 = (bf16[192,1536]{1,0:T(8,128)(2,1)S(1)}, bf16[192,1536]{1,0:T(8,128)(2,1)}, u32[]{:S(2)}, u32[]{:S(2)}) collective-permute-start(bf16[192,1536]{1,0:T(8,128)(2,1)S(1)} %constant_dynamic-update-slice_fusion.4.refs_3_), channel_id=1, source_target_pairs={{0,1},{1,0},{2,3},{3,2},{4,5},{5,4},{6,7},{7,6},{8,9},{9,8},{10,11... | collective-permute-start | bytes 1769480 | tf_op jit(solution)/shard_map/ppermute | solution.py:166

commit v8 on v7

--- a/solution.py
+++ b/solution.py
@@ -201,7 +201,7 @@
         q_text[0],
         kv_text[0],
     )
-    packed = lax.optimization_barrier((packed, second))[0]
+    packed = lax.optimization_barrier((packed, first))[0]
     moved = lax.all_to_all(packed, SEQ, 0, 0, tiled=True)
     mixed = pl.pallas_call(
         functools.partial(attend_kernel, vid),

time: 102 us -> 95.7 us (0.938)
  the two profiles are of different devices: /device:TPU:4 before, /device:TPU:1 now
where the time goes in v8:
time: 95.7 us; the launch traced here: 94.9 us
  starting transfers between devices  57.1 us (60%)
  waiting for transfers between devices  19.3 us (20%)
  Pallas kernels  13.5 us (14%)
  local copies, waits for them, and re-layouts  3.49 us (4%)
  between operations  1.5 us (2%)
    ppermute x2, starting transfers between devices, across(): return lax.ppermute(block, ('zl', 'zh'), between)  14.8 us
    ppermute x4, starting transfers between devices, gathered(): lax.ppermute(part, 'core', [(0, 1), (1, 0)])  12.9 us
    ppermute x1, waiting for transfers between devices, gathered(): left = lax.ppermute(column, 'x', up)  8.81 us
    all_to_all x1, starting transfers between devices, shards(): moved = lax.all_to_all(packed, SEQ, 0, 0, tiled=True)  7.06 us
    pallas_call x1, Pallas kernels, shards(): pl.pallas_call(functools.partial(attend_kernel, vid), out_shape=jax.Shape...  6.55 us
    all_to_all x1, starting transfers between devices, shards(): back = lax.all_to_all(mixed, SEQ, 0, 0, tiled=True)  6.07 us
    ppermute x1, starting transfers between devices, gathered(): lax.ppermute(right[half:], 'x', down)  4.56 us
    ppermute x1, waiting for transfers between devices, shards(): second = lax.ppermute(first, 'zl', [(0, 1), (1, 0)])  4.44 us
  transfers between devices with their start and end apart: 13, of which 4 were waited for; matrix products, arithmetic and copies ran while one was open for 4% of the time, Pallas kernels for 10%

profile of v8, /device:TPU:1, one launch (start us, length us, event | category | flops | bytes accessed | tf_op | source)
XLA Modules:
  0.0 94.9 jit_solution(14341380021072389618)
XLA Ops:
  0.6 11.5 %collective-permute-start = (bf16[48,1536]{1,0:T(8,128)(2,1)}, bf16[48,1536]{1,0:T(8,128)(2,1)S(1)}, u32[]{:S(2)}, u32[]{:S(2)}) collective-permute-start(bf16[48,1536]{1,0:T(8,128)(2,1)} %param.13), channel_id=1, source_target_pairs={{32,8},{8,32},{40,16},{16,40},{48,24},{24,48},{56,0},{0,56},{33,9}... | collective-permute-start | bytes 442376 | tf_op jit(solution)/shard_map/ppermute | solution.py:153
  12.8 3.1 %pack.1 = bf16[16,3,128,128]{3,2,1,0:T(8,128)(2,1)} custom-call(s32[1]{0:T(128)S(6)} %copy.16.length_ref, s32[1]{0:T(128)} %bitcast.4.base_ref, bf16[120,1536]{1,0:T(8,128)(2,1)} %bitcast.17, bf16[120,2,1536]{2,1,0:T(2,128)(2,1)} %bitcast.16, bf16[8,1536]{1,0:T(8,128)(2,1)} %bitcast.19, bf16[8,2,1536]{2,1,0:T(2,128)(2,1)} %bitcast.18), custom_call_target="tpu_custom_call" | custom-call | tf_op jit(solution)/shard_map/pack/pallas_call | solution.py:181
  15.9 7.1 %all-to-all-start = ((bf16[16,3,128,128]{3,2,1,0:T(8,128)(2,1)}), bf16[16,3,128,128]{3,2,1,0:T(8,128)(2,1)S(1)}, u32[]{:S(2)}, u32[]{:S(2)}) async-start(bf16[16,3,128,128]{3,2,1,0:T(8,128)(2,1)} %pack.1), calls=%async_computation | async-start | bytes 3145728 | tf_op jit(solution)/shard_map/all_to_all | solution.py:205
  23.0 3.3 %collective-permute-start.1 = (bf16[48,1536]{1,0:T(8,128)(2,1)S(1)}, bf16[48,1536]{1,0:T(8,128)(2,1)S(1)}, u32[]{:S(2)}, u32[]{:S(2)}) collective-permute-start(bf16[48,1536]{1,0:T(8,128)(2,1)S(1)} %collective-permute-done), channel_id=1, source_target_pairs={{0,32},{32,0},{1,33},{33,1},{2,34},{34,2},{3,35},{35,3},{4,36},{36... | collective-permute-start | bytes 442376 | tf_op jit(solution)/shard_map/ppermute | solution.py:175
  26.3 4.4 %collective-permute-done.1 = bf16[48,1536]{1,0:T(8,128)(2,1)S(1)} collective-permute-done((bf16[48,1536]{1,0:T(8,128)(2,1)S(1)}, bf16[48,1536]{1,0:T(8,128)(2,1)S(1)}, u32[]{:S(2)}, u32[]{:S(2)}) %collective-permute-start.1) | collective-permute-done | bytes 147488 | tf_op jit(solution)/shard_map/ppermute | solution.py:175
  30.7 3.3 %collective-permute-start.2 = (bf16[48,1536]{1,0:T(8,128)(2,1)S(1)}, bf16[48,1536]{1,0:T(8,128)(2,1)S(1)}, u32[]{:S(2)}, u32[]{:S(2)}) collective-permute-start(bf16[48,1536]{1,0:T(8,128)(2,1)S(1)} %collective-permute-done.1), channel_id=1, source_target_pairs={{32,8},{8,32},{40,16},{16,40},{48,24},{24,48},{56,0},{0,56},{33,9}... | collective-permute-start | bytes 442376 | tf_op jit(solution)/shard_map/ppermute | solution.py:153
  34.1 4.0 %collective-permute-done.2 = bf16[48,1536]{1,0:T(8,128)(2,1)S(1)} collective-permute-done((bf16[48,1536]{1,0:T(8,128)(2,1)S(1)}, bf16[48,1536]{1,0:T(8,128)(2,1)S(1)}, u32[]{:S(2)}, u32[]{:S(2)}) %collective-permute-start.2) | collective-permute-done | bytes 147488 | tf_op jit(solution)/shard_map/ppermute | solution.py:153
  38.1 3.1 %collective-permute-start.3 = (bf16[192,1536]{1,0:T(8,128)(2,1)S(1)}, bf16[192,1536]{1,0:T(8,128)(2,1)S(1)}, u32[]{:S(2)}, u32[]{:S(2)}) collective-permute-start(bf16[192,1536]{1,0:T(8,128)(2,1)S(1)} %constant_dynamic-update-slice_fusion.refs_0_), channel_id=1, source_target_pairs={{0,2},{2,4},{4,6},{6,0},{1,3},{3,5},{5,7},{7,1},{8,10},{10,12},{12... | collective-permute-start | bytes 1769480 | tf_op jit(solution)/shard_map/ppermute | solution.py:161
  41.3 3.4 %collective-permute-start.4 = (bf16[192,1536]{1,0:T(8,128)(2,1)S(1)}, bf16[192,1536]{1,0:T(8,128)(2,1)S(1)}, u32[]{:S(2)}, u32[]{:S(2)}) collective-permute-start(bf16[192,1536]{1,0:T(8,128)(2,1)S(1)} %constant_dynamic-update-slice_fusion.refs_0_), channel_id=1, source_target_pairs={{0,6},{2,0},{4,2},{6,4},{1,7},{3,1},{5,3},{7,5},{8,14},{10,8},{12,... | collective-permute-start | bytes 1769480 | tf_op jit(solution)/shard_map/ppermute | solution.py:162
  44.6 8.8 %collective-permute-done.3.refs_1_ = bf16[192,1536]{1,0:T(8,128)(2,1)S(1)} collective-permute-done((bf16[192,1536]{1,0:T(8,128)(2,1)S(1)}, bf16[192,1536]{1,0:T(8,128)(2,1)S(1)}, u32[]{:S(2)}, u32[]{:S(2)}) %collective-permute-start.3) | collective-permute-done | bytes 589856 | tf_op jit(solution)/shard_map/ppermute | solution.py:161
  53.5 0.7 slice.8
  54.2 1.9 %collective-permute-start.5 = (bf16[96,1536]{1,0:T(8,128)(2,1)}, bf16[96,1536]{1,0:T(8,128)(2,1)}, u32[]{:S(2)}, u32[]{:S(2)}) collective-permute-start(bf16[96,1536]{1,0:T(8,128)(2,1)} %slice.8), channel_id=1, source_target_pairs={{0,2},{2,4},{4,6},{6,0},{1,3},{3,5},{5,7},{7,1},{8,10},{10,12},{12... | collective-permute-start | bytes 884744 | tf_op jit(solution)/shard_map/ppermute | solution.py:164
  56.1 0.7 slice.9
  56.8 4.6 %collective-permute-start.6 = (bf16[96,1536]{1,0:T(8,128)(2,1)}, bf16[96,1536]{1,0:T(8,128)(2,1)}, u32[]{:S(2)}, u32[]{:S(2)}) collective-permute-start(bf16[96,1536]{1,0:T(8,128)(2,1)} %slice.9), channel_id=1, source_target_pairs={{0,6},{2,0},{4,2},{6,4},{1,7},{3,1},{5,3},{7,5},{8,14},{10,8},{12,... | collective-permute-start | bytes 884744 | tf_op jit(solution)/shard_map/ppermute | solution.py:164
  61.4 6.5 %attend.1 = bf16[16,144,128]{2,1,0:T(8,128)(2,1)} custom-call(s32[1]{0:T(128)S(6)} %copy.16.length_ref, bf16[16,3,128,128]{3,2,1,0:T(8,128)(2,1)S(1)} %all-to-all-done.x_ref), custom_call_target="tpu_custom_call" | custom-call | tf_op jit(solution)/shard_map/attend/pallas_call | solution.py:206
  68.0 6.1 %all-to-all-start.1 = ((bf16[16,144,128]{2,1,0:T(8,128)(2,1)}), bf16[16,144,128]{2,1,0:T(8,128)(2,1)S(1)}, u32[]{:S(2)}, u32[]{:S(2)}) async-start(bf16[16,144,128]{2,1,0:T(8,128)(2,1)} %attend.1), calls=%async_computation.1 | async-start | bytes 1179648 | tf_op jit(solution)/shard_map/all_to_all | solution.py:219
  74.1 6.6 %collective-permute-start.7 = (bf16[192,1536]{1,0:T(8,128)(2,1)S(1)}, bf16[192,1536]{1,0:T(8,128)(2,1)}, u32[]{:S(2)}, u32[]{:S(2)}) collective-permute-start(bf16[192,1536]{1,0:T(8,128)(2,1)S(1)} %constant_dynamic-update-slice_fusion.refs_0_), channel_id=1, source_target_pairs={{0,1},{1,0},{2,3},{3,2},{4,5},{5,4},{6,7},{7,6},{8,9},{9,8},{10,11... | collective-permute-start | bytes 1769480 | tf_op jit(solution)/shard_map/ppermute | solution.py:166
  80.7 1.9 %collective-permute-start.8 = (bf16[192,1536]{1,0:T(8,128)(2,1)S(1)}, bf16[192,1536]{1,0:T(8,128)(2,1)}, u32[]{:S(2)}, u32[]{:S(2)}) collective-permute-start(bf16[192,1536]{1,0:T(8,128)(2,1)S(1)} %collective-permute-done.3.refs_1_), channel_id=1, source_target_pairs={{0,1},{1,0},{2,3},{3,2},{4,5},{5,4},{6,7},{7,6},{8,9},{9,8},{10,11... | collective-permute-start | bytes 1769480 | tf_op jit(solution)/shard_map/ppermute | solution.py:166
  82.6 2.4 %collective-permute-start.9 = (bf16[192,1536]{1,0:T(8,128)(2,1)S(1)}, bf16[192,1536]{1,0:T(8,128)(2,1)}, u32[]{:S(2)}, u32[]{:S(2)}) collective-permute-start(bf16[192,1536]{1,0:T(8,128)(2,1)S(1)} %collective-permute-done.4.refs_2_), channel_id=1, source_target_pairs={{0,1},{1,0},{2,3},{3,2},{4,5},{5,4},{6,7},{7,6},{8,9},{9,8},{10,11... | collective-permute-start | bytes 1769480 | tf_op jit(solution)/shard_map/ppermute | solution.py:166
  85.0 1.0 %constant_dynamic-update-slice_fusion.5 = bf16[192,1536]{1,0:T(8,128)(2,1)S(1)} fusion(bf16[96,1536]{1,0:T(8,128)(2,1)} %collective-permute-done.5), kind=kLoop, calls=%fused_computation.5 | loop fusion | bytes 589824
  86.0 1.0 %constant_dynamic-update-slice_fusion.4.refs_3_ = bf16[192,1536]{1,0:T(8,128)(2,1)S(1)} fusion(bf16[192,1536]{1,0:T(8,128)(2,1)S(1)} %constant_dynamic-update-slice_fusion.5, bf16[96,1536]{1,0:T(8,128)(2,1)} %collective-permute-done.6), kind=kLoop, calls=%fused_computation.4 | loop fusion | bytes 589824 | tf_op jit(solution)/shard_map/concatenate | solution.py:165
  87.0 1.9 %collective-permute-start.10 = (bf16[192,1536]{1,0:T(8,128)(2,1)S(1)}, bf16[192,1536]{1,0:T(8,128)(2,1)}, u32[]{:S(2)}, u32[]{:S(2)}) collective-permute-start(bf16[192,1536]{1,0:T(8,128)(2,1)S(1)} %constant_dynamic-update-slice_fusion.4.refs_3_), channel_id=1, source_target_pairs={{0,1},{1,0},{2,3},{3,2},{4,5},{5,4},{6,7},{7,6},{8,9},{9,8},{10,11... | collective-permute-start | bytes 1769480 | tf_op jit(solution)/shard_map/ppermute | solution.py:166
  89.1 2.0 %collective-permute-done.10.refs_7_ = bf16[192,1536]{1,0:T(8,128)(2,1)} collective-permute-done((bf16[192,1536]{1,0:T(8,128)(2,1)S(1)}, bf16[192,1536]{1,0:T(8,128)(2,1)}, u32[]{:S(2)}, u32[]{:S(2)}) %collective-permute-start.10) | collective-permute-done | bytes 589856 | tf_op jit(solution)/shard_map/ppermute | solution.py:166
  91.1 3.9 %project.1 = (bf16[120,1536]{1,0:T(8,128)(2,1)}, bf16[8,1536]{1,0:T(8,128)(2,1)}, f32[12,1,120]{2,1,0:T(1,128)}, f32[8,12]{1,0:T(8,128)}, bf16[120,1536]{1,0:T(8,128)(2,1)}) custom-call(s32[4]{0:T(128)S(1)} %pad_add_fusion.spot_ref, bf16[16,144,128]{2,1,0:T(8,128)(2,1)S(1)} %all-to-all-done.1.x_ref, f32[1,1536]{1,0:T(1,128)S(1)} %copy-done, ...), custom_call_target="tpu_custom_call" | custom-call | tf_op jit(solution)/shard_map/project/pallas_call | solution.py:220
  (18 shorter events, 0.2 us)
Async XLA Ops:
  0.6 15.3 %collective-permute-start = (bf16[48,1536]{1,0:T(8,128)(2,1)}, bf16[48,1536]{1,0:T(8,128)(2,1)S(1)}, u32[]{:S(2)}, u32[]{:S(2)}) collective-permute-start(bf16[48,1536]{1,0:T(8,128)(2,1)} %param.13), channel_id=1, source_target_pairs={{32,8},{8,32},{40,16},{16,40},{48,24},{24,48},{56,0},{0,56},{33,9}... | collective-permute-start | bytes 442376 | tf_op jit(solution)/shard_map/ppermute | solution.py:153
  15.9 7.1 %copy-start.1 = (bf16[48,1536]{1,0:T(8,128)(2,1)S(1)}, bf16[48,1536]{1,0:T(8,128)(2,1)}, u32[]{:S(2)}) copy-start(bf16[48,1536]{1,0:T(8,128)(2,1)} %param.13) | copy-start | bytes 442372
  15.9 45.5 %all-to-all-start = ((bf16[16,3,128,128]{3,2,1,0:T(8,128)(2,1)}), bf16[16,3,128,128]{3,2,1,0:T(8,128)(2,1)S(1)}, u32[]{:S(2)}, u32[]{:S(2)}) async-start(bf16[16,3,128,128]{3,2,1,0:T(8,128)(2,1)} %pack.1), calls=%async_computation | async-start | bytes 3145728 | tf_op jit(solution)/shard_map/all_to_all | solution.py:205
  23.0 7.7 %collective-permute-start.1 = (bf16[48,1536]{1,0:T(8,128)(2,1)S(1)}, bf16[48,1536]{1,0:T(8,128)(2,1)S(1)}, u32[]{:S(2)}, u32[]{:S(2)}) collective-permute-start(bf16[48,1536]{1,0:T(8,128)(2,1)S(1)} %collective-permute-done), channel_id=1, source_target_pairs={{0,32},{32,0},{1,33},{33,1},{2,34},{34,2},{3,35},{35,3},{4,36},{36... | collective-permute-start | bytes 442376 | tf_op jit(solution)/shard_map/ppermute | solution.py:175
  30.7 7.4 %collective-permute-start.2 = (bf16[48,1536]{1,0:T(8,128)(2,1)S(1)}, bf16[48,1536]{1,0:T(8,128)(2,1)S(1)}, u32[]{:S(2)}, u32[]{:S(2)}) collective-permute-start(bf16[48,1536]{1,0:T(8,128)(2,1)S(1)} %collective-permute-done.1), channel_id=1, source_target_pairs={{32,8},{8,32},{40,16},{16,40},{48,24},{24,48},{56,0},{0,56},{33,9}... | collective-permute-start | bytes 442376 | tf_op jit(solution)/shard_map/ppermute | solution.py:153
  38.1 15.3 %collective-permute-start.3 = (bf16[192,1536]{1,0:T(8,128)(2,1)S(1)}, bf16[192,1536]{1,0:T(8,128)(2,1)S(1)}, u32[]{:S(2)}, u32[]{:S(2)}) collective-permute-start(bf16[192,1536]{1,0:T(8,128)(2,1)S(1)} %constant_dynamic-update-slice_fusion.refs_0_), channel_id=1, source_target_pairs={{0,2},{2,4},{4,6},{6,0},{1,3},{3,5},{5,7},{7,1},{8,10},{10,12},{12... | collective-permute-start | bytes 1769480 | tf_op jit(solution)/shard_map/ppermute | solution.py:161
  41.3 14.8 %collective-permute-start.4 = (bf16[192,1536]{1,0:T(8,128)(2,1)S(1)}, bf16[192,1536]{1,0:T(8,128)(2,1)S(1)}, u32[]{:S(2)}, u32[]{:S(2)}) collective-permute-start(bf16[192,1536]{1,0:T(8,128)(2,1)S(1)} %constant_dynamic-update-slice_fusion.refs_0_), channel_id=1, source_target_pairs={{0,6},{2,0},{4,2},{6,4},{1,7},{3,1},{5,3},{7,5},{8,14},{10,8},{12,... | collective-permute-start | bytes 1769480 | tf_op jit(solution)/shard_map/ppermute | solution.py:162
  54.2 30.9 %collective-permute-start.5 = (bf16[96,1536]{1,0:T(8,128)(2,1)}, bf16[96,1536]{1,0:T(8,128)(2,1)}, u32[]{:S(2)}, u32[]{:S(2)}) collective-permute-start(bf16[96,1536]{1,0:T(8,128)(2,1)} %slice.8), channel_id=1, source_target_pairs={{0,2},{2,4},{4,6},{6,0},{1,3},{3,5},{5,7},{7,1},{8,10},{10,12},{12... | collective-permute-start | bytes 884744 | tf_op jit(solution)/shard_map/ppermute | solution.py:164
  56.8 29.2 %collective-permute-start.6 = (bf16[96,1536]{1,0:T(8,128)(2,1)}, bf16[96,1536]{1,0:T(8,128)(2,1)}, u32[]{:S(2)}, u32[]{:S(2)}) collective-permute-start(bf16[96,1536]{1,0:T(8,128)(2,1)} %slice.9), channel_id=1, source_target_pairs={{0,6},{2,0},{4,2},{6,4},{1,7},{3,1},{5,3},{7,5},{8,14},{10,8},{12,... | collective-permute-start | bytes 884744 | tf_op jit(solution)/shard_map/ppermute | solution.py:164
  68.0 23.1 %copy-start = (f32[1,1536]{1,0:T(1,128)S(1)}, f32[1,1536]{1,0:T(1,128)}, u32[]{:S(2)}) copy-start(f32[1,1536]{1,0:T(1,128)} %gate_ref.1) | copy-start | bytes 18436
  68.0 23.1 %all-to-all-start.1 = ((bf16[16,144,128]{2,1,0:T(8,128)(2,1)}), bf16[16,144,128]{2,1,0:T(8,128)(2,1)S(1)}, u32[]{:S(2)}, u32[]{:S(2)}) async-start(bf16[16,144,128]{2,1,0:T(8,128)(2,1)} %attend.1), calls=%async_computation.1 | async-start | bytes 1179648 | tf_op jit(solution)/shard_map/all_to_all | solution.py:219
  74.1 15.0 %collective-permute-start.7 = (bf16[192,1536]{1,0:T(8,128)(2,1)S(1)}, bf16[192,1536]{1,0:T(8,128)(2,1)}, u32[]{:S(2)}, u32[]{:S(2)}) collective-permute-start(bf16[192,1536]{1,0:T(8,128)(2,1)S(1)} %constant_dynamic-update-slice_fusion.refs_0_), channel_id=1, source_target_pairs={{0,1},{1,0},{2,3},{3,2},{4,5},{5,4},{6,7},{7,6},{8,9},{9,8},{10,11... | collective-permute-start | bytes 1769480 | tf_op jit(solution)/shard_map/ppermute | solution.py:166
  80.7 8.4 %collective-permute-start.8 = (bf16[192,1536]{1,0:T(8,128)(2,1)S(1)}, bf16[192,1536]{1,0:T(8,128)(2,1)}, u32[]{:S(2)}, u32[]{:S(2)}) collective-permute-start(bf16[192,1536]{1,0:T(8,128)(2,1)S(1)} %collective-permute-done.3.refs_1_), channel_id=1, source_target_pairs={{0,1},{1,0},{2,3},{3,2},{4,5},{5,4},{6,7},{7,6},{8,9},{9,8},{10,11... | collective-permute-start | bytes 1769480 | tf_op jit(solution)/shard_map/ppermute | solution.py:166
  82.6 6.4 %collective-permute-start.9 = (bf16[192,1536]{1,0:T(8,128)(2,1)S(1)}, bf16[192,1536]{1,0:T(8,128)(2,1)}, u32[]{:S(2)}, u32[]{:S(2)}) collective-permute-start(bf16[192,1536]{1,0:T(8,128)(2,1)S(1)} %collective-permute-done.4.refs_2_), channel_id=1, source_target_pairs={{0,1},{1,0},{2,3},{3,2},{4,5},{5,4},{6,7},{7,6},{8,9},{9,8},{10,11... | collective-permute-start | bytes 1769480 | tf_op jit(solution)/shard_map/ppermute | solution.py:166
  87.0 4.0 %collective-permute-start.10 = (bf16[192,1536]{1,0:T(8,128)(2,1)S(1)}, bf16[192,1536]{1,0:T(8,128)(2,1)}, u32[]{:S(2)}, u32[]{:S(2)}) collective-permute-start(bf16[192,1536]{1,0:T(8,128)(2,1)S(1)} %constant_dynamic-update-slice_fusion.4.refs_3_), channel_id=1, source_target_pairs={{0,1},{1,0},{2,3},{3,2},{4,5},{5,4},{6,7},{7,6},{8,9},{9,8},{10,11... | collective-permute-start | bytes 1769480 | tf_op jit(solution)/shard_map/ppermute | solution.py:166

commit v9 on v8

--- a/solution.py
+++ b/solution.py
@@ -18,6 +18,7 @@
 SEQ = ("y", "zl")
 FSDP = ("zh", "x", "core")
 GROUP = 4
+WIDTH = 512
 VMEM = pltpu.VMEM
 
 
@@ -102,8 +103,14 @@
 
 
 def project_kernel(spot_ref, x_ref, gate_ref, *refs):
-    pieces = refs[:8]
-    av_ref, at_ref, lv_ref, lt_ref, pv_ref, turned_ref, mixed_ref = refs[8:]
+    pieces, swapped = refs[:4], refs[4:8]
+    av_ref, at_ref, lv_ref, lt_ref, pv_ref = refs[8:13]
+    turned_ref, mixed_ref, held_ref, total_ref, sems = refs[13:]
+    copies = [
+        pltpu.make_async_copy(piece, held_ref.at[i], sems.at[i]) for i, piece in enumerate(swapped)
+    ]
+    for copy in copies:
+        copy.start()
     vid = av_ref.shape[0]
     rows = vid + at_ref.shape[0]
     lses = []
@@ -126,21 +133,35 @@
     of_x = (x, x + nx - 1, x + 1, x + nx // 2)
     depth = pieces[0].shape[0]
     count = depth // nz
-    for i in range(len(pieces)):
+    for i in range(len(pieces) + len(swapped)):
         for j in range(nz):
             row = (of_z[j] + nz) % nz * nx + of_x[i % nx] % nx
             row = (row * SIZES["core"] + (core ^ (i // nx))) * count
             source = pl.ds(pl.multiple_of(row, 16), count)
             mixed_ref[pl.ds(i * depth + j * count, count), :] = turned_ref[source, :]
     mixed = mixed_ref[...].astype(jnp.float32).T[:vid].astype(jnp.bfloat16)
-    width = 512
-    for first in range(0, pv_ref.shape[1], width):
-        here = pl.ds(first, width)
-        out = jnp.zeros((vid, width), jnp.float32)
-        for i, piece in enumerate(pieces):
-            out += jnp.dot(
+    starts = range(0, pv_ref.shape[1], WIDTH)
+    for first in starts:
+        here = pl.ds(first, WIDTH)
+        total_ref[:, here] = sum(
+            jnp.dot(
                 mixed[:, i * depth : (i + 1) * depth], piece[:, here], preferred_element_type=jnp.float32
             )
+            for i, piece in enumerate(pieces)
+        )
+    for copy in copies:
+        copy.wait()
+    rest = mixed[:, len(pieces) * depth :]
+    for first in starts:
+        here = pl.ds(first, WIDTH)
+        out = total_ref[:, here] + sum(
+            jnp.dot(
+                rest[:, i * depth : (i + 1) * depth],
+                held_ref[i, :, here],
+                preferred_element_type=jnp.float32,
+            )
+            for i in range(len(swapped))
+        )
         pv_ref[:, here] = (out * gate_ref[:, here]).astype(jnp.bfloat16)
 
 
@@ -226,9 +247,15 @@
             jax.ShapeDtypeStruct((txt, HEADS), jnp.float32),
             jax.ShapeDtypeStruct((vid, feats), jnp.bfloat16),
         ),
-        in_specs=[smem, *[vmem] * (2 + len(pieces))],
+        in_specs=[smem, *[vmem] * 6, *[anywhere] * 4],
         out_specs=(vmem,) * 5,
-        scratch_shapes=[VMEM((feats, rows), jnp.bfloat16)] * 2,
+        scratch_shapes=[
+            VMEM((feats, rows), jnp.bfloat16),
+            VMEM((feats, rows), jnp.bfloat16),
+            VMEM((4, *pieces[0].shape), jnp.bfloat16),
+            VMEM((vid, feats), jnp.float32),
+            pltpu.SemaphoreType.DMA((4,)),
+        ],
         compiler_params=pltpu.CompilerParams(vmem_limit_bytes=16 << 20),
         name="project",
     )(spot.astype(jnp.int32), back, gate, *pieces)

time: 95.7 us -> 96 us (level)
  no operation moved by 1% of the time
where the time goes in v9:
time: 96 us; the launch traced here: 95.3 us
  starting transfers between devices  57.1 us (59%)
  waiting for transfers between devices  19.3 us (20%)
  Pallas kernels  13.9 us (14%)
  local copies, waits for them, and re-layouts  3.49 us (4%)
  between operations  1.5 us (2%)
    ppermute x2, starting transfers between devices, across(): return lax.ppermute(block, ('zl', 'zh'), between)  14.8 us
    ppermute x4, starting transfers between devices, gathered(): lax.ppermute(part, 'core', [(0, 1), (1, 0)])  12.9 us
    ppermute x1, waiting for transfers between devices, gathered(): left = lax.ppermute(column, 'x', up)  8.81 us
    all_to_all x1, starting transfers between devices, shards(): moved = lax.all_to_all(packed, SEQ, 0, 0, tiled=True)  7.06 us
    pallas_call x1, Pallas kernels, shards(): pl.pallas_call(functools.partial(attend_kernel, vid), out_shape=jax.Shape...  6.55 us
    all_to_all x1, starting transfers between devices, shards(): back = lax.all_to_all(mixed, SEQ, 0, 0, tiled=True)  6.07 us
    ppermute x1, starting transfers between devices, gathered(): lax.ppermute(right[half:], 'x', down)  4.56 us
    ppermute x1, waiting for transfers between devices, shards(): second = lax.ppermute(first, 'zl', [(0, 1), (1, 0)])  4.44 us
  transfers between devices with their start and end apart: 13, of which 4 were waited for; matrix products, arithmetic and copies ran while one was open for 4% of the time, Pallas kernels for 10%

profile of v9, /device:TPU:1, one launch (start us, length us, event | category | flops | bytes accessed | tf_op | source)
XLA Modules:
  0.0 95.3 jit_solution(12831875888198373518)
XLA Ops:
  0.6 11.5 %collective-permute-start = (bf16[48,1536]{1,0:T(8,128)(2,1)}, bf16[48,1536]{1,0:T(8,128)(2,1)S(1)}, u32[]{:S(2)}, u32[]{:S(2)}) collective-permute-start(bf16[48,1536]{1,0:T(8,128)(2,1)} %param.13), channel_id=1, source_target_pairs={{32,8},{8,32},{40,16},{16,40},{48,24},{24,48},{56,0},{0,56},{33,9}... | collective-permute-start | bytes 442376 | tf_op jit(solution)/shard_map/ppermute | solution.py:174
  12.8 3.1 %pack.1 = bf16[16,3,128,128]{3,2,1,0:T(8,128)(2,1)} custom-call(s32[1]{0:T(128)S(6)} %copy.16.length_ref, s32[1]{0:T(128)} %bitcast.4.base_ref, bf16[120,1536]{1,0:T(8,128)(2,1)} %bitcast.17, bf16[120,2,1536]{2,1,0:T(2,128)(2,1)} %bitcast.16, bf16[8,1536]{1,0:T(8,128)(2,1)} %bitcast.19, bf16[8,2,1536]{2,1,0:T(2,128)(2,1)} %bitcast.18), custom_call_target="tpu_custom_call" | custom-call | tf_op jit(solution)/shard_map/pack/pallas_call | solution.py:202
  15.9 7.1 %all-to-all-start = ((bf16[16,3,128,128]{3,2,1,0:T(8,128)(2,1)}), bf16[16,3,128,128]{3,2,1,0:T(8,128)(2,1)S(1)}, u32[]{:S(2)}, u32[]{:S(2)}) async-start(bf16[16,3,128,128]{3,2,1,0:T(8,128)(2,1)} %pack.1), calls=%async_computation | async-start | bytes 3145728 | tf_op jit(solution)/shard_map/all_to_all | solution.py:226
  23.0 3.3 %collective-permute-start.1 = (bf16[48,1536]{1,0:T(8,128)(2,1)S(1)}, bf16[48,1536]{1,0:T(8,128)(2,1)S(1)}, u32[]{:S(2)}, u32[]{:S(2)}) collective-permute-start(bf16[48,1536]{1,0:T(8,128)(2,1)S(1)} %collective-permute-done), channel_id=1, source_target_pairs={{0,32},{32,0},{1,33},{33,1},{2,34},{34,2},{3,35},{35,3},{4,36},{36... | collective-permute-start | bytes 442376 | tf_op jit(solution)/shard_map/ppermute | solution.py:196
  26.3 4.4 %collective-permute-done.1 = bf16[48,1536]{1,0:T(8,128)(2,1)S(1)} collective-permute-done((bf16[48,1536]{1,0:T(8,128)(2,1)S(1)}, bf16[48,1536]{1,0:T(8,128)(2,1)S(1)}, u32[]{:S(2)}, u32[]{:S(2)}) %collective-permute-start.1) | collective-permute-done | bytes 147488 | tf_op jit(solution)/shard_map/ppermute | solution.py:196
  30.7 3.3 %collective-permute-start.2 = (bf16[48,1536]{1,0:T(8,128)(2,1)S(1)}, bf16[48,1536]{1,0:T(8,128)(2,1)S(1)}, u32[]{:S(2)}, u32[]{:S(2)}) collective-permute-start(bf16[48,1536]{1,0:T(8,128)(2,1)S(1)} %collective-permute-done.1), channel_id=1, source_target_pairs={{32,8},{8,32},{40,16},{16,40},{48,24},{24,48},{56,0},{0,56},{33,9}... | collective-permute-start | bytes 442376 | tf_op jit(solution)/shard_map/ppermute | solution.py:174
  34.1 4.0 %collective-permute-done.2 = bf16[48,1536]{1,0:T(8,128)(2,1)S(1)} collective-permute-done((bf16[48,1536]{1,0:T(8,128)(2,1)S(1)}, bf16[48,1536]{1,0:T(8,128)(2,1)S(1)}, u32[]{:S(2)}, u32[]{:S(2)}) %collective-permute-start.2) | collective-permute-done | bytes 147488 | tf_op jit(solution)/shard_map/ppermute | solution.py:174
  38.1 3.1 %collective-permute-start.3 = (bf16[192,1536]{1,0:T(8,128)(2,1)S(1)}, bf16[192,1536]{1,0:T(8,128)(2,1)S(1)}, u32[]{:S(2)}, u32[]{:S(2)}) collective-permute-start(bf16[192,1536]{1,0:T(8,128)(2,1)S(1)} %constant_dynamic-update-slice_fusion.refs_0_), channel_id=1, source_target_pairs={{0,2},{2,4},{4,6},{6,0},{1,3},{3,5},{5,7},{7,1},{8,10},{10,12},{12... | collective-permute-start | bytes 1769480 | tf_op jit(solution)/shard_map/ppermute | solution.py:182
  41.3 3.4 %collective-permute-start.4 = (bf16[192,1536]{1,0:T(8,128)(2,1)S(1)}, bf16[192,1536]{1,0:T(8,128)(2,1)S(1)}, u32[]{:S(2)}, u32[]{:S(2)}) collective-permute-start(bf16[192,1536]{1,0:T(8,128)(2,1)S(1)} %constant_dynamic-update-slice_fusion.refs_0_), channel_id=1, source_target_pairs={{0,6},{2,0},{4,2},{6,4},{1,7},{3,1},{5,3},{7,5},{8,14},{10,8},{12,... | collective-permute-start | bytes 1769480 | tf_op jit(solution)/shard_map/ppermute | solution.py:183
  44.6 8.8 %collective-permute-done.3.refs_1_ = bf16[192,1536]{1,0:T(8,128)(2,1)S(1)} collective-permute-done((bf16[192,1536]{1,0:T(8,128)(2,1)S(1)}, bf16[192,1536]{1,0:T(8,128)(2,1)S(1)}, u32[]{:S(2)}, u32[]{:S(2)}) %collective-permute-start.3) | collective-permute-done | bytes 589856 | tf_op jit(solution)/shard_map/ppermute | solution.py:182
  53.5 0.7 slice.8
  54.2 1.9 %collective-permute-start.5 = (bf16[96,1536]{1,0:T(8,128)(2,1)}, bf16[96,1536]{1,0:T(8,128)(2,1)}, u32[]{:S(2)}, u32[]{:S(2)}) collective-permute-start(bf16[96,1536]{1,0:T(8,128)(2,1)} %slice.8), channel_id=1, source_target_pairs={{0,2},{2,4},{4,6},{6,0},{1,3},{3,5},{5,7},{7,1},{8,10},{10,12},{12... | collective-permute-start | bytes 884744 | tf_op jit(solution)/shard_map/ppermute | solution.py:185
  56.1 0.7 slice.9
  56.8 4.6 %collective-permute-start.6 = (bf16[96,1536]{1,0:T(8,128)(2,1)}, bf16[96,1536]{1,0:T(8,128)(2,1)}, u32[]{:S(2)}, u32[]{:S(2)}) collective-permute-start(bf16[96,1536]{1,0:T(8,128)(2,1)} %slice.9), channel_id=1, source_target_pairs={{0,6},{2,0},{4,2},{6,4},{1,7},{3,1},{5,3},{7,5},{8,14},{10,8},{12,... | collective-permute-start | bytes 884744 | tf_op jit(solution)/shard_map/ppermute | solution.py:185
  61.4 6.5 %attend.1 = bf16[16,144,128]{2,1,0:T(8,128)(2,1)} custom-call(s32[1]{0:T(128)S(6)} %copy.16.length_ref, bf16[16,3,128,128]{3,2,1,0:T(8,128)(2,1)S(1)} %all-to-all-done.x_ref), custom_call_target="tpu_custom_call" | custom-call | tf_op jit(solution)/shard_map/attend/pallas_call | solution.py:227
  68.0 6.1 %all-to-all-start.1 = ((bf16[16,144,128]{2,1,0:T(8,128)(2,1)}), bf16[16,144,128]{2,1,0:T(8,128)(2,1)S(1)}, u32[]{:S(2)}, u32[]{:S(2)}) async-start(bf16[16,144,128]{2,1,0:T(8,128)(2,1)} %attend.1), calls=%async_computation.1 | async-start | bytes 1179648 | tf_op jit(solution)/shard_map/all_to_all | solution.py:240
  74.1 6.6 %collective-permute-start.7 = (bf16[192,1536]{1,0:T(8,128)(2,1)S(1)}, bf16[192,1536]{1,0:T(8,128)(2,1)}, u32[]{:S(2)}, u32[]{:S(2)}) collective-permute-start(bf16[192,1536]{1,0:T(8,128)(2,1)S(1)} %constant_dynamic-update-slice_fusion.refs_0_), channel_id=1, source_target_pairs={{0,1},{1,0},{2,3},{3,2},{4,5},{5,4},{6,7},{7,6},{8,9},{9,8},{10,11... | collective-permute-start | bytes 1769480 | tf_op jit(solution)/shard_map/ppermute | solution.py:187
  80.7 1.9 %collective-permute-start.8 = (bf16[192,1536]{1,0:T(8,128)(2,1)S(1)}, bf16[192,1536]{1,0:T(8,128)(2,1)}, u32[]{:S(2)}, u32[]{:S(2)}) collective-permute-start(bf16[192,1536]{1,0:T(8,128)(2,1)S(1)} %collective-permute-done.3.refs_1_), channel_id=1, source_target_pairs={{0,1},{1,0},{2,3},{3,2},{4,5},{5,4},{6,7},{7,6},{8,9},{9,8},{10,11... | collective-permute-start | bytes 1769480 | tf_op jit(solution)/shard_map/ppermute | solution.py:187
  82.6 2.4 %collective-permute-start.9 = (bf16[192,1536]{1,0:T(8,128)(2,1)S(1)}, bf16[192,1536]{1,0:T(8,128)(2,1)}, u32[]{:S(2)}, u32[]{:S(2)}) collective-permute-start(bf16[192,1536]{1,0:T(8,128)(2,1)S(1)} %collective-permute-done.4.refs_2_), channel_id=1, source_target_pairs={{0,1},{1,0},{2,3},{3,2},{4,5},{5,4},{6,7},{7,6},{8,9},{9,8},{10,11... | collective-permute-start | bytes 1769480 | tf_op jit(solution)/shard_map/ppermute | solution.py:187
  85.0 1.0 %constant_dynamic-update-slice_fusion.5 = bf16[192,1536]{1,0:T(8,128)(2,1)S(1)} fusion(bf16[96,1536]{1,0:T(8,128)(2,1)} %collective-permute-done.5), kind=kLoop, calls=%fused_computation.5 | loop fusion | bytes 589824
  86.0 1.0 %constant_dynamic-update-slice_fusion.4.refs_3_ = bf16[192,1536]{1,0:T(8,128)(2,1)S(1)} fusion(bf16[192,1536]{1,0:T(8,128)(2,1)S(1)} %constant_dynamic-update-slice_fusion.5, bf16[96,1536]{1,0:T(8,128)(2,1)} %collective-permute-done.6), kind=kLoop, calls=%fused_computation.4 | loop fusion | bytes 589824 | tf_op jit(solution)/shard_map/concatenate | solution.py:186
  87.0 1.9 %collective-permute-start.10 = (bf16[192,1536]{1,0:T(8,128)(2,1)S(1)}, bf16[192,1536]{1,0:T(8,128)(2,1)}, u32[]{:S(2)}, u32[]{:S(2)}) collective-permute-start(bf16[192,1536]{1,0:T(8,128)(2,1)S(1)} %constant_dynamic-update-slice_fusion.4.refs_3_), channel_id=1, source_target_pairs={{0,1},{1,0},{2,3},{3,2},{4,5},{5,4},{6,7},{7,6},{8,9},{9,8},{10,11... | collective-permute-start | bytes 1769480 | tf_op jit(solution)/shard_map/ppermute | solution.py:187
  89.1 2.0 %collective-permute-done.10.refs_7_ = bf16[192,1536]{1,0:T(8,128)(2,1)} collective-permute-done((bf16[192,1536]{1,0:T(8,128)(2,1)S(1)}, bf16[192,1536]{1,0:T(8,128)(2,1)}, u32[]{:S(2)}, u32[]{:S(2)}) %collective-permute-start.10) | collective-permute-done | bytes 589856 | tf_op jit(solution)/shard_map/ppermute | solution.py:187
  91.1 4.3 %project.1 = (bf16[120,1536]{1,0:T(8,128)(2,1)}, bf16[8,1536]{1,0:T(8,128)(2,1)}, f32[12,1,120]{2,1,0:T(1,128)}, f32[8,12]{1,0:T(8,128)}, bf16[120,1536]{1,0:T(8,128)(2,1)}) custom-call(s32[4]{0:T(128)S(1)} %pad_add_fusion.spot_ref, bf16[16,144,128]{2,1,0:T(8,128)(2,1)S(1)} %all-to-all-done.1.x_ref, f32[1,1536]{1,0:T(1,128)S(1)} %copy-done, ...), custom_call_target="tpu_custom_call" | custom-call | tf_op jit(solution)/shard_map/project/pallas_call | solution.py:241
  (18 shorter events, 0.2 us)
Async XLA Ops:
  0.6 15.3 %collective-permute-start = (bf16[48,1536]{1,0:T(8,128)(2,1)}, bf16[48,1536]{1,0:T(8,128)(2,1)S(1)}, u32[]{:S(2)}, u32[]{:S(2)}) collective-permute-start(bf16[48,1536]{1,0:T(8,128)(2,1)} %param.13), channel_id=1, source_target_pairs={{32,8},{8,32},{40,16},{16,40},{48,24},{24,48},{56,0},{0,56},{33,9}... | collective-permute-start | bytes 442376 | tf_op jit(solution)/shard_map/ppermute | solution.py:174
  15.9 7.1 %copy-start.1 = (bf16[48,1536]{1,0:T(8,128)(2,1)S(1)}, bf16[48,1536]{1,0:T(8,128)(2,1)}, u32[]{:S(2)}) copy-start(bf16[48,1536]{1,0:T(8,128)(2,1)} %param.13) | copy-start | bytes 442372
  15.9 45.5 %all-to-all-start = ((bf16[16,3,128,128]{3,2,1,0:T(8,128)(2,1)}), bf16[16,3,128,128]{3,2,1,0:T(8,128)(2,1)S(1)}, u32[]{:S(2)}, u32[]{:S(2)}) async-start(bf16[16,3,128,128]{3,2,1,0:T(8,128)(2,1)} %pack.1), calls=%async_computation | async-start | bytes 3145728 | tf_op jit(solution)/shard_map/all_to_all | solution.py:226
  23.0 7.7 %collective-permute-start.1 = (bf16[48,1536]{1,0:T(8,128)(2,1)S(1)}, bf16[48,1536]{1,0:T(8,128)(2,1)S(1)}, u32[]{:S(2)}, u32[]{:S(2)}) collective-permute-start(bf16[48,1536]{1,0:T(8,128)(2,1)S(1)} %collective-permute-done), channel_id=1, source_target_pairs={{0,32},{32,0},{1,33},{33,1},{2,34},{34,2},{3,35},{35,3},{4,36},{36... | collective-permute-start | bytes 442376 | tf_op jit(solution)/shard_map/ppermute | solution.py:196
  30.7 7.4 %collective-permute-start.2 = (bf16[48,1536]{1,0:T(8,128)(2,1)S(1)}, bf16[48,1536]{1,0:T(8,128)(2,1)S(1)}, u32[]{:S(2)}, u32[]{:S(2)}) collective-permute-start(bf16[48,1536]{1,0:T(8,128)(2,1)S(1)} %collective-permute-done.1), channel_id=1, source_target_pairs={{32,8},{8,32},{40,16},{16,40},{48,24},{24,48},{56,0},{0,56},{33,9}... | collective-permute-start | bytes 442376 | tf_op jit(solution)/shard_map/ppermute | solution.py:174
  38.1 15.3 %collective-permute-start.3 = (bf16[192,1536]{1,0:T(8,128)(2,1)S(1)}, bf16[192,1536]{1,0:T(8,128)(2,1)S(1)}, u32[]{:S(2)}, u32[]{:S(2)}) collective-permute-start(bf16[192,1536]{1,0:T(8,128)(2,1)S(1)} %constant_dynamic-update-slice_fusion.refs_0_), channel_id=1, source_target_pairs={{0,2},{2,4},{4,6},{6,0},{1,3},{3,5},{5,7},{7,1},{8,10},{10,12},{12... | collective-permute-start | bytes 1769480 | tf_op jit(solution)/shard_map/ppermute | solution.py:182
  41.3 14.8 %collective-permute-start.4 = (bf16[192,1536]{1,0:T(8,128)(2,1)S(1)}, bf16[192,1536]{1,0:T(8,128)(2,1)S(1)}, u32[]{:S(2)}, u32[]{:S(2)}) collective-permute-start(bf16[192,1536]{1,0:T(8,128)(2,1)S(1)} %constant_dynamic-update-slice_fusion.refs_0_), channel_id=1, source_target_pairs={{0,6},{2,0},{4,2},{6,4},{1,7},{3,1},{5,3},{7,5},{8,14},{10,8},{12,... | collective-permute-start | bytes 1769480 | tf_op jit(solution)/shard_map/ppermute | solution.py:183
  54.2 30.9 %collective-permute-start.5 = (bf16[96,1536]{1,0:T(8,128)(2,1)}, bf16[96,1536]{1,0:T(8,128)(2,1)}, u32[]{:S(2)}, u32[]{:S(2)}) collective-permute-start(bf16[96,1536]{1,0:T(8,128)(2,1)} %slice.8), channel_id=1, source_target_pairs={{0,2},{2,4},{4,6},{6,0},{1,3},{3,5},{5,7},{7,1},{8,10},{10,12},{12... | collective-permute-start | bytes 884744 | tf_op jit(solution)/shard_map/ppermute | solution.py:185
  56.8 29.2 %collective-permute-start.6 = (bf16[96,1536]{1,0:T(8,128)(2,1)}, bf16[96,1536]{1,0:T(8,128)(2,1)}, u32[]{:S(2)}, u32[]{:S(2)}) collective-permute-start(bf16[96,1536]{1,0:T(8,128)(2,1)} %slice.9), channel_id=1, source_target_pairs={{0,6},{2,0},{4,2},{6,4},{1,7},{3,1},{5,3},{7,5},{8,14},{10,8},{12,... | collective-permute-start | bytes 884744 | tf_op jit(solution)/shard_map/ppermute | solution.py:185
  68.0 23.1 %copy-start = (f32[1,1536]{1,0:T(1,128)S(1)}, f32[1,1536]{1,0:T(1,128)}, u32[]{:S(2)}) copy-start(f32[1,1536]{1,0:T(1,128)} %gate_ref.1) | copy-start | bytes 18436
  68.0 23.1 %all-to-all-start.1 = ((bf16[16,144,128]{2,1,0:T(8,128)(2,1)}), bf16[16,144,128]{2,1,0:T(8,128)(2,1)S(1)}, u32[]{:S(2)}, u32[]{:S(2)}) async-start(bf16[16,144,128]{2,1,0:T(8,128)(2,1)} %attend.1), calls=%async_computation.1 | async-start | bytes 1179648 | tf_op jit(solution)/shard_map/all_to_all | solution.py:240
  74.1 15.0 %collective-permute-start.7 = (bf16[192,1536]{1,0:T(8,128)(2,1)S(1)}, bf16[192,1536]{1,0:T(8,128)(2,1)}, u32[]{:S(2)}, u32[]{:S(2)}) collective-permute-start(bf16[192,1536]{1,0:T(8,128)(2,1)S(1)} %constant_dynamic-update-slice_fusion.refs_0_), channel_id=1, source_target_pairs={{0,1},{1,0},{2,3},{3,2},{4,5},{5,4},{6,7},{7,6},{8,9},{9,8},{10,11... | collective-permute-start | bytes 1769480 | tf_op jit(solution)/shard_map/ppermute | solution.py:187
  80.7 8.4 %collective-permute-start.8 = (bf16[192,1536]{1,0:T(8,128)(2,1)S(1)}, bf16[192,1536]{1,0:T(8,128)(2,1)}, u32[]{:S(2)}, u32[]{:S(2)}) collective-permute-start(bf16[192,1536]{1,0:T(8,128)(2,1)S(1)} %collective-permute-done.3.refs_1_), channel_id=1, source_target_pairs={{0,1},{1,0},{2,3},{3,2},{4,5},{5,4},{6,7},{7,6},{8,9},{9,8},{10,11... | collective-permute-start | bytes 1769480 | tf_op jit(solution)/shard_map/ppermute | solution.py:187
  82.6 6.4 %collective-permute-start.9 = (bf16[192,1536]{1,0:T(8,128)(2,1)S(1)}, bf16[192,1536]{1,0:T(8,128)(2,1)}, u32[]{:S(2)}, u32[]{:S(2)}) collective-permute-start(bf16[192,1536]{1,0:T(8,128)(2,1)S(1)} %collective-permute-done.4.refs_2_), channel_id=1, source_target_pairs={{0,1},{1,0},{2,3},{3,2},{4,5},{5,4},{6,7},{7,6},{8,9},{9,8},{10,11... | collective-permute-start | bytes 1769480 | tf_op jit(solution)/shard_map/ppermute | solution.py:187
  87.0 4.0 %collective-permute-start.10 = (bf16[192,1536]{1,0:T(8,128)(2,1)S(1)}, bf16[192,1536]{1,0:T(8,128)(2,1)}, u32[]{:S(2)}, u32[]{:S(2)}) collective-permute-start(bf16[192,1536]{1,0:T(8,128)(2,1)S(1)} %constant_dynamic-update-slice_fusion.4.refs_3_), channel_id=1, source_target_pairs={{0,1},{1,0},{2,3},{3,2},{4,5},{5,4},{6,7},{7,6},{8,9},{9,8},{10,11... | collective-permute-start | bytes 1769480 | tf_op jit(solution)/shard_map/ppermute | solution.py:187

commit v10 on v8

--- a/solution.py
+++ b/solution.py
@@ -160,10 +160,13 @@
     down = [(i, (i - 1) % nx) for i in range(nx)]
     left = lax.ppermute(column, "x", up)
     right = lax.ppermute(column, "x", down)
+    partner = [(0, 1), (1, 0)]
+    other = lax.ppermute(column, "core", partner)
+    right, other = lax.optimization_barrier((right, other))
     half = column.shape[0] // 2
     far = [lax.ppermute(left[:half], "x", up), lax.ppermute(right[half:], "x", down)]
-    mine = [column, left, right, jnp.concatenate(far, axis=0)]
-    return mine + [lax.ppermute(part, "core", [(0, 1), (1, 0)]) for part in mine]
+    mine = [left, right, jnp.concatenate(far, axis=0)]
+    return [column, *mine, other, *(lax.ppermute(part, "core", partner) for part in mine)]
 
 
 def shards(sources, q_video, kv_video, q_text, kv_text, text_lengths, gate, w_out):

time: 95.7 us -> 96.8 us (1.011)
  the two profiles are of different devices: /device:TPU:1 before, /device:TPU:8 now
where the time goes in v10:
time: 96.8 us; the launch traced here: 96 us
  starting transfers between devices  57 us (59%)
  waiting for transfers between devices  19.4 us (20%)
  Pallas kernels  13.3 us (14%)
  local copies, waits for them, and re-layouts  4.77 us (5%)
  between operations  1.49 us (2%)
    ppermute x2, starting transfers between devices, across(): return lax.ppermute(block, ('zl', 'zh'), between)  16.4 us
    all_to_all x1, starting transfers between devices, shards(): moved = lax.all_to_all(packed, SEQ, 0, 0, tiled=True)  7.56 us
    all_to_all x1, starting transfers between devices, shards(): back = lax.all_to_all(mixed, SEQ, 0, 0, tiled=True)  7.36 us
    ppermute x1, waiting for transfers between devices, gathered(): left = lax.ppermute(column, 'x', up)  6.96 us
    pallas_call x1, Pallas kernels, shards(): pl.pallas_call(functools.partial(attend_kernel, vid), out_shape=jax.Shape...  6.53 us
    ppermute x3, starting transfers between devices, gathered(): lax.ppermute(part, 'core', partner)  6.24 us
    ppermute x1, starting transfers between devices, gathered(): lax.ppermute(right[half:], 'x', down)  4.85 us
    ppermute x1, waiting for transfers between devices, shards(): second = lax.ppermute(first, 'zl', [(0, 1), (1, 0)])  4 us
  transfers between devices with their start and end apart: 13, of which 6 were waited for; matrix products, arithmetic and copies ran while one was open for 4% of the time, Pallas kernels for 10%

profile of v10, /device:TPU:8, one launch (start us, length us, event | category | flops | bytes accessed | tf_op | source)
XLA Modules:
  0.0 96.0 jit_solution(4255093458225668915)
XLA Ops:
  0.6 10.9 %collective-permute-start = (bf16[48,1536]{1,0:T(8,128)(2,1)}, bf16[48,1536]{1,0:T(8,128)(2,1)S(1)}, u32[]{:S(2)}, u32[]{:S(2)}) collective-permute-start(bf16[48,1536]{1,0:T(8,128)(2,1)} %param.13), channel_id=1, source_target_pairs={{32,8},{8,32},{40,16},{16,40},{48,24},{24,48},{56,0},{0,56},{33,9}... | collective-permute-start | bytes 442376 | tf_op jit(solution)/shard_map/ppermute | solution.py:153
  12.2 3.1 %pack.1 = bf16[16,3,128,128]{3,2,1,0:T(8,128)(2,1)} custom-call(s32[1]{0:T(128)S(6)} %copy.16.length_ref, s32[1]{0:T(128)} %bitcast.4.base_ref, bf16[120,1536]{1,0:T(8,128)(2,1)} %bitcast.17, bf16[120,2,1536]{2,1,0:T(2,128)(2,1)} %bitcast.16, bf16[8,1536]{1,0:T(8,128)(2,1)} %bitcast.19, bf16[8,2,1536]{2,1,0:T(2,128)(2,1)} %bitcast.18), custom_call_target="tpu_custom_call" | custom-call | tf_op jit(solution)/shard_map/pack/pallas_call | solution.py:184
  15.6 7.6 %all-to-all-start = ((bf16[16,3,128,128]{3,2,1,0:T(8,128)(2,1)}), bf16[16,3,128,128]{3,2,1,0:T(8,128)(2,1)S(1)}, u32[]{:S(2)}, u32[]{:S(2)}) async-start(bf16[16,3,128,128]{3,2,1,0:T(8,128)(2,1)} %pack.1), calls=%async_computation | async-start | bytes 3145728 | tf_op jit(solution)/shard_map/all_to_all | solution.py:208
  23.2 3.4 %collective-permute-start.1 = (bf16[48,1536]{1,0:T(8,128)(2,1)S(1)}, bf16[48,1536]{1,0:T(8,128)(2,1)S(1)}, u32[]{:S(2)}, u32[]{:S(2)}) collective-permute-start(bf16[48,1536]{1,0:T(8,128)(2,1)S(1)} %collective-permute-done), channel_id=1, source_target_pairs={{0,32},{32,0},{1,33},{33,1},{2,34},{34,2},{3,35},{35,3},{4,36},{36... | collective-permute-start | bytes 442376 | tf_op jit(solution)/shard_map/ppermute | solution.py:178
  26.6 4.0 %collective-permute-done.1 = bf16[48,1536]{1,0:T(8,128)(2,1)S(1)} collective-permute-done((bf16[48,1536]{1,0:T(8,128)(2,1)S(1)}, bf16[48,1536]{1,0:T(8,128)(2,1)S(1)}, u32[]{:S(2)}, u32[]{:S(2)}) %collective-permute-start.1) | collective-permute-done | bytes 147488 | tf_op jit(solution)/shard_map/ppermute | solution.py:178
  30.6 5.5 %collective-permute-start.2 = (bf16[48,1536]{1,0:T(8,128)(2,1)S(1)}, bf16[48,1536]{1,0:T(8,128)(2,1)S(1)}, u32[]{:S(2)}, u32[]{:S(2)}) collective-permute-start(bf16[48,1536]{1,0:T(8,128)(2,1)S(1)} %collective-permute-done.1), channel_id=1, source_target_pairs={{32,8},{8,32},{40,16},{16,40},{48,24},{24,48},{56,0},{0,56},{33,9}... | collective-permute-start | bytes 442376 | tf_op jit(solution)/shard_map/ppermute | solution.py:153
  36.1 3.1 %collective-permute-done.2 = bf16[48,1536]{1,0:T(8,128)(2,1)S(1)} collective-permute-done((bf16[48,1536]{1,0:T(8,128)(2,1)S(1)}, bf16[48,1536]{1,0:T(8,128)(2,1)S(1)}, u32[]{:S(2)}, u32[]{:S(2)}) %collective-permute-start.2) | collective-permute-done | bytes 147488 | tf_op jit(solution)/shard_map/ppermute | solution.py:153
  39.2 3.4 %collective-permute-start.3 = (bf16[192,1536]{1,0:T(8,128)(2,1)S(1)}, bf16[192,1536]{1,0:T(8,128)(2,1)S(1)}, u32[]{:S(2)}, u32[]{:S(2)}) collective-permute-start(bf16[192,1536]{1,0:T(8,128)(2,1)S(1)} %constant_dynamic-update-slice_fusion.refs_0_), channel_id=1, source_target_pairs={{0,2},{2,4},{4,6},{6,0},{1,3},{3,5},{5,7},{7,1},{8,10},{10,12},{12... | collective-permute-start | bytes 1769480 | tf_op jit(solution)/shard_map/ppermute | solution.py:161
  42.6 3.7 %collective-permute-start.4 = (bf16[192,1536]{1,0:T(8,128)(2,1)S(1)}, bf16[192,1536]{1,0:T(8,128)(2,1)S(1)}, u32[]{:S(2)}, u32[]{:S(2)}) collective-permute-start(bf16[192,1536]{1,0:T(8,128)(2,1)S(1)} %constant_dynamic-update-slice_fusion.refs_0_), channel_id=1, source_target_pairs={{0,6},{2,0},{4,2},{6,4},{1,7},{3,1},{5,3},{7,5},{8,14},{10,8},{12,... | collective-permute-start | bytes 1769480 | tf_op jit(solution)/shard_map/ppermute | solution.py:162
  46.3 1.9 %collective-permute-start.5 = (bf16[192,1536]{1,0:T(8,128)(2,1)S(1)}, bf16[192,1536]{1,0:T(8,128)(2,1)S(1)}, u32[]{:S(2)}, u32[]{:S(2)}) collective-permute-start(bf16[192,1536]{1,0:T(8,128)(2,1)S(1)} %constant_dynamic-update-slice_fusion.refs_0_), channel_id=1, source_target_pairs={{0,1},{1,0},{2,3},{3,2},{4,5},{5,4},{6,7},{7,6},{8,9},{9,8},{10,11... | collective-permute-start | bytes 1769480 | tf_op jit(solution)/shard_map/ppermute | solution.py:164
  48.2 7.0 %collective-permute-done.3.refs_1_ = bf16[192,1536]{1,0:T(8,128)(2,1)S(1)} collective-permute-done((bf16[192,1536]{1,0:T(8,128)(2,1)S(1)}, bf16[192,1536]{1,0:T(8,128)(2,1)S(1)}, u32[]{:S(2)}, u32[]{:S(2)}) %collective-permute-start.3) | collective-permute-done | bytes 589856 | tf_op jit(solution)/shard_map/ppermute | solution.py:161
  55.9 2.2 %collective-permute-start.6 = (bf16[96,1536]{1,0:T(8,128)(2,1)}, bf16[96,1536]{1,0:T(8,128)(2,1)}, u32[]{:S(2)}, u32[]{:S(2)}) collective-permute-start(bf16[96,1536]{1,0:T(8,128)(2,1)} %slice.8), channel_id=1, source_target_pairs={{0,2},{2,4},{4,6},{6,0},{1,3},{3,5},{5,7},{7,1},{8,10},{10,12},{12... | collective-permute-start | bytes 884744 | tf_op jit(solution)/shard_map/ppermute | solution.py:167
  59.1 4.9 %collective-permute-start.7 = (bf16[96,1536]{1,0:T(8,128)(2,1)}, bf16[96,1536]{1,0:T(8,128)(2,1)}, u32[]{:S(2)}, u32[]{:S(2)}) collective-permute-start(bf16[96,1536]{1,0:T(8,128)(2,1)} %slice.7), channel_id=1, source_target_pairs={{0,6},{2,0},{4,2},{6,4},{1,7},{3,1},{5,3},{7,5},{8,14},{10,8},{12,... | collective-permute-start | bytes 884744 | tf_op jit(solution)/shard_map/ppermute | solution.py:167
  64.0 6.5 %attend.1 = bf16[16,144,128]{2,1,0:T(8,128)(2,1)} custom-call(s32[1]{0:T(128)S(6)} %copy.16.length_ref, bf16[16,3,128,128]{3,2,1,0:T(8,128)(2,1)S(1)} %all-to-all-done.x_ref), custom_call_target="tpu_custom_call" | custom-call | tf_op jit(solution)/shard_map/attend/pallas_call | solution.py:209
  70.5 7.4 %all-to-all-start.1 = ((bf16[16,144,128]{2,1,0:T(8,128)(2,1)}), bf16[16,144,128]{2,1,0:T(8,128)(2,1)S(1)}, u32[]{:S(2)}, u32[]{:S(2)}) async-start(bf16[16,144,128]{2,1,0:T(8,128)(2,1)} %attend.1), calls=%async_computation.1 | async-start | bytes 1179648 | tf_op jit(solution)/shard_map/all_to_all | solution.py:222
  77.8 1.9 %collective-permute-start.9 = (bf16[192,1536]{1,0:T(8,128)(2,1)S(1)}, bf16[192,1536]{1,0:T(8,128)(2,1)}, u32[]{:S(2)}, u32[]{:S(2)}) collective-permute-start(bf16[192,1536]{1,0:T(8,128)(2,1)S(1)} %collective-permute-done.4.refs_2_), channel_id=1, source_target_pairs={{0,1},{1,0},{2,3},{3,2},{4,5},{5,4},{6,7},{7,6},{8,9},{9,8},{10,11... | collective-permute-start | bytes 1769480 | tf_op jit(solution)/shard_map/ppermute | solution.py:169
  79.8 2.4 %collective-permute-start.8 = (bf16[192,1536]{1,0:T(8,128)(2,1)S(1)}, bf16[192,1536]{1,0:T(8,128)(2,1)}, u32[]{:S(2)}, u32[]{:S(2)}) collective-permute-start(bf16[192,1536]{1,0:T(8,128)(2,1)S(1)} %collective-permute-done.3.refs_1_), channel_id=1, source_target_pairs={{0,1},{1,0},{2,3},{3,2},{4,5},{5,4},{6,7},{7,6},{8,9},{9,8},{10,11... | collective-permute-start | bytes 1769480 | tf_op jit(solution)/shard_map/ppermute | solution.py:169
  82.2 1.0 %constant_dynamic-update-slice_fusion.5 = bf16[192,1536]{1,0:T(8,128)(2,1)S(1)} fusion(bf16[96,1536]{1,0:T(8,128)(2,1)} %collective-permute-done.6), kind=kLoop, calls=%fused_computation.5 | loop fusion | bytes 589824
  83.2 1.0 %constant_dynamic-update-slice_fusion.4.refs_3_ = bf16[192,1536]{1,0:T(8,128)(2,1)S(1)} fusion(bf16[192,1536]{1,0:T(8,128)(2,1)S(1)} %constant_dynamic-update-slice_fusion.5, bf16[96,1536]{1,0:T(8,128)(2,1)} %collective-permute-done.7), kind=kLoop, calls=%fused_computation.4 | loop fusion | bytes 589824 | tf_op jit(solution)/shard_map/concatenate | solution.py:168
  84.2 1.9 %collective-permute-start.10 = (bf16[192,1536]{1,0:T(8,128)(2,1)S(1)}, bf16[192,1536]{1,0:T(8,128)(2,1)}, u32[]{:S(2)}, u32[]{:S(2)}) collective-permute-start(bf16[192,1536]{1,0:T(8,128)(2,1)S(1)} %constant_dynamic-update-slice_fusion.4.refs_3_), channel_id=1, source_target_pairs={{0,1},{1,0},{2,3},{3,2},{4,5},{5,4},{6,7},{7,6},{8,9},{9,8},{10,11... | collective-permute-start | bytes 1769480 | tf_op jit(solution)/shard_map/ppermute | solution.py:169
  86.2 2.0 %collective-permute-done.10.refs_7_ = bf16[192,1536]{1,0:T(8,128)(2,1)} collective-permute-done((bf16[192,1536]{1,0:T(8,128)(2,1)S(1)}, bf16[192,1536]{1,0:T(8,128)(2,1)}, u32[]{:S(2)}, u32[]{:S(2)}) %collective-permute-start.10) | collective-permute-done | bytes 589856 | tf_op jit(solution)/shard_map/ppermute | solution.py:169
  88.2 3.0 %all-to-all-done.1.x_ref = bf16[16,144,128]{2,1,0:T(8,128)(2,1)S(1)} async-done(((bf16[16,144,128]{2,1,0:T(8,128)(2,1)}), bf16[16,144,128]{2,1,0:T(8,128)(2,1)S(1)}, u32[]{:S(2)}, u32[]{:S(2)}) %all-to-all-start.1) | async-done | bytes 589856 | tf_op jit(solution)/shard_map/all_to_all | solution.py:222
  91.2 1.1 %copy-done.1 = bf16[192,1536]{1,0:T(8,128)(2,1)S(1)} copy-done((bf16[192,1536]{1,0:T(8,128)(2,1)S(1)}, bf16[192,1536]{1,0:T(8,128)(2,1)}, u32[]{:S(2)}) %copy-start.1) | copy-done | bytes 589848
  92.3 3.7 %project.1 = (bf16[120,1536]{1,0:T(8,128)(2,1)}, bf16[8,1536]{1,0:T(8,128)(2,1)}, f32[12,1,120]{2,1,0:T(1,128)}, f32[8,12]{1,0:T(8,128)}, bf16[120,1536]{1,0:T(8,128)(2,1)}) custom-call(s32[4]{0:T(128)S(1)} %pad_add_fusion.spot_ref, bf16[16,144,128]{2,1,0:T(8,128)(2,1)S(1)} %all-to-all-done.1.x_ref, f32[1,1536]{1,0:T(1,128)S(1)} %copy-done.2, ...), custom_call_target="tpu_custom_call" | custom-call | tf_op jit(solution)/shard_map/project/pallas_call | solution.py:223
  (22 shorter events, 2.1 us)
Async XLA Ops:
  0.6 15.0 %collective-permute-start = (bf16[48,1536]{1,0:T(8,128)(2,1)}, bf16[48,1536]{1,0:T(8,128)(2,1)S(1)}, u32[]{:S(2)}, u32[]{:S(2)}) collective-permute-start(bf16[48,1536]{1,0:T(8,128)(2,1)} %param.13), channel_id=1, source_target_pairs={{32,8},{8,32},{40,16},{16,40},{48,24},{24,48},{56,0},{0,56},{33,9}... | collective-permute-start | bytes 442376 | tf_op jit(solution)/shard_map/ppermute | solution.py:153
  15.3 7.9 %copy-start.3 = (bf16[48,1536]{1,0:T(8,128)(2,1)S(1)}, bf16[48,1536]{1,0:T(8,128)(2,1)}, u32[]{:S(2)}) copy-start(bf16[48,1536]{1,0:T(8,128)(2,1)} %param.13) | copy-start | bytes 442372
  15.6 48.3 %all-to-all-start = ((bf16[16,3,128,128]{3,2,1,0:T(8,128)(2,1)}), bf16[16,3,128,128]{3,2,1,0:T(8,128)(2,1)S(1)}, u32[]{:S(2)}, u32[]{:S(2)}) async-start(bf16[16,3,128,128]{3,2,1,0:T(8,128)(2,1)} %pack.1), calls=%async_computation | async-start | bytes 3145728 | tf_op jit(solution)/shard_map/all_to_all | solution.py:208
  23.2 7.4 %collective-permute-start.1 = (bf16[48,1536]{1,0:T(8,128)(2,1)S(1)}, bf16[48,1536]{1,0:T(8,128)(2,1)S(1)}, u32[]{:S(2)}, u32[]{:S(2)}) collective-permute-start(bf16[48,1536]{1,0:T(8,128)(2,1)S(1)} %collective-permute-done), channel_id=1, source_target_pairs={{0,32},{32,0},{1,33},{33,1},{2,34},{34,2},{3,35},{35,3},{4,36},{36... | collective-permute-start | bytes 442376 | tf_op jit(solution)/shard_map/ppermute | solution.py:178
  30.6 8.6 %collective-permute-start.2 = (bf16[48,1536]{1,0:T(8,128)(2,1)S(1)}, bf16[48,1536]{1,0:T(8,128)(2,1)S(1)}, u32[]{:S(2)}, u32[]{:S(2)}) collective-permute-start(bf16[48,1536]{1,0:T(8,128)(2,1)S(1)} %collective-permute-done.1), channel_id=1, source_target_pairs={{32,8},{8,32},{40,16},{16,40},{48,24},{24,48},{56,0},{0,56},{33,9}... | collective-permute-start | bytes 442376 | tf_op jit(solution)/shard_map/ppermute | solution.py:153
  39.2 16.0 %collective-permute-start.3 = (bf16[192,1536]{1,0:T(8,128)(2,1)S(1)}, bf16[192,1536]{1,0:T(8,128)(2,1)S(1)}, u32[]{:S(2)}, u32[]{:S(2)}) collective-permute-start(bf16[192,1536]{1,0:T(8,128)(2,1)S(1)} %constant_dynamic-update-slice_fusion.refs_0_), channel_id=1, source_target_pairs={{0,2},{2,4},{4,6},{6,0},{1,3},{3,5},{5,7},{7,1},{8,10},{10,12},{12... | collective-permute-start | bytes 1769480 | tf_op jit(solution)/shard_map/ppermute | solution.py:161
  42.6 15.5 %collective-permute-start.4 = (bf16[192,1536]{1,0:T(8,128)(2,1)S(1)}, bf16[192,1536]{1,0:T(8,128)(2,1)S(1)}, u32[]{:S(2)}, u32[]{:S(2)}) collective-permute-start(bf16[192,1536]{1,0:T(8,128)(2,1)S(1)} %constant_dynamic-update-slice_fusion.refs_0_), channel_id=1, source_target_pairs={{0,6},{2,0},{4,2},{6,4},{1,7},{3,1},{5,3},{7,5},{8,14},{10,8},{12,... | collective-permute-start | bytes 1769480 | tf_op jit(solution)/shard_map/ppermute | solution.py:162
  46.3 11.8 %collective-permute-start.5 = (bf16[192,1536]{1,0:T(8,128)(2,1)S(1)}, bf16[192,1536]{1,0:T(8,128)(2,1)S(1)}, u32[]{:S(2)}, u32[]{:S(2)}) collective-permute-start(bf16[192,1536]{1,0:T(8,128)(2,1)S(1)} %constant_dynamic-update-slice_fusion.refs_0_), channel_id=1, source_target_pairs={{0,1},{1,0},{2,3},{3,2},{4,5},{5,4},{6,7},{7,6},{8,9},{9,8},{10,11... | collective-permute-start | bytes 1769480 | tf_op jit(solution)/shard_map/ppermute | solution.py:164
  55.9 26.3 %collective-permute-start.6 = (bf16[96,1536]{1,0:T(8,128)(2,1)}, bf16[96,1536]{1,0:T(8,128)(2,1)}, u32[]{:S(2)}, u32[]{:S(2)}) collective-permute-start(bf16[96,1536]{1,0:T(8,128)(2,1)} %slice.8), channel_id=1, source_target_pairs={{0,2},{2,4},{4,6},{6,0},{1,3},{3,5},{5,7},{7,1},{8,10},{10,12},{12... | collective-permute-start | bytes 884744 | tf_op jit(solution)/shard_map/ppermute | solution.py:167
  58.1 1.0 %copy-start = (bf16[192,1536]{1,0:T(8,128)(2,1)}, bf16[192,1536]{1,0:T(8,128)(2,1)S(1)}, u32[]{:S(2)}) copy-start(bf16[192,1536]{1,0:T(8,128)(2,1)S(1)} %collective-permute-done.5.refs_4_) | copy-start | bytes 1769476
  59.1 24.1 %collective-permute-start.7 = (bf16[96,1536]{1,0:T(8,128)(2,1)}, bf16[96,1536]{1,0:T(8,128)(2,1)}, u32[]{:S(2)}, u32[]{:S(2)}) collective-permute-start(bf16[96,1536]{1,0:T(8,128)(2,1)} %slice.7), channel_id=1, source_target_pairs={{0,6},{2,0},{4,2},{6,4},{1,7},{3,1},{5,3},{7,5},{8,14},{10,8},{12,... | collective-permute-start | bytes 884744 | tf_op jit(solution)/shard_map/ppermute | solution.py:167
  70.5 20.8 %copy-start.2 = (f32[1,1536]{1,0:T(1,128)S(1)}, f32[1,1536]{1,0:T(1,128)}, u32[]{:S(2)}) copy-start(f32[1,1536]{1,0:T(1,128)} %gate_ref.1) | copy-start | bytes 18436
  70.5 20.8 %all-to-all-start.1 = ((bf16[16,144,128]{2,1,0:T(8,128)(2,1)}), bf16[16,144,128]{2,1,0:T(8,128)(2,1)S(1)}, u32[]{:S(2)}, u32[]{:S(2)}) async-start(bf16[16,144,128]{2,1,0:T(8,128)(2,1)} %attend.1), calls=%async_computation.1 | async-start | bytes 1179648 | tf_op jit(solution)/shard_map/all_to_all | solution.py:222
  77.8 8.3 %collective-permute-start.9 = (bf16[192,1536]{1,0:T(8,128)(2,1)S(1)}, bf16[192,1536]{1,0:T(8,128)(2,1)}, u32[]{:S(2)}, u32[]{:S(2)}) collective-permute-start(bf16[192,1536]{1,0:T(8,128)(2,1)S(1)} %collective-permute-done.4.refs_2_), channel_id=1, source_target_pairs={{0,1},{1,0},{2,3},{3,2},{4,5},{5,4},{6,7},{7,6},{8,9},{9,8},{10,11... | collective-permute-start | bytes 1769480 | tf_op jit(solution)/shard_map/ppermute | solution.py:169
  79.8 6.4 %collective-permute-start.8 = (bf16[192,1536]{1,0:T(8,128)(2,1)S(1)}, bf16[192,1536]{1,0:T(8,128)(2,1)}, u32[]{:S(2)}, u32[]{:S(2)}) collective-permute-start(bf16[192,1536]{1,0:T(8,128)(2,1)S(1)} %collective-permute-done.3.refs_1_), channel_id=1, source_target_pairs={{0,1},{1,0},{2,3},{3,2},{4,5},{5,4},{6,7},{7,6},{8,9},{9,8},{10,11... | collective-permute-start | bytes 1769480 | tf_op jit(solution)/shard_map/ppermute | solution.py:169
  84.2 4.0 %collective-permute-start.10 = (bf16[192,1536]{1,0:T(8,128)(2,1)S(1)}, bf16[192,1536]{1,0:T(8,128)(2,1)}, u32[]{:S(2)}, u32[]{:S(2)}) collective-permute-start(bf16[192,1536]{1,0:T(8,128)(2,1)S(1)} %constant_dynamic-update-slice_fusion.4.refs_3_), channel_id=1, source_target_pairs={{0,1},{1,0},{2,3},{3,2},{4,5},{5,4},{6,7},{7,6},{8,9},{9,8},{10,11... | collective-permute-start | bytes 1769480 | tf_op jit(solution)/shard_map/ppermute | solution.py:169
  91.2 1.1 %copy-start.1 = (bf16[192,1536]{1,0:T(8,128)(2,1)S(1)}, bf16[192,1536]{1,0:T(8,128)(2,1)}, u32[]{:S(2)}) copy-start(bf16[192,1536]{1,0:T(8,128)(2,1)} %copy-done) | copy-start | bytes 1769476
